TPU v7x, 32 devices: a whole 2x2x4 slice. The times are simulated.
32 devices in a mesh: rep: 8 (over z, x), shard: 4 (over y, core).
Axes of the slice: x: 2, y: 2, z: 4, core: 2. Of those that a mesh axis runs over, the one named last changes fastest.
Arguments:
- tokens: bfloat16 [4096, 1024], P(('rep', 'shard')), may hold values from -6 to 6
- cotangent: bfloat16 [4096, 1024], P(('rep', 'shard')), may hold values from -6 to 6
- w_qkv: bfloat16 [2, 1024, 3072], P(None, 'shard'), may hold values from -0.1875 to 0.1875
- w_out: bfloat16 [2, 1024, 1024], P(None, 'shard'), may hold values from -1.5 to 1.5
- w_up: bfloat16 [2, 1024, 4096], P(None, 'shard'), may hold values from -0.1875 to 0.1875
- w_down: bfloat16 [2, 4096, 1024], P(None, 'shard'), may hold values from -0.09375 to 0.09375
- ln_gain: bfloat16 [2, 1024, 2], P(None, 'shard'), may hold values from 0.25 to 1.75
- ln_bias: bfloat16 [2, 1024, 2], P(None, 'shard'), may hold values from -3 to 3
- positions: bfloat16 [512, 1024], P('shard'), may hold values from -6 to 6
- segments: int32 [4096], P(('rep', 'shard')), may hold values from 0 to 1, as said below
- keep_mask: int32 [4096], P(('rep', 'shard')), may hold values from 0 to 1, as said below
- buckets: int32 [255], replicated, may hold values from 161 to 351, as said below
Outputs:
- output: bfloat16 [4096, 1024], P(('rep', 'shard'))
- grad_tokens: float32 [4096, 1024], P(('rep', 'shard'))
- grad_qkv: float32 [2, 1024, 3072], P(None, 'shard')
- grad_out: float32 [2, 1024, 1024], P(None, 'shard')
- grad_up: float32 [2, 1024, 4096], P(None, 'shard')
- grad_down: float32 [2, 4096, 1024], P(None, 'shard')
- grad_gain: float32 [2, 1024, 2], P(None, 'shard')
- grad_bias: float32 [2, 1024, 2], P(None, 'shard')
- grad_positions: float32 [512, 1024], P('shard')
Inputs may be any that keep to these rules, and one draw needn't show every extreme that they name: `segments`: in each sequence of 128 tokens the document numbers start at 0, never fall, rise by one at each new document, and every document holds 60 tokens or more. `keep_mask`: in each sequence of 128 tokens the ones come first; at most 30 tokens at the end are padding. `buckets`: 256 at distance 0, never falling as i - j rises, symmetric about distance 0, distances below 64 in size each with a bucket of their own.
All inputs are finite; a program needn't handle non-finite values.
Results may differ from a plain program's by a relative error of at most 0.028.
Values may be sent and summed in bfloat16 or wider, within the bound.
No kernel may reach another device: no remote copies, remote signals or barrier semaphores. Data moves between devices by JAX's collectives and lax.ppermute only.
A program may use at most 320 MiB of HBM per device.

v0:
```python
from functools import partial
import math

import jax
import jax.numpy as jnp
from jax import lax
from jax.sharding import PartitionSpec as P

D = 1024
H = 16
DH = 64
LAYERS = 2


NEG_FILL = -1e30
NORM_EPS = 1e-07


def layer_norm(values, gain, bias):
    centre = values - jnp.mean(values, axis=-1, keepdims=True)
    spread_sq = jnp.mean(centre * centre, axis=-1, keepdims=True)
    return centre * lax.rsqrt(spread_sq + NORM_EPS) * gain + bias


def skew(table):
    count, rows, width = table.shape
    padded = jnp.pad(table, ((0, 0), (0, 0), (0, 1)))
    flat = padded.reshape(count, 2 * rows * rows)
    picked = flat[:, rows - 1 : rows - 1 + rows * (2 * rows - 1)]
    return picked.reshape(count, rows, 2 * rows - 1)[:, :, :rows]


def unskew(values):
    count, rows, _ = values.shape
    padded = jnp.pad(values, ((0, 0), (0, 0), (0, rows - 1)))
    flat = jnp.pad(padded.reshape(count, rows * (2 * rows - 1)), ((0, 0), (rows - 1, 1)))
    return flat.reshape(count, rows, 2 * rows)[:, :, : 2 * rows - 1]


def score_terms(heads_q, heads_k, rel_rev):
    rev_q = rel_rev[:, :D].reshape(-1, H, DH)
    rev_k = rel_rev[:, D:].reshape(-1, H, DH)
    direct = jnp.einsum("ihd,jhd->hij", heads_q, heads_k, preferred_element_type=jnp.float32)
    by_key = jnp.einsum("ihd,shd->his", heads_q, rev_k, preferred_element_type=jnp.float32)
    by_query = jnp.einsum("jhd,shd->hjs", heads_k, rev_q, preferred_element_type=jnp.float32)
    combined = direct + skew(by_key) + jnp.swapaxes(skew(by_query), 1, 2)
    return combined / math.sqrt(3 * DH)


def forward_layer(hidden, weights, rel_rows, rev_ids, allowed):
    w_qkv, w_out, w_up, w_down, norm_gains, biases = weights
    length = hidden.shape[0]
    hidden_low = hidden.astype(jnp.bfloat16)
    qkv_all = jnp.dot(hidden_low, w_qkv, preferred_element_type=jnp.float32).astype(jnp.bfloat16)
    rel_all = jnp.dot(rel_rows, w_qkv[:, : 2 * D], preferred_element_type=jnp.float32).astype(
        jnp.bfloat16
    )
    rel_rev = jnp.take(rel_all, rev_ids, axis=0)
    heads_q = qkv_all[:, :D].reshape(length, H, DH)
    heads_k = qkv_all[:, D : 2 * D].reshape(length, H, DH)
    heads_v = qkv_all[:, 2 * D :].reshape(length, H, DH)
    scores = score_terms(heads_q, heads_k, rel_rev)
    masked = jnp.where(allowed[None], scores, NEG_FILL)
    row_max = jnp.max(masked, axis=-1, keepdims=True)
    exp_terms = jnp.exp(masked - row_max)
    row_total = jnp.sum(exp_terms, axis=-1, keepdims=True)
    log_total = row_max + jnp.log(row_total)
    probs = (exp_terms / row_total).astype(jnp.bfloat16)
    context = jnp.einsum("hij,jhd->ihd", probs, heads_v, preferred_element_type=jnp.float32)
    context = context.reshape(length, D).astype(jnp.bfloat16)
    attn_sum = hidden + jnp.dot(context, w_out, preferred_element_type=jnp.float32)
    gains_f = norm_gains.astype(jnp.float32)
    biases_f = biases.astype(jnp.float32)
    mid_out = layer_norm(attn_sum, gains_f[:, 0], biases_f[:, 0])
    pre_act = jnp.dot(mid_out.astype(jnp.bfloat16), w_up, preferred_element_type=jnp.float32)
    activation = jax.nn.gelu(pre_act, approximate=False).astype(jnp.bfloat16)
    ffn_sum = mid_out + jnp.dot(activation, w_down, preferred_element_type=jnp.float32)
    layer_out = layer_norm(ffn_sum, gains_f[:, 1], biases_f[:, 1])
    saved = (
        hidden_low,
        heads_q,
        heads_k,
        heads_v,
        rel_rev,
        log_total,
        context,
        attn_sum,
        mid_out,
        pre_act,
        activation,
        ffn_sum,
    )
    return (layer_out, saved)


def backward_layer(upstream, saved, weights, rel_rows, rev_ids, allowed):
    w_qkv, w_out, w_up, w_down, norm_gains, biases = weights
    (
        hidden_low,
        heads_q,
        heads_k,
        heads_v,
        rel_rev,
        log_total,
        context,
        attn_sum,
        mid_out,
        pre_act,
        activation,
        ffn_sum,
    ) = saved
    length = hidden_low.shape[0]
    gains_f = norm_gains.astype(jnp.float32)
    biases_f = biases.astype(jnp.float32)
    norm_value, norm_back = jax.vjp(layer_norm, ffn_sum, gains_f[:, 1], biases_f[:, 1])
    d_ffn, d_gain_two, d_bias_two = norm_back(upstream)
    d_branch = d_ffn.astype(jnp.bfloat16)
    g_down = jnp.einsum("tf,td->fd", activation, d_branch, preferred_element_type=jnp.float32)
    d_act = jnp.einsum("td,fd->tf", d_branch, w_down, preferred_element_type=jnp.float32)
    gelu_value, gelu_back = jax.vjp(partial(jax.nn.gelu, approximate=False), pre_act)
    d_pre = gelu_back(d_act)[0].astype(jnp.bfloat16)
    g_up = jnp.einsum(
        "td,tf->df", mid_out.astype(jnp.bfloat16), d_pre, preferred_element_type=jnp.float32
    )
    d_mid = d_ffn + jnp.einsum("tf,df->td", d_pre, w_up, preferred_element_type=jnp.float32)
    first_value, first_back = jax.vjp(layer_norm, attn_sum, gains_f[:, 0], biases_f[:, 0])
    d_attn, d_gain_one, d_bias_one = first_back(d_mid)
    d_att_low = d_attn.astype(jnp.bfloat16)
    g_out = jnp.einsum("tc,td->cd", context, d_att_low, preferred_element_type=jnp.float32)
    d_context = jnp.einsum("td,cd->tc", d_att_low, w_out, preferred_element_type=jnp.float32)
    d_context = d_context.astype(jnp.bfloat16).reshape(length, H, DH)
    scores = score_terms(heads_q, heads_k, rel_rev)
    probs = jnp.exp(jnp.where(allowed[None], scores, NEG_FILL) - log_total)
    d_value = jnp.einsum(
        "hij,ihd->jhd", probs.astype(jnp.bfloat16), d_context, preferred_element_type=jnp.float32
    )
    d_probs = jnp.einsum("ihd,jhd->hij", d_context, heads_v, preferred_element_type=jnp.float32)
    d_scores = (probs * (d_probs - jnp.sum(d_probs * probs, axis=-1, keepdims=True))).astype(
        jnp.bfloat16
    )
    score_scale = 1.0 / math.sqrt(3 * DH)
    rev_q = rel_rev[:, :D].reshape(-1, H, DH)
    rev_k = rel_rev[:, D:].reshape(-1, H, DH)
    key_side = unskew(d_scores)
    query_side = unskew(jnp.swapaxes(d_scores, 1, 2))
    d_query = jnp.einsum("hij,jhd->ihd", d_scores, heads_k, preferred_element_type=jnp.float32)
    d_query = d_query + jnp.einsum(
        "his,shd->ihd", key_side, rev_k, preferred_element_type=jnp.float32
    )
    d_key = jnp.einsum("hij,ihd->jhd", d_scores, heads_q, preferred_element_type=jnp.float32)
    d_key = d_key + jnp.einsum(
        "hjs,shd->jhd", query_side, rev_q, preferred_element_type=jnp.float32
    )
    d_query = d_query * score_scale
    d_key = d_key * score_scale
    d_rev_k = (
        jnp.einsum("his,ihd->shd", key_side, heads_q, preferred_element_type=jnp.float32)
        * score_scale
    )
    d_rev_q = (
        jnp.einsum("hjs,jhd->shd", query_side, heads_k, preferred_element_type=jnp.float32)
        * score_scale
    )
    d_rev = jnp.concatenate([d_rev_q.reshape(-1, D), d_rev_k.reshape(-1, D)], axis=1)
    d_rel = jax.ops.segment_sum(d_rev, rev_ids, num_segments=rel_rows.shape[0]).astype(jnp.bfloat16)
    d_qkv = jnp.concatenate(
        [d_query.reshape(length, D), d_key.reshape(length, D), d_value.reshape(length, D)], axis=1
    ).astype(jnp.bfloat16)
    g_qkv = jnp.einsum("tc,tk->ck", hidden_low, d_qkv, preferred_element_type=jnp.float32)
    g_rel = jnp.einsum("bc,bk->ck", rel_rows, d_rel, preferred_element_type=jnp.float32)
    g_qkv = g_qkv.at[:, : 2 * D].add(g_rel)
    g_rows = jnp.einsum("bk,ck->bc", d_rel, w_qkv[:, : 2 * D], preferred_element_type=jnp.float32)
    d_hidden = d_attn + jnp.einsum("tk,ck->tc", d_qkv, w_qkv, preferred_element_type=jnp.float32)
    g_gain = jnp.stack([d_gain_one, d_gain_two], axis=1)
    g_bias = jnp.stack([d_bias_one, d_bias_two], axis=1)
    return (d_hidden, (g_qkv, g_out, g_up, g_down, g_gain, g_bias, g_rows))


def reduce_grads(g_qkv, g_out, g_up, g_down, g_gain, g_bias, g_rows):
    owned = (
        lax.psum_scatter(
            g_qkv.astype(jnp.bfloat16), "shard", scatter_dimension=0, tiled=True
        ).astype(jnp.float32),
        lax.psum_scatter(
            g_out.astype(jnp.bfloat16), "shard", scatter_dimension=0, tiled=True
        ).astype(jnp.float32),
        lax.psum_scatter(
            g_up.astype(jnp.bfloat16), "shard", scatter_dimension=0, tiled=True
        ).astype(jnp.float32),
        lax.psum_scatter(
            g_down.astype(jnp.bfloat16), "shard", scatter_dimension=0, tiled=True
        ).astype(jnp.float32),
        lax.psum_scatter(
            g_gain.astype(jnp.bfloat16), "shard", scatter_dimension=0, tiled=True
        ).astype(jnp.float32),
        lax.psum_scatter(
            g_bias.astype(jnp.bfloat16), "shard", scatter_dimension=0, tiled=True
        ).astype(jnp.float32),
        lax.psum_scatter(
            g_rows.astype(jnp.bfloat16), "shard", scatter_dimension=0, tiled=True
        ).astype(jnp.float32),
    )
    return (
        lax.psum(owned[0].astype(jnp.bfloat16), "rep").astype(jnp.float32),
        lax.psum(owned[1].astype(jnp.bfloat16), "rep").astype(jnp.float32),
        lax.psum(owned[2].astype(jnp.bfloat16), "rep").astype(jnp.float32),
        lax.psum(owned[3].astype(jnp.bfloat16), "rep").astype(jnp.float32),
        lax.psum(owned[4].astype(jnp.bfloat16), "rep").astype(jnp.float32),
        lax.psum(owned[5].astype(jnp.bfloat16), "rep").astype(jnp.float32),
        lax.psum(owned[6].astype(jnp.bfloat16), "rep").astype(jnp.float32),
    )


def per_device(
    tokens,
    cotangent,
    w_qkv,
    w_out,
    w_up,
    w_down,
    ln_gain,
    ln_bias,
    positions,
    segments,
    keep_mask,
    buckets,
):
    length = tokens.shape[0]
    rev_ids = buckets[::-1]
    allowed = (segments[:, None] == segments[None, :]) & (keep_mask[None, :] == 1)
    allowed = allowed | jnp.eye(length, dtype=bool)
    rel_rows = lax.all_gather(positions, "shard", axis=0, tiled=True)
    hidden = tokens.astype(jnp.float32)
    kept_weights = []
    kept_saved = []
    for layer_id in range(LAYERS):
        weights = (
            lax.all_gather(w_qkv[layer_id], "shard", axis=0, tiled=True),
            lax.all_gather(w_out[layer_id], "shard", axis=0, tiled=True),
            lax.all_gather(w_up[layer_id], "shard", axis=0, tiled=True),
            lax.all_gather(w_down[layer_id], "shard", axis=0, tiled=True),
            lax.all_gather(ln_gain[layer_id], "shard", axis=0, tiled=True),
            lax.all_gather(ln_bias[layer_id], "shard", axis=0, tiled=True),
        )
        hidden, saved = forward_layer(hidden, weights, rel_rows, rev_ids, allowed)
        kept_weights.append(weights)
        kept_saved.append(saved)
    layer_out = hidden.astype(jnp.bfloat16)
    upstream = cotangent.astype(jnp.float32)
    reduced_all = [None] * LAYERS
    rows_total = None
    for layer_id in reversed(range(LAYERS)):
        weights = kept_weights[layer_id]
        upstream, layer_grads = backward_layer(
            upstream, kept_saved[layer_id], weights, rel_rows, rev_ids, allowed
        )
        reduced = reduce_grads(
            layer_grads[0],
            layer_grads[1],
            layer_grads[2],
            layer_grads[3],
            layer_grads[4],
            layer_grads[5],
            layer_grads[6],
        )
        reduced_all[layer_id] = reduced
        rows_total = reduced[6] if rows_total is None else rows_total + reduced[6]
    return (
        layer_out,
        upstream,
        jnp.stack([entry[0] for entry in reduced_all]),
        jnp.stack([entry[1] for entry in reduced_all]),
        jnp.stack([entry[2] for entry in reduced_all]),
        jnp.stack([entry[3] for entry in reduced_all]),
        jnp.stack([entry[4] for entry in reduced_all]),
        jnp.stack([entry[5] for entry in reduced_all]),
        rows_total,
    )


def solution(mesh):
    placed = (
        P(("rep", "shard"), None),
        P(("rep", "shard"), None),
        P(None, "shard", None),
        P(None, "shard", None),
        P(None, "shard", None),
        P(None, "shard", None),
        P(None, "shard", None),
        P(None, "shard", None),
        P("shard", None),
        P(("rep", "shard")),
        P(("rep", "shard")),
        P(),
    )
    return jax.shard_map(
        per_device,
        mesh=mesh,
        in_specs=placed,
        out_specs=(
            P(("rep", "shard"), None),
            P(("rep", "shard"), None),
            P(None, "shard", None),
            P(None, "shard", None),
            P(None, "shard", None),
            P(None, "shard", None),
            P(None, "shard", None),
            P(None, "shard", None),
            P("shard", None),
        ),
        check_vma=False,
    )
```

profile of v0, /device:TPU:0, one launch (start us, length us, event | category | flops | bytes accessed | tf_op | source)
XLA Modules:
  0.0 1610.1 jit_solution(14167681359408826117)
XLA Ops:
  48.3 12.0 all-gather.24.cloned.1.call-done
  65.4 13.3 all-gather.22.cloned.1.call-done
  78.6 48.6 %all-gather.32.cloned.1.call-done = bf16[1,1024,3072]{2,1,0:T(8,128)(2,1)} async-done(((bf16[1,256,3072]{2,1,0:T(8,128)(2,1)}), bf16[1,1024,3072]{2,1,0:T(8,128)(2,1)}) %all-gather.32.cloned.1.call-update) | async-done | bytes 6291472 | tf_op jit(solution)/shard_map/all_gather | solution.py:238
  168.4 43.1 %all-gather.28.cloned.1.call-done = bf16[1,1024,4096]{2,1,0:T(8,128)(2,1)} async-done(((bf16[1,256,4096]{2,1,0:T(8,128)(2,1)}), bf16[1,1024,4096]{2,1,0:T(8,128)(2,1)}) %all-gather.28.cloned.1.call-update) | async-done | bytes 8388624 | tf_op jit(solution)/shard_map/all_gather | solution.py:240
  211.5 9.4 multiply_convert_fusion.1
  221.0 50.3 %all-gather.30.cloned.1.call-done = bf16[1,4096,1024]{2,1,0:T(8,128)(2,1)} async-done(((bf16[1,1024,1024]{2,1,0:T(8,128)(2,1)}), bf16[1,4096,1024]{2,1,0:T(8,128)(2,1)}) %all-gather.30.cloned.1.call-update) | async-done | bytes 8388624 | tf_op jit(solution)/shard_map/all_gather | solution.py:241
  314.9 41.6 %all-gather.36.cloned.1.call-done = bf16[1,1024,4096]{2,1,0:T(8,128)(2,1)} async-done(((bf16[1,256,4096]{2,1,0:T(8,128)(2,1)}), bf16[1,1024,4096]{2,1,0:T(8,128)(2,1)}) %all-gather.36.cloned.1.call-update) | async-done | bytes 8388624 | tf_op jit(solution)/shard_map/all_gather | solution.py:240
  356.5 9.1 multiply_convert_fusion
  365.6 50.8 %all-gather.38.cloned.1.call-done = bf16[1,4096,1024]{2,1,0:T(8,128)(2,1)} async-done(((bf16[1,1024,1024]{2,1,0:T(8,128)(2,1)}), bf16[1,4096,1024]{2,1,0:T(8,128)(2,1)}) %all-gather.38.cloned.1.call-update) | async-done | bytes 8388624 | tf_op jit(solution)/shard_map/all_gather | solution.py:241
  423.7 7.4 add_convert_fusion.1
  467.6 7.6 add_convert_fusion
  508.8 7.2 scatter_custom_fusion
  516.1 6.8 fusion.66
  533.3 7.2 scatter_custom_fusion.1
  554.7 7.7 fusion.138
  562.4 9.8 fusion.1
  572.3 8.4 convert_element_type.259
  591.3 12.4 copy.152
  603.6 9.8 fusion
  613.4 8.3 convert_element_type.257
  655.4 50.1 %reduce-scatter.25.cloned.1.call-done = bf16[256,3072]{0,1:T(8,128)(2,1)} async-done(((bf16[1024,3072]{0,1:T(8,128)(2,1)}), bf16[256,3072]{0,1:T(8,128)(2,1)}) %reduce-scatter.25.cloned.1.call-update) | async-done | bytes 1572880 | tf_op jit(solution)/shard_map/reduce_scatter | solution.py:181
  705.6 61.0 %reduce-scatter.23.cloned.1.call-done = bf16[256,3072]{0,1:T(8,128)(2,1)} async-done(((bf16[1024,3072]{0,1:T(8,128)(2,1)}), bf16[256,3072]{0,1:T(8,128)(2,1)}) %reduce-scatter.23.cloned.1.call-update) | async-done | bytes 1572880 | tf_op jit(solution)/shard_map/reduce_scatter | solution.py:181
  766.5 74.8 %reduce-scatter.31.cloned.1.call-done = bf16[256,4096]{1,0:T(8,128)(2,1)} async-done(((bf16[1024,4096]{1,0:T(8,128)(2,1)}), bf16[256,4096]{1,0:T(8,128)(2,1)}) %reduce-scatter.31.cloned.1.call-update) | async-done | bytes 2097168 | tf_op jit(solution)/shard_map/reduce_scatter | solution.py:187
  841.3 74.9 %reduce-scatter.33.cloned.1.call-done = bf16[256,4096]{1,0:T(8,128)(2,1)} async-done(((bf16[1024,4096]{1,0:T(8,128)(2,1)}), bf16[256,4096]{1,0:T(8,128)(2,1)}) %reduce-scatter.33.cloned.1.call-update) | async-done | bytes 2097168 | tf_op jit(solution)/shard_map/reduce_scatter | solution.py:187
  916.2 74.2 %reduce-scatter.35.cloned.1.call-done = bf16[1024,1024]{1,0:T(8,128)(2,1)} async-done(((bf16[4096,1024]{1,0:T(8,128)(2,1)}), bf16[1024,1024]{1,0:T(8,128)(2,1)}) %reduce-scatter.35.cloned.1.call-update) | async-done | bytes 2097168 | tf_op jit(solution)/shard_map/reduce_scatter | solution.py:190
  990.4 74.5 %reduce-scatter.37.cloned.1.call-done = bf16[1024,1024]{1,0:T(8,128)(2,1)} async-done(((bf16[4096,1024]{1,0:T(8,128)(2,1)}), bf16[1024,1024]{1,0:T(8,128)(2,1)}) %reduce-scatter.37.cloned.1.call-update) | async-done | bytes 2097168 | tf_op jit(solution)/shard_map/reduce_scatter | solution.py:190
  1071.9 15.4 reduce-scatter.49.cloned.1.call-done
  1088.2 21.8 %reduce-scatter.45.cloned.1.call-done = bf16[256,2]{1,0:T(8,128)(2,1)} async-done(((bf16[1024,2]{1,0:T(8,128)(2,1)}), bf16[256,2]{1,0:T(8,128)(2,1)}) %reduce-scatter.45.cloned.1.call-update) | async-done | bytes 1040
  1110.9 21.6 %reduce-scatter.47.cloned.1.call-done = bf16[256,2]{1,0:T(8,128)(2,1)} async-done(((bf16[1024,2]{1,0:T(8,128)(2,1)}), bf16[256,2]{1,0:T(8,128)(2,1)}) %reduce-scatter.47.cloned.1.call-update) | async-done | bytes 1040
  1133.4 21.8 %reduce-scatter.43.cloned.1.call-done = bf16[256,2]{1,0:T(8,128)(2,1)} async-done(((bf16[1024,2]{1,0:T(8,128)(2,1)}), bf16[256,2]{1,0:T(8,128)(2,1)}) %reduce-scatter.43.cloned.1.call-update) | async-done | bytes 1040
  1156.1 21.9 %all-reduce.12 = (bf16[1,256,2]{1,2,0:T(2,128)(2,1)S(1)}, bf16[1,256,2]{1,2,0:T(2,128)(2,1)S(1)}, bf16[1,256,2]{1,2,0:T(2,128)(2,1)S(1)}, bf16[1,256,2]{1,2,0:T(2,128)(2,1)S(1)}) all-reduce(bf16[1,256,2]{1,2,0:T(2,128)(2,1)S(1)} %bitcast.375, bf16[1,256,2]{1,2,0:T(2,128)(2,1)S(1)} %bitcast.377, ...), channel_id=1, replica_groups=mesh['rep'=8,'shard'=4] {'rep'}, use_global_device_ids=true, to_apply=%region_48.50 | all-reduce | flops 2048 | bytes 8192 | tf_op jit(solution)/shard_map/psum | solution.py:208
  1179.2 400.8 %all-reduce.16.cloned.1.call-done = (bf16[1,256,3072]{1,2,0:T(8,128)(2,1)}, bf16[1,256,3072]{1,2,0:T(8,128)(2,1)}, bf16[1,256,1024]{2,1,0:T(8,128)(2,1)}, bf16[1...) async-done(((bf16[1,256,3072]{1,2,0:T(8,128)(2,1)}, ...) | async-done | bytes 13107216 | tf_op jit(solution)/shard_map/psum | solution.py:204
  (429 shorter events, 310.5 us)
Async XLA Ops:
  7.2 53.1 %all-gather.24.cloned.1.call-start = ((), (), s32[]{:S(2)}) async-start(), calls=%async_computation.25 | async-start | bytes 7864320 | tf_op jit(solution)/shard_map/all_gather | solution.py:238
  11.0 67.6 %all-gather.22.cloned.1.call-start = ((), (), s32[]{:S(2)}) async-start(), calls=%async_computation.14 | async-start | bytes 1310720 | tf_op jit(solution)/shard_map/all_gather | solution.py:232
  11.7 115.5 %all-gather.32.cloned.1.call-start = ((), (), s32[]{:S(2)}) async-start(), calls=%async_computation.29 | async-start | bytes 7864320 | tf_op jit(solution)/shard_map/all_gather | solution.py:238
  12.5 153.5 %all-gather.26.cloned.1.call-start = ((), (), s32[]{:S(2)}) async-start(), calls=%async_computation.26 | async-start | bytes 2621440 | tf_op jit(solution)/shard_map/all_gather | solution.py:239
  13.6 197.9 %all-gather.28.cloned.1.call-start = ((), (), s32[]{:S(2)}) async-start(), calls=%async_computation.27 | async-start | bytes 10485760 | tf_op jit(solution)/shard_map/all_gather | solution.py:240
  18.4 252.9 %all-gather.30.cloned.1.call-start = ((), (), s32[]{:S(2)}) async-start(), calls=%async_computation.28 | async-start | bytes 10485760 | tf_op jit(solution)/shard_map/all_gather | solution.py:241
  23.6 288.7 %all-gather.34.cloned.1.call-start = ((), (), s32[]{:S(2)}) async-start(), calls=%async_computation.30 | async-start | bytes 2621440 | tf_op jit(solution)/shard_map/all_gather | solution.py:239
  24.4 332.1 %all-gather.36.cloned.1.call-start = ((), (), s32[]{:S(2)}) async-start(), calls=%async_computation.31 | async-start | bytes 10485760 | tf_op jit(solution)/shard_map/all_gather | solution.py:240
  24.5 23.7 %copy-start.74 = (s32[128]{0:T(128)S(1)}, s32[128]{0:T(128)}, u32[]{:S(2)}) copy-start(s32[128]{0:T(128)} %param.27) | copy-start | bytes 1540
  24.5 35.8 %copy-start.44 = (bf16[128,1024]{1,0:T(8,128)(2,1)S(1)}, bf16[128,1024]{1,0:T(8,128)(2,1)}, u32[]{:S(2)}) copy-start(bf16[128,1024]{1,0:T(8,128)(2,1)} %param.18) | copy-start | bytes 786436
  25.1 391.3 %all-gather.38.cloned.1.call-start = ((), (), s32[]{:S(2)}) async-start(), calls=%async_computation.32 | async-start | bytes 10485760 | tf_op jit(solution)/shard_map/all_gather | solution.py:241
  25.9 629.5 %reduce-scatter.41.cloned.1.call-start = ((), (), s32[]{:S(2)}) async-start(), calls=%async_computation.24 | async-start | bytes 1310720 | tf_op jit(solution)/shard_map/reduce_scatter | solution.py:199
  26.1 22.1 %copy-start.73 = (s32[255]{0:T(256)}, s32[255]{0:T(256)S(1)}, u32[]{:S(2)}) copy-start(s32[255]{0:T(256)S(1)} %get-tuple-element.95) | copy-start | bytes 3064
  43.1 228.2 %copy-start.70 = (f32[1024,1]{0,1:T(1,128)}, f32[1024,1]{0,1:T(1,128)S(1)}, u32[]{:S(2)}) copy-start(f32[1024,1]{0,1:T(1,128)S(1)} %get-tuple-element.122) | copy-start | bytes 12292
  64.5 98.9 %copy-start.16 = (bf16[128,1024]{0,1:T(8,128)(2,1)}, bf16[128,1024]{0,1:T(8,128)(2,1)S(1)}, u32[]{:S(2)}) copy-start(bf16[128,1024]{0,1:T(8,128)(2,1)S(1)} %copy.92) | copy-start | bytes 786436
  165.9 55.1 %copy-start.65 = (bf16[16,64,128]{2,1,0:T(8,128)(2,1)}, bf16[16,64,128]{2,1,0:T(8,128)(2,1)S(1)}, u32[]{:S(2)}) copy-start(bf16[16,64,128]{2,1,0:T(8,128)(2,1)S(1)} %convolution_convert_fusion.11) | copy-start | bytes 786436
  281.6 26.7 %copy-start.19 = (bf16[128,1024]{0,1:T(8,128)(2,1)}, bf16[128,1024]{0,1:T(8,128)(2,1)S(1)}, u32[]{:S(2)}) copy-start(bf16[128,1024]{0,1:T(8,128)(2,1)S(1)} %copy.100) | copy-start | bytes 786436
  282.8 25.5 %copy-start.21 = (bf16[128,1024]{0,1:T(8,128)(2,1)}, bf16[128,1024]{0,1:T(8,128)(2,1)S(1)}, u32[]{:S(2)}) copy-start(bf16[128,1024]{0,1:T(8,128)(2,1)S(1)} %copy.99) | copy-start | bytes 786436
  522.9 132.4 %reduce-scatter.39.cloned.1.call-start = ((), (), s32[]{:S(2)}) async-start(), calls=%async_computation.23 | async-start | bytes 1310720 | tf_op jit(solution)/shard_map/reduce_scatter | solution.py:199
  547.4 108.0 %reduce-scatter.27.cloned.1.call-start = ((), (), s32[]{:S(2)}) async-start(), calls=%async_computation.17 | async-start | bytes 2621440 | tf_op jit(solution)/shard_map/reduce_scatter | solution.py:184
  550.7 104.7 %reduce-scatter.29.cloned.1.call-start = ((), (), s32[]{:S(2)}) async-start(), calls=%async_computation.18 | async-start | bytes 2621440 | tf_op jit(solution)/shard_map/reduce_scatter | solution.py:184
  554.0 151.5 %reduce-scatter.25.cloned.1.call-start = ((), (), s32[]{:S(2)}) async-start(), calls=%async_computation.16 | async-start | bytes 7864320 | tf_op jit(solution)/shard_map/reduce_scatter | solution.py:181
  580.7 185.9 %reduce-scatter.23.cloned.1.call-start = ((), (), s32[]{:S(2)}) async-start(), calls=%async_computation.15 | async-start | bytes 7864320 | tf_op jit(solution)/shard_map/reduce_scatter | solution.py:181
  621.8 219.5 %reduce-scatter.31.cloned.1.call-start = ((), (), s32[]{:S(2)}) async-start(), calls=%async_computation.19 | async-start | bytes 10485760 | tf_op jit(solution)/shard_map/reduce_scatter | solution.py:187
  628.9 287.3 %reduce-scatter.33.cloned.1.call-start = ((), (), s32[]{:S(2)}) async-start(), calls=%async_computation.20 | async-start | bytes 10485760 | tf_op jit(solution)/shard_map/reduce_scatter | solution.py:187
  636.2 354.2 %reduce-scatter.35.cloned.1.call-start = ((), (), s32[]{:S(2)}) async-start(), calls=%async_computation.21 | async-start | bytes 10485760 | tf_op jit(solution)/shard_map/reduce_scatter | solution.py:190
  643.3 421.6 %reduce-scatter.37.cloned.1.call-start = ((), (), s32[]{:S(2)}) async-start(), calls=%async_computation.22 | async-start | bytes 10485760 | tf_op jit(solution)/shard_map/reduce_scatter | solution.py:190
  650.4 436.9 %reduce-scatter.49.cloned.1.call-start = ((), (), s32[]{:S(2)}) async-start(), calls=%async_computation.36 | async-start | bytes 327680
  652.3 457.7 %reduce-scatter.45.cloned.1.call-start = ((), (), s32[]{:S(2)}) async-start(), calls=%async_computation.34 | async-start | bytes 327680
  653.3 479.2 %reduce-scatter.47.cloned.1.call-start = ((), (), s32[]{:S(2)}) async-start(), calls=%async_computation.35 | async-start | bytes 327680
  654.3 500.9 %reduce-scatter.43.cloned.1.call-start = ((), (), s32[]{:S(2)}) async-start(), calls=%async_computation.33 | async-start | bytes 327680
  655.3 924.7 %all-reduce.16.cloned.1.call-start = ((), (), s32[]{:S(2)}) async-start(), calls=%async_computation.37 | async-start | bytes 26214400 | tf_op jit(solution)/shard_map/psum | solution.py:204
  (83 other events, 299.6 us)
Sparse Core Ops, SparseCore 0:
  11.1 49.1 all-gather.23
  61.9 16.7 all-gather.21
  80.8 46.3 all-gather.31
  128.6 22.5 all-gather.25
  153.2 58.2 all-gather.27
  213.0 58.2 all-gather.29
  273.4 22.5 all-gather.33
  298.2 58.2 all-gather.35
  358.1 58.2 all-gather.37
  523.1 24.8 reduce-scatter.40
  550.7 24.8 reduce-scatter.38
  578.0 31.4 reduce-scatter.26
  612.7 31.4 reduce-scatter.28
  647.1 58.3 reduce-scatter.24
  708.1 58.3 reduce-scatter.22
  769.5 71.7 reduce-scatter.30
  844.5 71.6 reduce-scatter.32
  918.6 71.7 reduce-scatter.34
  993.1 71.6 reduce-scatter.36
  1067.2 20.0 reduce-scatter.48
  1089.9 20.0 reduce-scatter.44
  1112.4 20.0 reduce-scatter.46
  1135.1 20.0 reduce-scatter.42
  1161.5 418.4 all-reduce.15
where the time goes:
time: 1620 us; the launch traced here: 1610 us
  waiting for transfers between devices  1150 us (71%)
  matrix products  192 us (12%)
  local copies, waits for them, and re-layouts  148 us (9%)
  other arithmetic  54.8 us (3%)
  blocking collectives  43.8 us (3%)
    psum x1, waiting for transfers between devices, reduce_grads(): lax.psum(owned[0].astype(jnp.bfloat16), 'rep').astype(jnp.float32)  401 us
    reduce_scatter x2, waiting for transfers between devices, reduce_grads(): lax.psum_scatter(g_up.astype(jnp.bfloat16), 'shard', scatter_dimension=0,...  150 us
    reduce_scatter x2, waiting for transfers between devices, reduce_grads(): lax.psum_scatter(g_down.astype(jnp.bfloat16), 'shard', scatter_dimension=...  149 us
    reduce_scatter x2, waiting for transfers between devices, reduce_grads(): lax.psum_scatter(g_qkv.astype(jnp.bfloat16), 'shard', scatter_dimension=0...  111 us
    all_gather x2, waiting for transfers between devices, per_device(): lax.all_gather(w_down[layer_id], 'shard', axis=0, tiled=True)  101 us
    all_gather x2, waiting for transfers between devices, per_device(): lax.all_gather(w_up[layer_id], 'shard', axis=0, tiled=True)  84.7 us
    unnamed x28, waiting for transfers between devices  84.3 us
    all_gather x2, waiting for transfers between devices, per_device(): lax.all_gather(w_qkv[layer_id], 'shard', axis=0, tiled=True)  60.5 us
  transfers between devices with their start and end apart: 24, of which 18 were waited for; matrix products, arithmetic and copies ran while one was open for 16% of the time, Pallas kernels for 0%

commit v1 on v0

v1 whole, which is shorter than its diff:
```python
from functools import partial
import math

import jax
import jax.numpy as jnp
from jax import lax
from jax.experimental import pallas as pl
from jax.experimental.pallas import tpu as pltpu
from jax.sharding import PartitionSpec as P

D = 1024
H = 16
DH = 64
LAYERS = 2
LEN = 128
SPAN = 2 * LEN
SCALE = 1.0 / math.sqrt(3 * DH)
NEG_FILL = -1e30
NORM_EPS = 1e-07
F32 = jnp.float32
BF16 = jnp.bfloat16


def mm(a, b):
    return jnp.dot(a, b, preferred_element_type=F32)


def mm_nt(a, b):
    return lax.dot_general(a, b, (((1,), (1,)), ((), ())), preferred_element_type=F32)


def mm_tn(a, b):
    return lax.dot_general(a, b, (((0,), (0,)), ((), ())), preferred_element_type=F32)


def swap(value, axis, mask):
    size = lax.axis_size(axis)
    return lax.ppermute(value, axis, [(i, i ^ mask) for i in range(size)])


def rising_masks(axis):
    size = lax.axis_size(axis)
    masks, mask = [], 1
    while mask < size:
        masks.append(mask)
        mask *= 2
    return masks


def group_order(axis):
    order = [0]
    for mask in reversed(rising_masks(axis)):
        order = order + [place ^ mask for place in order]
    return order


def gather_tokens(rows):
    for mask in reversed(rising_masks("shard")):
        rows = jnp.concatenate([rows, swap(rows, "shard", mask)], axis=0)
    return rows


def scatter_tokens(partial_rows):
    total = partial_rows
    for mask in rising_masks("shard"):
        half = total.shape[0] // 2
        sent = total[half:].astype(BF16)
        total = total[:half] + swap(sent, "shard", mask).astype(F32)
    return total


def by_columns(owned, me):
    rows, parts, n, c = owned.shape
    whole = jnp.zeros((n * rows, parts * c), owned.dtype)
    for mask in range(n):
        other = jnp.bitwise_xor(me, mask)
        block = lax.dynamic_index_in_dim(owned, other, 2, keepdims=False).reshape(rows, parts * c)
        if mask:
            block = swap(block, "shard", mask)
        whole = lax.dynamic_update_slice(whole, block, (other * rows, 0))
    return whole


def by_rows(columns, me, n, parts):
    rows = columns.shape[0] // n
    c = columns.shape[1] // parts
    whole = jnp.zeros((rows, parts, n, c), columns.dtype)
    for mask in range(n):
        other = jnp.bitwise_xor(me, mask)
        block = lax.dynamic_slice_in_dim(columns, other * rows, rows, 0)
        if mask:
            block = swap(block, "shard", mask)
        block = block.reshape(rows, parts, 1, c)
        whole = lax.dynamic_update_slice(whole, block, (0, 0, other, 0))
    return whole.reshape(rows, parts * n * c)


def attention_forward_kernel(heads, qkv_ref, rel_ref, allowed_ref, context_ref, probs_ref):
    width = heads * DH
    allowed = allowed_ref[0] > 0
    for head in range(heads):
        at = head * DH
        q = qkv_ref[:, at : at + DH]
        k = qkv_ref[:, width + at : width + at + DH]
        v = qkv_ref[:, 2 * width + at : 2 * width + at + DH]
        rel_q = rel_ref[:, at : at + DH]
        rel_k = rel_ref[:, width + at : width + at + DH]
        by_key = pltpu.roll(mm_nt(q, rel_k), LEN + 1, 1, stride=1, stride_axis=0)[:, :LEN]
        by_query = pltpu.roll(mm_nt(k, rel_q), LEN + 1, 1, stride=1, stride_axis=0)[:, :LEN]
        scores = (mm_nt(q, k) + by_key + by_query.T) * SCALE
        masked = jnp.where(allowed, scores, NEG_FILL)
        terms = jnp.exp(masked - jnp.max(masked, axis=1, keepdims=True))
        probs = terms / jnp.sum(terms, axis=1, keepdims=True)
        probs_ref[0, head] = probs
        context_ref[:, at : at + DH] = mm(probs.astype(BF16), v).astype(BF16)


def attention_forward(qkv, rel_back, allowed, heads):
    count = allowed.shape[0]
    width = heads * DH
    return pl.pallas_call(
        partial(attention_forward_kernel, heads),
        grid=(count,),
        in_specs=[
            pl.BlockSpec((LEN, 3 * width), lambda s: (s, 0)),
            pl.BlockSpec((SPAN, 2 * width), lambda s: (0, 0)),
            pl.BlockSpec((1, LEN, LEN), lambda s: (s, 0, 0)),
        ],
        out_specs=[
            pl.BlockSpec((LEN, width), lambda s: (s, 0)),
            pl.BlockSpec((1, heads, LEN, LEN), lambda s: (s, 0, 0, 0)),
        ],
        out_shape=[
            jax.ShapeDtypeStruct((count * LEN, width), BF16),
            jax.ShapeDtypeStruct((count, heads, LEN, LEN), F32),
        ],
        compiler_params=pltpu.CompilerParams(vmem_limit_bytes=24 * 1024 * 1024),
        name="attention_forward",
    )(qkv, rel_back, allowed)


def attention_backward_kernel(heads, qkv_ref, rel_ref, probs_ref, grad_ref, dqkv_ref, drel_ref):
    width = heads * DH

    @pl.when(pl.program_id(0) == 0)
    def _():
        drel_ref[...] = jnp.zeros_like(drel_ref)

    row = lax.broadcasted_iota(jnp.int32, (LEN, LEN), 0)
    column = lax.broadcasted_iota(jnp.int32, (LEN, LEN), 1)
    flip = jnp.where(row + column == LEN - 1, 1.0, 0.0).astype(BF16)
    blank = jnp.zeros((LEN, LEN), F32)

    def spread(flipped):
        wide = jnp.concatenate([flipped, blank], axis=1)
        return pltpu.roll(wide, 0, 1, stride=1, stride_axis=0).astype(BF16)

    for head in range(heads):
        at = head * DH
        q = qkv_ref[:, at : at + DH]
        k = qkv_ref[:, width + at : width + at + DH]
        v = qkv_ref[:, 2 * width + at : 2 * width + at + DH]
        rel_q = rel_ref[:, at : at + DH]
        rel_k = rel_ref[:, width + at : width + at + DH]
        grad = grad_ref[:, at : at + DH]
        probs = probs_ref[0, head]
        d_value = mm_tn(probs.astype(BF16), grad)
        d_probs = mm_nt(grad, v)
        inner = jnp.sum(d_probs * probs, axis=1, keepdims=True)
        d_scores = (probs * (d_probs - inner)).astype(BF16)
        key_side = spread(mm(d_scores, flip))
        query_side = spread(mm_tn(d_scores, flip))
        d_query = (mm(d_scores, k) + mm(key_side, rel_k)) * SCALE
        d_key = (mm_tn(d_scores, q) + mm(query_side, rel_q)) * SCALE
        dqkv_ref[:, at : at + DH] = d_query.astype(BF16)
        dqkv_ref[:, width + at : width + at + DH] = d_key.astype(BF16)
        dqkv_ref[:, 2 * width + at : 2 * width + at + DH] = d_value.astype(BF16)
        drel_ref[:, at : at + DH] += mm_tn(query_side, k) * SCALE
        drel_ref[:, width + at : width + at + DH] += mm_tn(key_side, q) * SCALE


def attention_backward(qkv, rel_ahead, probs, d_context, heads):
    count = probs.shape[0]
    width = heads * DH
    return pl.pallas_call(
        partial(attention_backward_kernel, heads),
        grid=(count,),
        in_specs=[
            pl.BlockSpec((LEN, 3 * width), lambda s: (s, 0)),
            pl.BlockSpec((SPAN, 2 * width), lambda s: (0, 0)),
            pl.BlockSpec((1, heads, LEN, LEN), lambda s: (s, 0, 0, 0)),
            pl.BlockSpec((LEN, width), lambda s: (s, 0)),
        ],
        out_specs=[
            pl.BlockSpec((LEN, 3 * width), lambda s: (s, 0)),
            pl.BlockSpec((SPAN, 2 * width), lambda s: (0, 0)),
        ],
        out_shape=[
            jax.ShapeDtypeStruct((count * LEN, 3 * width), BF16),
            jax.ShapeDtypeStruct((SPAN, 2 * width), F32),
        ],
        compiler_params=pltpu.CompilerParams(vmem_limit_bytes=24 * 1024 * 1024),
        name="attention_backward",
    )(qkv, rel_ahead, probs, d_context)


def normed(values):
    centre = values - jnp.mean(values, axis=-1, keepdims=True)
    inverse = lax.rsqrt(jnp.mean(centre * centre, axis=-1, keepdims=True) + NORM_EPS)
    return centre * inverse, inverse


def norm_backward(upstream, values, gain):
    hat, inverse = normed(values)
    pushed = upstream * gain
    first = jnp.mean(pushed, axis=-1, keepdims=True)
    second = jnp.mean(pushed * hat, axis=-1, keepdims=True)
    back = inverse * (pushed - first - hat * second)
    return back, jnp.sum(upstream * hat, axis=0), jnp.sum(upstream, axis=0)


def gelu(x):
    return 0.5 * x * (1.0 + lax.erf(x * math.sqrt(0.5)))


def gelu_slope(x):
    density = jnp.exp(-0.5 * x * x) * (1.0 / math.sqrt(2.0 * math.pi))
    return 0.5 * (1.0 + lax.erf(x * math.sqrt(0.5))) + x * density


def over_replicas(value):
    return lax.psum(value.astype(BF16), "rep").astype(F32)


def per_device(
    tokens,
    cotangent,
    w_qkv,
    w_out,
    w_up,
    w_down,
    ln_gain,
    ln_bias,
    positions,
    segments,
    keep_mask,
    buckets,
):
    n = lax.axis_size("shard")
    me = lax.axis_index("shard")
    own = D // n
    heads = H // n
    ff_own = w_down.shape[1]
    order = group_order("shard")

    labels = gather_tokens(jnp.stack([segments, keep_mask]).reshape(1, 2, LEN).astype(F32))
    segment, keep = labels[:, 0], labels[:, 1]
    allowed = (segment[:, :, None] == segment[:, None, :]) & (keep[:, None, :] == 1.0)
    allowed = (allowed | jnp.eye(LEN, dtype=bool)[None]).astype(F32)
    norms = jnp.stack([ln_gain, ln_bias]).reshape(1, 2, LAYERS, own, 2)
    norms = lax.all_gather(norms, "shard", axis=0, tiled=True)
    norms = norms.transpose(1, 2, 4, 0, 3).reshape(2, LAYERS, 2, D).astype(F32)
    gains, biases = norms[0], norms[1]
    all_positions = lax.all_gather(positions, "shard", axis=0, tiled=True)
    ahead = jnp.concatenate([buckets, buckets[-1:]])
    back = jnp.concatenate([buckets[::-1], buckets[:1]])
    rows_used = jnp.take(all_positions, jnp.concatenate([back, ahead]), axis=0)
    rows_ahead = rows_used[SPAN:]

    weights = []
    for layer in range(LAYERS):
        qkv_cols = by_columns(w_qkv[layer].reshape(own, 3, n, own), me)
        up_cols = by_columns(w_up[layer].reshape(own, 1, n, ff_own), me)
        weights.append((qkv_cols, w_out[layer], up_cols, w_down[layer]))

    hidden = tokens.astype(F32)
    kept = []
    for layer in range(LAYERS):
        qkv_cols, out_rows, up_cols, down_rows = weights[layer]
        hidden_all = gather_tokens(hidden.astype(BF16))
        qkv = mm(hidden_all, qkv_cols).astype(BF16)
        rel = mm(rows_used, qkv_cols[:, : 2 * own]).astype(BF16)
        context, probs = attention_forward(qkv, rel[:SPAN], allowed, heads)
        attn_sum = hidden + scatter_tokens(mm(context, out_rows))
        mid = normed(attn_sum)[0] * gains[layer, 0] + biases[layer, 0]
        mid_all = gather_tokens(mid.astype(BF16))
        pre_act = mm(mid_all, up_cols)
        activation = gelu(pre_act).astype(BF16)
        ffn_sum = mid + scatter_tokens(mm(activation, down_rows))
        hidden = normed(ffn_sum)[0] * gains[layer, 1] + biases[layer, 1]
        kept.append(
            (hidden_all, qkv, rel[SPAN:], context, probs, attn_sum, mid_all, pre_act, activation, ffn_sum)
        )
    output = hidden.astype(BF16)

    upstream = cotangent.astype(F32)
    grads = [None] * LAYERS
    small = [None] * LAYERS
    row_grads = jnp.zeros((SPAN, D), F32)
    for layer in reversed(range(LAYERS)):
        qkv_cols, out_rows, up_cols, down_rows = weights[layer]
        hidden_all, qkv, rel, context, probs, attn_sum, mid_all, pre_act, activation, ffn_sum = kept[layer]
        d_ffn, d_gain_two, d_bias_two = norm_backward(upstream, ffn_sum, gains[layer, 1])
        branch_all = gather_tokens(d_ffn.astype(BF16))
        g_down = mm_tn(activation, branch_all)
        d_pre = (mm_nt(branch_all, down_rows) * gelu_slope(pre_act)).astype(BF16)
        g_up = mm_tn(mid_all, d_pre)
        d_mid = d_ffn + scatter_tokens(mm_nt(d_pre, up_cols))
        d_attn, d_gain_one, d_bias_one = norm_backward(d_mid, attn_sum, gains[layer, 0])
        att_all = gather_tokens(d_attn.astype(BF16))
        g_out = mm_tn(context, att_all)
        d_context = mm_nt(att_all, out_rows).astype(BF16)
        d_qkv, d_rel = attention_backward(qkv, rel, probs, d_context, heads)
        d_rel = d_rel.astype(BF16)
        g_qkv = mm_tn(hidden_all, d_qkv)
        g_qkv = g_qkv.at[:, : 2 * own].add(mm_tn(rows_ahead, d_rel))
        row_grads = row_grads + mm_nt(d_rel, qkv_cols[:, : 2 * own])
        upstream = d_attn + scatter_tokens(mm_nt(d_qkv, qkv_cols))
        grads[layer] = (
            over_replicas(by_rows(g_qkv.astype(BF16), me, n, 3)),
            over_replicas(g_out),
            over_replicas(by_rows(g_up.astype(BF16), me, n, 1)),
            over_replicas(g_down),
        )
        small[layer] = (
            jnp.stack([d_gain_one, d_gain_two]),
            jnp.stack([d_bias_one, d_bias_two]),
        )

    owned_rows = positions.shape[0]
    owners = jnp.bitwise_xor(me, jnp.array(order))
    row_ids = (owners[:, None] * owned_rows + jnp.arange(owned_rows)[None, :]).reshape(-1)
    live = jnp.arange(SPAN) < 2 * LEN - 1
    picks = ((row_ids[:, None] == ahead[None, :]) & live[None, :]).astype(BF16)
    position_part = mm(picks, row_grads.astype(BF16)).reshape(n, owned_rows * D)
    norm_part = jnp.stack(
        [jnp.stack([entry[0] for entry in small]), jnp.stack([entry[1] for entry in small])]
    )
    norm_part = norm_part.reshape(2, LAYERS, 2, n, own).transpose(3, 0, 1, 2, 4)
    norm_part = jnp.take(norm_part, owners, axis=0).reshape(n, 2 * LAYERS * 2 * own)
    packed = jnp.concatenate([position_part, norm_part], axis=1)
    packed = scatter_tokens(packed)
    packed = over_replicas(packed)[0]
    grad_positions = packed[: owned_rows * D].reshape(owned_rows, D)
    norm_part = packed[owned_rows * D :].reshape(2, LAYERS, 2, own).transpose(0, 1, 3, 2)
    return (
        output,
        upstream,
        jnp.stack([entry[0] for entry in grads]),
        jnp.stack([entry[1] for entry in grads]),
        jnp.stack([entry[2] for entry in grads]),
        jnp.stack([entry[3] for entry in grads]),
        norm_part[0],
        norm_part[1],
        grad_positions,
    )


def solution(mesh):
    tokens = P(("rep", "shard"), None)
    rows = P(None, "shard", None)
    labels = P(("rep", "shard"))
    return jax.shard_map(
        per_device,
        mesh=mesh,
        in_specs=(
            tokens,
            tokens,
            rows,
            rows,
            rows,
            rows,
            rows,
            rows,
            P("shard", None),
            labels,
            labels,
            P(),
        ),
        out_specs=(tokens, tokens, rows, rows, rows, rows, rows, rows, P("shard", None)),
        check_vma=False,
    )
```

time: 1620 us -> 1090 us (0.67)
  waiting for transfers between devices: 1150 us -> 589 us
  matrix products: 192 us -> 52.9 us
  local copies, waits for them, and re-layouts: 148 us -> 283 us
  starting transfers between devices: 1.56 us -> 41.8 us
  Pallas kernels: 0 us -> 39.7 us
  blocking collectives: 43.8 us -> 5.4 us
    reduce_scatter x10 -> x0, waiting for transfers between devices: 410 us -> none  [the longest x2 150 us: reduce_grads(): lax.psum_scatter(g_up.astype(jnp.bfloat16), 'shard', scatter_dimension=0,...]
    all_gather x9 -> x1, waiting for transfers between devices: 260 us -> 0.02 us  [per_device(): all_positions = lax.all_gather(positions, 'shard', axis=0, tiled=True)]
    ppermute x0 -> x60, waiting for transfers between devices: none -> 185 us  [swap(): return lax.ppermute(value, axis, [(i, i ^ mask) for i in range(size)])]
    dynamic_update_slice x0 -> x33, local copies, waits for them, and re-layouts: none -> 169 us  [the longest x17 159 us: by_rows(): whole = lax.dynamic_update_slice(whole, block, (0, 0, other, 0))]
    dot_general x54 -> x30, matrix products: 192 us -> 52.9 us  [the longest x10 20.7 us: mm_tn(): lax.dot_general(a, b, (((0,), (0,)), ((), ())), preferred_element_type=F32)]
    unnamed x28 -> x2, waiting for transfers between devices: 84.3 us -> 0.03 us
    ppermute x0 -> x60, starting transfers between devices: none -> 41.8 us  [swap(): return lax.ppermute(value, axis, [(i, i ^ mask) for i in range(size)])]
    pallas_call x0 -> x4, Pallas kernels: none -> 39.7 us  [the longest x2 20.9 us: attention_backward(): pl.pallas_call(partial(attention_backward_kernel, heads), grid=(count,),...]
  transfers between devices with their start and end apart: 24 -> 62, of which waited for: 18 -> 29; matrix products, arithmetic and copies ran while one was open for 16% -> 30% of each run, Pallas kernels for 0% -> 1%
where the time goes in v1:
time: 1090 us; the launch traced here: 1080 us
  waiting for transfers between devices  589 us (54%)
  local copies, waits for them, and re-layouts  283 us (26%)
  matrix products  52.9 us (5%)
  other arithmetic  47.9 us (4%)
  starting transfers between devices  41.8 us (4%)
  Pallas kernels  39.7 us (4%)
  between operations  16.4 us (2%)
    psum x1, waiting for transfers between devices, over_replicas(): return lax.psum(value.astype(BF16), 'rep').astype(F32)  404 us
    ppermute x60, waiting for transfers between devices, swap(): return lax.ppermute(value, axis, [(i, i ^ mask) for i in range(size)])  185 us
    dynamic_update_slice x17, local copies, waits for them, and re-layouts, by_rows(): whole = lax.dynamic_update_slice(whole, block, (0, 0, other, 0))  159 us
    ppermute x60, starting transfers between devices, swap(): return lax.ppermute(value, axis, [(i, i ^ mask) for i in range(size)])  41.8 us
    unnamed x189, local copies, waits for them, and re-layouts  22.8 us
    reshape x9, local copies, waits for them, and re-layouts, by_rows(): block = block.reshape(rows, parts, 1, c)  22.1 us
  transfers between devices with their start and end apart: 62, of which 29 were waited for; matrix products, arithmetic and copies ran while one was open for 30% of the time, Pallas kernels for 1%

profile of v1, /device:TPU:0, one launch (start us, length us, event | category | flops | bytes accessed | tf_op | source)
XLA Modules:
  0.0 1076.2 jit_solution(15048550519041986182)
XLA Ops:
  26.1 21.0 %collective-permute-done.5 = f32[1,2,128]{2,1,0:T(2,128)S(1)} collective-permute-done((f32[1,2,128]{2,1,0:T(2,128)S(1)}, f32[1,2,128]{2,1,0:T(2,128)S(1)}, u32[]{:S(2)}, u32[]{:S(2)}) %collective-permute-start.5) | collective-permute-done | bytes 1056 | tf_op jit(solution)/shard_map/ppermute | solution.py:38
  65.0 9.2 attention_forward.2
  78.8 5.4 all-gather
  114.7 7.2 collective-permute-done.12
  123.0 9.4 collective-permute-done.13
  144.0 6.6 collective-permute-done.15
  151.9 7.1 collective-permute-done.19
  159.1 6.9 collective-permute-done.20
  166.1 6.3 collective-permute-done.16
  175.4 9.5 attention_forward.3
  188.2 7.9 collective-permute-done.22
  210.9 6.2 collective-permute-done.26
  218.2 9.4 collective-permute-done.27
  236.4 6.9 collective-permute-done.29
  246.0 6.0 collective-permute-done.30
  261.0 6.8 collective-permute-done.33
  279.5 10.7 attention_backward.2
  300.7 24.6 %collective-permute-done.37 = bf16[128,1024]{1,0:T(8,128)(2,1)S(1)} collective-permute-done((bf16[128,1024]{1,0:T(8,128)(2,1)S(1)}, bf16[128,1024]{1,0:T(8,128)(2,1)S(1)}, u32[]{:S(2)}, u32[]{:S(2)}) %collective-permute-start.37) | collective-permute-done | bytes 262176 | tf_op jit(solution)/shard_map/ppermute | solution.py:38
  354.0 16.5 %dynamic_update_slice.116 = bf16[256,3,4,256]{3,2,1,0:T(4,128)(2,1)} dynamic-update-slice(bf16[256,3,4,256]{3,2,1,0:T(4,128)(2,1)} %broadcast.244.clone, bf16[256,3,1,256]{3,2,1,0:T(2,128)(2,1)S(1)} %copy.84, s32[]{:T(128)} %constant.151.clone.1, s32[]{:T(128)} %constant.151.clone.1, s32[]{:T(128)S(6)} %select_n.112, s32[]{:T(128)} %constant.151.clone.1) | dynamic-update-slice | bytes 786436 | tf_op jit(solution)/shard_map/dynamic_update_slice | solution.py:94
  378.8 16.5 %dynamic_update_slice.117 = bf16[256,3,4,256]{3,2,1,0:T(4,128)(2,1)} dynamic-update-slice(bf16[256,3,4,256]{3,2,1,0:T(4,128)(2,1)} %dynamic_update_slice.116, bf16[256,3,1,256]{3,2,1,0:T(2,128)(2,1)S(1)} %copy.85, s32[]{:T(128)} %constant.151.clone.1, s32[]{:T(128)} %constant.151.clone.1, s32[]{:T(128)S(6)} %select_n.114, s32[]{:T(128)} %constant.151.clone.1) | dynamic-update-slice | bytes 786436 | tf_op jit(solution)/shard_map/dynamic_update_slice | solution.py:94
  395.3 16.6 %dynamic_update_slice.118 = bf16[256,3,4,256]{3,2,1,0:T(4,128)(2,1)} dynamic-update-slice(bf16[256,3,4,256]{3,2,1,0:T(4,128)(2,1)} %dynamic_update_slice.117, bf16[256,3,1,256]{3,2,1,0:T(2,128)(2,1)} %copy.86, s32[]{:T(128)} %constant.151.clone.1, s32[]{:T(128)} %constant.151.clone.1, s32[]{:T(128)S(6)} %select_n.116, s32[]{:T(128)} %constant.151.clone.1) | dynamic-update-slice | bytes 786436 | tf_op jit(solution)/shard_map/dynamic_update_slice | solution.py:94
  412.0 16.5 %dynamic_update_slice.119 = bf16[256,3,4,256]{3,2,1,0:T(4,128)(2,1)} dynamic-update-slice(bf16[256,3,4,256]{3,2,1,0:T(4,128)(2,1)} %dynamic_update_slice.118, bf16[256,3,1,256]{3,2,1,0:T(2,128)(2,1)S(1)} %copy-done.33, s32[]{:T(128)} %constant.151.clone.1, s32[]{:T(128)} %constant.151.clone.1, s32[]{:T(128)S(6)} %select_n.118, s32[]{:T(128)} %constant.151.clone.1) | dynamic-update-slice | bytes 786436 | tf_op jit(solution)/shard_map/dynamic_update_slice | solution.py:94
  445.2 23.0 %collective-permute-done.41 = bf16[128,1024]{1,0:T(8,128)(2,1)S(1)} collective-permute-done((bf16[128,1024]{1,0:T(8,128)(2,1)S(1)}, bf16[128,1024]{1,0:T(8,128)(2,1)S(1)}, u32[]{:S(2)}, u32[]{:S(2)}) %collective-permute-start.41) | collective-permute-done | bytes 262176 | tf_op jit(solution)/shard_map/ppermute | solution.py:38
  481.3 10.2 attention_backward.3
  521.8 18.5 %dynamic_update_slice.123 = bf16[256,1,4,1024]{3,2,0,1:T(4,128)(2,1)} dynamic-update-slice(bf16[256,1,4,1024]{3,2,0,1:T(4,128)(2,1)} %copy.88, bf16[256,1,1,1024]{3,2,0,1:T(2,128)(2,1)S(1)} %copy.89, s32[]{:T(128)} %constant.151.clone.1, s32[]{:T(128)} %constant.151.clone.1, s32[]{:T(128)S(6)} %select_n.118, s32[]{:T(128)} %constant.151.clone.1) | dynamic-update-slice | bytes 1048580 | tf_op jit(solution)/shard_map/dynamic_update_slice | solution.py:94
  547.1 16.5 %dynamic_update_slice.112 = bf16[256,3,4,256]{3,2,1,0:T(4,128)(2,1)} dynamic-update-slice(bf16[256,3,4,256]{3,2,1,0:T(4,128)(2,1)} %broadcast.244.clone.1, bf16[256,3,1,256]{3,2,1,0:T(2,128)(2,1)S(1)} %copy.80, s32[]{:T(128)} %constant.151.clone.1, s32[]{:T(128)} %constant.151.clone.1, s32[]{:T(128)S(6)} %select_n.112, s32[]{:T(128)} %constant.151.clone.1) | dynamic-update-slice | bytes 786436 | tf_op jit(solution)/shard_map/dynamic_update_slice | solution.py:94
  574.2 16.5 %dynamic_update_slice.113 = bf16[256,3,4,256]{3,2,1,0:T(4,128)(2,1)} dynamic-update-slice(bf16[256,3,4,256]{3,2,1,0:T(4,128)(2,1)} %dynamic_update_slice.112, bf16[256,3,1,256]{3,2,1,0:T(2,128)(2,1)S(1)} %copy.81, s32[]{:T(128)} %constant.151.clone.1, s32[]{:T(128)} %constant.151.clone.1, s32[]{:T(128)S(6)} %select_n.114, s32[]{:T(128)} %constant.151.clone.1) | dynamic-update-slice | bytes 786436 | tf_op jit(solution)/shard_map/dynamic_update_slice | solution.py:94
  590.7 16.6 %dynamic_update_slice.114 = bf16[256,3,4,256]{3,2,1,0:T(4,128)(2,1)} dynamic-update-slice(bf16[256,3,4,256]{3,2,1,0:T(4,128)(2,1)} %dynamic_update_slice.113, bf16[256,3,1,256]{3,2,1,0:T(2,128)(2,1)} %copy.82, s32[]{:T(128)} %constant.151.clone.1, s32[]{:T(128)} %constant.151.clone.1, s32[]{:T(128)S(6)} %select_n.116, s32[]{:T(128)} %constant.151.clone.1) | dynamic-update-slice | bytes 786436 | tf_op jit(solution)/shard_map/dynamic_update_slice | solution.py:94
  607.4 16.5 %dynamic_update_slice.115 = bf16[256,3,4,256]{3,2,1,0:T(4,128)(2,1)} dynamic-update-slice(bf16[256,3,4,256]{3,2,1,0:T(4,128)(2,1)} %dynamic_update_slice.114, bf16[256,3,1,256]{3,2,1,0:T(2,128)(2,1)S(1)} %copy-done.32, s32[]{:T(128)} %constant.151.clone.1, s32[]{:T(128)} %constant.151.clone.1, s32[]{:T(128)S(6)} %select_n.118, s32[]{:T(128)} %constant.151.clone.1) | dynamic-update-slice | bytes 786436 | tf_op jit(solution)/shard_map/dynamic_update_slice | solution.py:94
  635.7 8.0 collective-permute-done.45
  644.6 403.9 %all-reduce.3.cloned.1.call-done = (bf16[1,256,3072]{2,1,0:T(8,128)(2,1)}, bf16[1,256,3072]{2,1,0:T(8,128)(2,1)}, bf16[1,256,1024]{2,1,0:T(8,128)(2,1)}, bf16[1,...) async-done(((bf16[1,256,3072]{2,1,0:T(8,128)(2,1)}, ...) | async-done | bytes 12849168 | tf_op jit(solution)/shard_map/psum | solution.py:232
  1053.2 5.1 maximum_convert_fusion.2
  (507 shorter events, 291.5 us)
Async XLA Ops:
  7.2 51.3 %all-gather.3.cloned.1.call-start = ((), (), s32[]{:S(2)}) async-start(), calls=%async_computation | async-start | bytes 1310720 | tf_op jit(solution)/shard_map/all_gather | solution.py:264
  7.2 41.3 %collective-permute-start = (bf16[128,1024]{1,0:T(8,128)(2,1)}, bf16[128,1024]{1,0:T(8,128)(2,1)}, u32[]{:S(2)}, u32[]{:S(2)}) collective-permute-start(bf16[128,1024]{1,0:T(8,128)(2,1)} %param.17), channel_id=1, source_target_pairs={{0,2},{1,3},{2,0},{3,1},{4,6},{5,7},{6,4},{7,5},{8,10},{9,11},{10,... | collective-permute-start | bytes 786440 | tf_op jit(solution)/shard_map/ppermute | solution.py:38
  21.3 29.9 %collective-permute-start.2 = (bf16[256,768]{0,1:T(8,128)(2,1)}, bf16[256,768]{0,1:T(8,128)(2,1)}, u32[]{:S(2)}, u32[]{:S(2)}) collective-permute-start(bf16[256,768]{0,1:T(8,128)(2,1)} %bitcast.2), channel_id=1, source_target_pairs={{0,1},{1,0},{2,3},{3,2},{4,5},{5,4},{6,7},{7,6},{8,9},{9,8},{10,11... | collective-permute-start | bytes 1179656 | tf_op jit(solution)/shard_map/ppermute | solution.py:38
  21.3 31.0 %collective-permute-start.3 = (bf16[256,768]{0,1:T(8,128)(2,1)}, bf16[256,768]{0,1:T(8,128)(2,1)}, u32[]{:S(2)}, u32[]{:S(2)}) collective-permute-start(bf16[256,768]{0,1:T(8,128)(2,1)} %bitcast.3), channel_id=1, source_target_pairs={{0,2},{1,3},{2,0},{3,1},{4,6},{5,7},{6,4},{7,5},{8,10},{9,11},{10,... | collective-permute-start | bytes 1179656 | tf_op jit(solution)/shard_map/ppermute | solution.py:38
  21.3 32.0 %collective-permute-start.4 = (bf16[256,768]{0,1:T(8,128)(2,1)}, bf16[256,768]{0,1:T(8,128)(2,1)}, u32[]{:S(2)}, u32[]{:S(2)}) collective-permute-start(bf16[256,768]{0,1:T(8,128)(2,1)} %bitcast.4), channel_id=1, source_target_pairs={{0,3},{1,2},{2,1},{3,0},{4,7},{5,6},{6,5},{7,4},{8,11},{9,10},{10,... | collective-permute-start | bytes 1179656 | tf_op jit(solution)/shard_map/ppermute | solution.py:38
  23.2 1025.3 %all-reduce.3.cloned.1.call-start = ((), (), s32[]{:S(2)}) async-start(), calls=%async_computation.1 | async-start | bytes 26230784 | tf_op jit(solution)/shard_map/psum | solution.py:232
  23.2 23.8 %collective-permute-start.5 = (f32[1,2,128]{2,1,0:T(2,128)S(1)}, f32[1,2,128]{2,1,0:T(2,128)S(1)}, u32[]{:S(2)}, u32[]{:S(2)}) collective-permute-start(f32[1,2,128]{2,1,0:T(2,128)S(1)} %add_convert_fusion.1), channel_id=1, source_target_pairs={{0,2},{1,3},{2,0},{3,1},{4,6},{5,7},{6,4},{7,5},{8,10},{9,11},{10,... | collective-permute-start | bytes 3080 | tf_op jit(solution)/shard_map/ppermute | solution.py:38
  97.9 14.0 %collective-permute-start.9 = (bf16[128,1024]{1,0:T(8,128)(2,1)}, bf16[128,1024]{1,0:T(8,128)(2,1)}, u32[]{:S(2)}, u32[]{:S(2)}) collective-permute-start(bf16[128,1024]{1,0:T(8,128)(2,1)} %fusion.67), channel_id=1, source_target_pairs={{0,2},{1,3},{2,0},{3,1},{4,6},{5,7},{6,4},{7,5},{8,10},{9,11},{10,... | collective-permute-start | bytes 786440 | tf_op jit(solution)/shard_map/ppermute | solution.py:38
  106.9 15.0 %collective-permute-start.12 = (bf16[256,1024]{1,0:T(8,128)(2,1)}, bf16[256,1024]{1,0:T(8,128)(2,1)}, u32[]{:S(2)}, u32[]{:S(2)}) collective-permute-start(bf16[256,1024]{1,0:T(8,128)(2,1)} %bitcast.164), channel_id=1, source_target_pairs={{0,2},{1,3},{2,0},{3,1},{4,6},{5,7},{6,4},{7,5},{8,10},{9,11},{10,... | collective-permute-start | bytes 1572872 | tf_op jit(solution)/shard_map/ppermute | solution.py:38
  109.4 23.0 %collective-permute-start.13 = (bf16[256,1024]{1,0:T(8,128)(2,1)}, bf16[256,1024]{1,0:T(8,128)(2,1)}, u32[]{:S(2)}, u32[]{:S(2)}) collective-permute-start(bf16[256,1024]{1,0:T(8,128)(2,1)} %bitcast.162), channel_id=1, source_target_pairs={{0,3},{1,2},{2,1},{3,0},{4,7},{5,6},{6,5},{7,4},{8,11},{9,10},{10,... | collective-permute-start | bytes 1572872 | tf_op jit(solution)/shard_map/ppermute | solution.py:38
  112.9 20.6 %collective-permute-start.10 = (bf16[256,1024]{1,0:T(8,128)(2,1)S(1)}, bf16[256,1024]{1,0:T(8,128)(2,1)S(1)}, u32[]{:S(2)}, u32[]{:S(2)}) collective-permute-start(bf16[256,1024]{1,0:T(8,128)(2,1)S(1)} %pad_maximum_fusion.9), channel_id=1, source_target_pairs={{0,1},{1,0},{2,3},{3,2},{4,5},{5,4},{6,7},{7,6},{8,9},{9,8},{10,11... | collective-permute-start | bytes 1572872 | tf_op jit(solution)/shard_map/ppermute | solution.py:38
  141.9 17.1 %collective-permute-start.19 = (bf16[256,768]{0,1:T(8,128)(2,1)S(1)}, bf16[256,768]{0,1:T(8,128)(2,1)S(1)}, u32[]{:S(2)}, u32[]{:S(2)}) collective-permute-start(bf16[256,768]{0,1:T(8,128)(2,1)S(1)} %bitcast.168), channel_id=1, source_target_pairs={{0,2},{1,3},{2,0},{3,1},{4,6},{5,7},{6,4},{7,5},{8,10},{9,11},{10,... | collective-permute-start | bytes 1179656 | tf_op jit(solution)/shard_map/ppermute | solution.py:38
  143.5 22.4 %collective-permute-start.20 = (bf16[256,768]{0,1:T(8,128)(2,1)S(1)}, bf16[256,768]{0,1:T(8,128)(2,1)S(1)}, u32[]{:S(2)}, u32[]{:S(2)}) collective-permute-start(bf16[256,768]{0,1:T(8,128)(2,1)S(1)} %bitcast.167), channel_id=1, source_target_pairs={{0,3},{1,2},{2,1},{3,0},{4,7},{5,6},{6,5},{7,4},{8,11},{9,10},{10,... | collective-permute-start | bytes 1179656 | tf_op jit(solution)/shard_map/ppermute | solution.py:38
  151.3 21.1 %collective-permute-start.16 = (bf16[128,1024]{1,0:T(8,128)(2,1)S(1)}, bf16[128,1024]{1,0:T(8,128)(2,1)S(1)}, u32[]{:S(2)}, u32[]{:S(2)}) collective-permute-start(bf16[128,1024]{1,0:T(8,128)(2,1)S(1)} %fusion.68), channel_id=1, source_target_pairs={{0,2},{1,3},{2,0},{3,1},{4,6},{5,7},{6,4},{7,5},{8,10},{9,11},{10,... | collective-permute-start | bytes 786440 | tf_op jit(solution)/shard_map/ppermute | solution.py:38
  202.1 15.0 %collective-permute-start.26 = (bf16[256,1024]{1,0:T(8,128)(2,1)}, bf16[256,1024]{1,0:T(8,128)(2,1)}, u32[]{:S(2)}, u32[]{:S(2)}) collective-permute-start(bf16[256,1024]{1,0:T(8,128)(2,1)} %bitcast.163), channel_id=1, source_target_pairs={{0,2},{1,3},{2,0},{3,1},{4,6},{5,7},{6,4},{7,5},{8,10},{9,11},{10,... | collective-permute-start | bytes 1572872 | tf_op jit(solution)/shard_map/ppermute | solution.py:38
  205.7 21.9 %collective-permute-start.27 = (bf16[256,1024]{1,0:T(8,128)(2,1)}, bf16[256,1024]{1,0:T(8,128)(2,1)}, u32[]{:S(2)}, u32[]{:S(2)}) collective-permute-start(bf16[256,1024]{1,0:T(8,128)(2,1)} %bitcast.161), channel_id=1, source_target_pairs={{0,3},{1,2},{2,1},{3,0},{4,7},{5,6},{6,5},{7,4},{8,11},{9,10},{10,... | collective-permute-start | bytes 1572872 | tf_op jit(solution)/shard_map/ppermute | solution.py:38
  209.1 19.5 %collective-permute-start.24 = (bf16[256,1024]{1,0:T(8,128)(2,1)S(1)}, bf16[256,1024]{1,0:T(8,128)(2,1)S(1)}, u32[]{:S(2)}, u32[]{:S(2)}) collective-permute-start(bf16[256,1024]{1,0:T(8,128)(2,1)S(1)} %pad_maximum_fusion.11), channel_id=1, source_target_pairs={{0,1},{1,0},{2,3},{3,2},{4,5},{5,4},{6,7},{7,6},{8,9},{9,8},{10,11... | collective-permute-start | bytes 1572872 | tf_op jit(solution)/shard_map/ppermute | solution.py:38
  294.5 33.8 %collective-permute-start.56 = (bf16[256,1024]{0,1:T(8,128)(2,1)S(1)}, bf16[256,1024]{0,1:T(8,128)(2,1)S(1)}, u32[]{:S(2)}, u32[]{:S(2)}) collective-permute-start(bf16[256,1024]{0,1:T(8,128)(2,1)S(1)} %get-tuple-element.101), channel_id=1, source_target_pairs={{0,2},{1,3},{2,0},{3,1},{4,6},{5,7},{6,4},{7,5},{8,10},{9,11},{10,... | collective-permute-start | bytes 1572872 | tf_op jit(solution)/shard_map/ppermute | solution.py:38
  296.0 32.3 %collective-permute-start.57 = (bf16[256,1024]{0,1:T(8,128)(2,1)S(1)}, bf16[256,1024]{0,1:T(8,128)(2,1)S(1)}, u32[]{:S(2)}, u32[]{:S(2)}) collective-permute-start(bf16[256,1024]{0,1:T(8,128)(2,1)S(1)} %get-tuple-element.100), channel_id=1, source_target_pairs={{0,3},{1,2},{2,1},{3,0},{4,7},{5,6},{6,5},{7,4},{8,11},{9,10},{10,... | collective-permute-start | bytes 1572872 | tf_op jit(solution)/shard_map/ppermute | solution.py:38
  298.8 26.4 %collective-permute-start.37 = (bf16[128,1024]{1,0:T(8,128)(2,1)S(1)}, bf16[128,1024]{1,0:T(8,128)(2,1)S(1)}, u32[]{:S(2)}, u32[]{:S(2)}) collective-permute-start(bf16[128,1024]{1,0:T(8,128)(2,1)S(1)} %slice.537), channel_id=1, source_target_pairs={{0,2},{1,3},{2,0},{3,1},{4,6},{5,7},{6,4},{7,5},{8,10},{9,11},{10,... | collective-permute-start | bytes 786440 | tf_op jit(solution)/shard_map/ppermute | solution.py:38
  340.9 29.6 %collective-permute-start.49 = (bf16[256,768]{0,1:T(8,128)(2,1)}, bf16[256,768]{0,1:T(8,128)(2,1)}, u32[]{:S(2)}, u32[]{:S(2)}) collective-permute-start(bf16[256,768]{0,1:T(8,128)(2,1)} %get-tuple-element.117), channel_id=1, source_target_pairs={{0,1},{1,0},{2,3},{3,2},{4,5},{5,4},{6,7},{7,6},{8,9},{9,8},{10,11... | collective-permute-start | bytes 1179656 | tf_op jit(solution)/shard_map/ppermute | solution.py:38
  341.3 31.5 %collective-permute-start.50 = (bf16[256,768]{0,1:T(8,128)(2,1)}, bf16[256,768]{0,1:T(8,128)(2,1)}, u32[]{:S(2)}, u32[]{:S(2)}) collective-permute-start(bf16[256,768]{0,1:T(8,128)(2,1)} %get-tuple-element.116), channel_id=1, source_target_pairs={{0,2},{1,3},{2,0},{3,1},{4,6},{5,7},{6,4},{7,5},{8,10},{9,11},{10,... | collective-permute-start | bytes 1179656 | tf_op jit(solution)/shard_map/ppermute | solution.py:38
  342.9 33.0 %collective-permute-start.51 = (bf16[256,768]{0,1:T(8,128)(2,1)}, bf16[256,768]{0,1:T(8,128)(2,1)}, u32[]{:S(2)}, u32[]{:S(2)}) collective-permute-start(bf16[256,768]{0,1:T(8,128)(2,1)} %get-tuple-element.115), channel_id=1, source_target_pairs={{0,3},{1,2},{2,1},{3,0},{4,7},{5,6},{6,5},{7,4},{8,11},{9,10},{10,... | collective-permute-start | bytes 1179656 | tf_op jit(solution)/shard_map/ppermute | solution.py:38
  348.3 90.3 %collective-permute-start.40 = (bf16[256,1024]{1,0:T(8,128)(2,1)}, bf16[256,1024]{1,0:T(8,128)(2,1)}, u32[]{:S(2)}, u32[]{:S(2)}) collective-permute-start(bf16[256,1024]{1,0:T(8,128)(2,1)} %slice.527), channel_id=1, source_target_pairs={{0,1},{1,0},{2,3},{3,2},{4,5},{5,4},{6,7},{7,6},{8,9},{9,8},{10,11... | collective-permute-start | bytes 1572872 | tf_op jit(solution)/shard_map/ppermute | solution.py:38
  436.8 36.7 %collective-permute-start.52 = (bf16[256,1024]{0,1:T(8,128)(2,1)S(1)}, bf16[256,1024]{0,1:T(8,128)(2,1)S(1)}, u32[]{:S(2)}, u32[]{:S(2)}) collective-permute-start(bf16[256,1024]{0,1:T(8,128)(2,1)S(1)} %get-tuple-element.99), channel_id=1, source_target_pairs={{0,1},{1,0},{2,3},{3,2},{4,5},{5,4},{6,7},{7,6},{8,9},{9,8},{10,11... | collective-permute-start | bytes 1572872 | tf_op jit(solution)/shard_map/ppermute | solution.py:38
  436.8 74.7 %collective-permute-start.53 = (bf16[256,1024]{0,1:T(8,128)(2,1)}, bf16[256,1024]{0,1:T(8,128)(2,1)}, u32[]{:S(2)}, u32[]{:S(2)}) collective-permute-start(bf16[256,1024]{0,1:T(8,128)(2,1)} %get-tuple-element.98), channel_id=1, source_target_pairs={{0,2},{1,3},{2,0},{3,1},{4,6},{5,7},{6,4},{7,5},{8,10},{9,11},{10,... | collective-permute-start | bytes 1572872 | tf_op jit(solution)/shard_map/ppermute | solution.py:38
  438.4 80.9 %collective-permute-start.54 = (bf16[256,1024]{0,1:T(8,128)(2,1)}, bf16[256,1024]{0,1:T(8,128)(2,1)}, u32[]{:S(2)}, u32[]{:S(2)}) collective-permute-start(bf16[256,1024]{0,1:T(8,128)(2,1)} %get-tuple-element.97), channel_id=1, source_target_pairs={{0,3},{1,2},{2,1},{3,0},{4,7},{5,6},{6,5},{7,4},{8,11},{9,10},{10,... | collective-permute-start | bytes 1572872 | tf_op jit(solution)/shard_map/ppermute | solution.py:38
  439.9 28.3 %collective-permute-start.41 = (bf16[128,1024]{1,0:T(8,128)(2,1)S(1)}, bf16[128,1024]{1,0:T(8,128)(2,1)S(1)}, u32[]{:S(2)}, u32[]{:S(2)}) collective-permute-start(bf16[128,1024]{1,0:T(8,128)(2,1)S(1)} %slice.536), channel_id=1, source_target_pairs={{0,2},{1,3},{2,0},{3,1},{4,6},{5,7},{6,4},{7,5},{8,10},{9,11},{10,... | collective-permute-start | bytes 786440 | tf_op jit(solution)/shard_map/ppermute | solution.py:38
  506.4 59.6 %collective-permute-start.46 = (bf16[256,768]{0,1:T(8,128)(2,1)}, bf16[256,768]{0,1:T(8,128)(2,1)}, u32[]{:S(2)}, u32[]{:S(2)}) collective-permute-start(bf16[256,768]{0,1:T(8,128)(2,1)} %get-tuple-element.113), channel_id=1, source_target_pairs={{0,1},{1,0},{2,3},{3,2},{4,5},{5,4},{6,7},{7,6},{8,9},{9,8},{10,11... | collective-permute-start | bytes 1179656 | tf_op jit(solution)/shard_map/ppermute | solution.py:38
  506.8 61.5 %collective-permute-start.47 = (bf16[256,768]{0,1:T(8,128)(2,1)}, bf16[256,768]{0,1:T(8,128)(2,1)}, u32[]{:S(2)}, u32[]{:S(2)}) collective-permute-start(bf16[256,768]{0,1:T(8,128)(2,1)} %get-tuple-element.112), channel_id=1, source_target_pairs={{0,2},{1,3},{2,0},{3,1},{4,6},{5,7},{6,4},{7,5},{8,10},{9,11},{10,... | collective-permute-start | bytes 1179656 | tf_op jit(solution)/shard_map/ppermute | solution.py:38
  508.4 62.9 %collective-permute-start.48 = (bf16[256,768]{0,1:T(8,128)(2,1)}, bf16[256,768]{0,1:T(8,128)(2,1)}, u32[]{:S(2)}, u32[]{:S(2)}) collective-permute-start(bf16[256,768]{0,1:T(8,128)(2,1)} %get-tuple-element.111), channel_id=1, source_target_pairs={{0,3},{1,2},{2,1},{3,0},{4,7},{5,6},{6,5},{7,4},{8,11},{9,10},{10,... | collective-permute-start | bytes 1179656 | tf_op jit(solution)/shard_map/ppermute | solution.py:38
  511.5 116.5 %collective-permute-start.59 = (bf16[1,133120]{1,0:T(2,128)(2,1)}, bf16[1,133120]{1,0:T(2,128)(2,1)}, u32[]{:S(2)}, u32[]{:S(2)}) collective-permute-start(bf16[1,133120]{1,0:T(2,128)(2,1)} %slice.534), channel_id=1, source_target_pairs={{0,2},{1,3},{2,0},{3,1},{4,6},{5,7},{6,4},{7,5},{8,10},{9,11},{10,... | collective-permute-start | bytes 798728 | tf_op jit(solution)/shard_map/ppermute | solution.py:38
  (120 other events, 842.4 us)
Sparse Core Ops, SparseCore 0:
  23.3 22.7 all-gather.2
  630.5 417.8 all-reduce.2

commit v2 on v1

--- a/solution.py
+++ b/solution.py
@@ -14,6 +14,8 @@
 LAYERS = 2
 LEN = 128
 SPAN = 2 * LEN
+FIRST_ROW = 160
+LIVE_ROWS = 192
 SCALE = 1.0 / math.sqrt(3 * DH)
 NEG_FILL = -1e30
 NORM_EPS = 1e-07
@@ -60,6 +62,21 @@
     return rows
 
 
+def gather_positions(positions, n, me):
+    last_row = FIRST_ROW + LIVE_ROWS
+    rows = positions.shape[0]
+    if n != 4 or FIRST_ROW // rows != 1 or (last_row - 1) // rows != 2:
+        whole = lax.all_gather(positions, "shard", axis=0, tiled=True)
+        return whole[FIRST_ROW:last_row]
+    size = LIVE_ROWS // 2
+    mine = jnp.where(me == 1, positions[rows - size :], positions[:size])
+    passed = lax.ppermute(mine, "shard", [(1, 3), (2, 0)])
+    held = jnp.where((me == 1) | (me == 2), mine, passed)
+    other = swap(held, "shard", 1)
+    low = me % 2 == 1
+    return jnp.concatenate([jnp.where(low, held, other), jnp.where(low, other, held)], axis=0)
+
+
 def scatter_tokens(partial_rows):
     total = partial_rows
     for mask in rising_masks("shard"):
@@ -69,30 +86,145 @@
     return total
 
 
-def by_columns(owned, me):
-    rows, parts, n, c = owned.shape
+def by_columns(owned, me, n, parts):
+    rows = owned.shape[0]
+    c = owned.shape[1] // (parts * n)
     whole = jnp.zeros((n * rows, parts * c), owned.dtype)
     for mask in range(n):
         other = jnp.bitwise_xor(me, mask)
-        block = lax.dynamic_index_in_dim(owned, other, 2, keepdims=False).reshape(rows, parts * c)
+        block = [
+            lax.dynamic_slice(owned, (0, (part * n + other) * c), (rows, c)) for part in range(parts)
+        ]
+        block = block[0] if parts == 1 else jnp.concatenate(block, axis=1)
         if mask:
             block = swap(block, "shard", mask)
         whole = lax.dynamic_update_slice(whole, block, (other * rows, 0))
     return whole
 
 
-def by_rows(columns, me, n, parts):
-    rows = columns.shape[0] // n
-    c = columns.shape[1] // parts
-    whole = jnp.zeros((rows, parts, n, c), columns.dtype)
+def halve(value, masks, axis):
+    me = lax.axis_index("rep")
+    for mask in masks:
+        size = value.shape[axis] // 2
+        upper = (jnp.bitwise_and(me, mask) != 0).astype(jnp.int32)
+        sent = lax.dynamic_slice_in_dim(value, (1 - upper) * size, size, axis)
+        held = lax.dynamic_slice_in_dim(value, upper * size, size, axis)
+        value = (held.astype(F32) + swap(sent, "rep", mask).astype(F32)).astype(BF16)
+    return value
+
+
+def double(value, masks):
+    for mask in reversed(masks[1:]):
+        value = jnp.concatenate([value, swap(value, "rep", mask)], axis=0)
+    return value, swap(value, "rep", masks[0])
+
+
+def block_places(masks):
+    reps = lax.axis_size("rep")
+    order = [0]
+    for mask in reversed(masks):
+        order = order + [place ^ mask for place in order]
+    owners = jnp.bitwise_xor(lax.axis_index("rep"), jnp.array(order, jnp.int32))
+    places = jnp.zeros((reps,), jnp.int32)
+    weight = reps
+    for mask in masks:
+        weight //= 2
+        places = places + weight * (jnp.bitwise_and(owners, mask) != 0).astype(jnp.int32)
+    return places
+
+
+def place_kernel(parts, n, c, half, index_ref, near_ref, far_ref, *rest):
+    out_ref = rest[-1]
+    step = pl.program_id(0)
+
+    def put(source):
+        if n == 0:
+            out_ref[0] = source[0].astype(F32)
+            return
+        for mask in range(n):
+            start = index_ref[half * 2 + mask] * c
+            for part in range(parts):
+                at = pl.multiple_of(start + part * n * c, c)
+                out_ref[0, :, pl.ds(at, c)] = source[0, mask, :, part * c : (part + 1) * c].astype(F32)
+
+    @pl.when(step < half)
+    def _():
+        put(near_ref)
+
+    @pl.when(step >= half)
+    def _():
+        put(far_ref)
+
+
+def place(near, far, index, layer, out, shape, parts, n):
+    half = near.shape[0]
+    rows = shape[1] // (2 * half)
+    block = (1,) + near.shape[1:]
+    zeros = (0,) * (len(block) - 1)
+    c = shape[2] // (parts * n) if n else 0
+    in_specs = [
+        pl.BlockSpec(block, lambda s, index: (jnp.minimum(s, half - 1),) + zeros),
+        pl.BlockSpec(block, lambda s, index: (jnp.maximum(s - half, 0),) + zeros),
+    ]
+    operands = [index, near, far]
+    aliases = {}
+    if out is not None:
+        in_specs.append(pl.BlockSpec(memory_space=pl.ANY))
+        operands.append(out)
+        aliases = {3: 0}
+    return pl.pallas_call(
+        partial(place_kernel, parts, n, c, half),
+        grid_spec=pltpu.PrefetchScalarGridSpec(
+            num_scalar_prefetch=1,
+            grid=(2 * half,),
+            in_specs=in_specs,
+            out_specs=pl.BlockSpec((1, rows, shape[2]), lambda s, index: (layer, index[s], 0)),
+        ),
+        out_shape=jax.ShapeDtypeStruct(shape, F32),
+        input_output_aliases=aliases,
+        compiler_params=pltpu.CompilerParams(vmem_limit_bytes=24 * 1024 * 1024),
+        name="place",
+    )(*operands)
+
+
+def reduced_rows(grad, masks, layer, out):
+    rows, columns = grad.shape
+    reps = lax.axis_size("rep")
+    shape = (LAYERS, rows, columns)
+    if (rows // reps) % 16:
+        total = lax.psum(grad.astype(BF16), "rep").astype(F32)
+        out = jnp.zeros(shape, F32) if out is None else out
+        return out.at[layer].set(total)
+    mine = halve(grad.astype(BF16), masks, 0)
+    near, far = double(mine[None], masks)
+    return place(near, far, block_places(masks), layer, out, shape, 1, 0)
+
+
+def reduced_columns(grad, masks, layer, out, parts):
+    n = lax.axis_size("shard")
+    me = lax.axis_index("shard")
+    reps = lax.axis_size("rep")
+    rows = grad.shape[0] // n
+    c = grad.shape[1] // parts
+    shape = (LAYERS, rows, parts * n * c)
+    grad = grad.astype(BF16).reshape(n, rows, parts * c)
+    exact = (rows // reps) % 16 == 0 and c % 128 == 0
+    if exact:
+        grad = halve(grad, masks, 1)
+    blocks = []
     for mask in range(n):
-        other = jnp.bitwise_xor(me, mask)
-        block = lax.dynamic_slice_in_dim(columns, other * rows, rows, 0)
-        if mask:
-            block = swap(block, "shard", mask)
-        block = block.reshape(rows, parts, 1, c)
-        whole = lax.dynamic_update_slice(whole, block, (0, 0, other, 0))
-    return whole.reshape(rows, parts * n * c)
+        block = lax.dynamic_index_in_dim(grad, jnp.bitwise_xor(me, mask), 0, keepdims=False)
+        blocks.append(swap(block, "shard", mask) if mask else block)
+    blocks = jnp.stack(blocks)
+    others = jnp.bitwise_xor(me, jnp.arange(n, dtype=jnp.int32))
+    if exact:
+        near, far = double(blocks[None], masks)
+        index = jnp.concatenate([block_places(masks), others])
+        return place(near, far, index, layer, out, shape, parts, n)
+    total = lax.psum(jnp.take(blocks, others, axis=0), "rep").astype(F32)
+    total = total.reshape(n, rows, parts, c).transpose(1, 2, 0, 3).reshape(rows, parts * n * c)
+    out = jnp.zeros(shape, F32) if out is None else out
+    return out.at[layer].set(total)
 
 
 def attention_forward_kernel(heads, qkv_ref, rel_ref, allowed_ref, context_ref, probs_ref):
@@ -228,10 +360,6 @@
     return 0.5 * (1.0 + lax.erf(x * math.sqrt(0.5))) + x * density
 
 
-def over_replicas(value):
-    return lax.psum(value.astype(BF16), "rep").astype(F32)
-
-
 def per_device(
     tokens,
     cotangent,
@@ -250,27 +378,36 @@
     me = lax.axis_index("shard")
     own = D // n
     heads = H // n
-    ff_own = w_down.shape[1]
     order = group_order("shard")
 
-    labels = gather_tokens(jnp.stack([segments, keep_mask]).reshape(1, 2, LEN).astype(F32))
-    segment, keep = labels[:, 0], labels[:, 1]
+    small_part = jnp.concatenate(
+        [
+            segments.astype(F32),
+            keep_mask.astype(F32),
+            jnp.stack([ln_gain, ln_bias]).transpose(0, 1, 3, 2).astype(F32).reshape(-1),
+        ]
+    )
+    small_all = gather_tokens(small_part[None])
+    segment, keep = small_all[:, :LEN], small_all[:, LEN : 2 * LEN]
     allowed = (segment[:, :, None] == segment[:, None, :]) & (keep[:, None, :] == 1.0)
     allowed = (allowed | jnp.eye(LEN, dtype=bool)[None]).astype(F32)
-    norms = jnp.stack([ln_gain, ln_bias]).reshape(1, 2, LAYERS, own, 2)
-    norms = lax.all_gather(norms, "shard", axis=0, tiled=True)
-    norms = norms.transpose(1, 2, 4, 0, 3).reshape(2, LAYERS, 2, D).astype(F32)
+    places = [order.index(place) for place in range(n)]
+    places = jnp.take(jnp.array(places), jnp.bitwise_xor(me, jnp.arange(n)))
+    norms = jnp.take(small_all[:, 2 * LEN :], places, axis=0).reshape(n, 2, LAYERS, 2, own)
+    norms = norms.transpose(1, 2, 3, 0, 4).reshape(2, LAYERS, 2, D)
     gains, biases = norms[0], norms[1]
-    all_positions = lax.all_gather(positions, "shard", axis=0, tiled=True)
+    live_rows = gather_positions(positions, n, me)
     ahead = jnp.concatenate([buckets, buckets[-1:]])
     back = jnp.concatenate([buckets[::-1], buckets[:1]])
-    rows_used = jnp.take(all_positions, jnp.concatenate([back, ahead]), axis=0)
+    wanted = jnp.concatenate([back, ahead]) - FIRST_ROW
+    picks = (wanted[:, None] == jnp.arange(LIVE_ROWS)[None, :]).astype(BF16)
+    rows_used = mm(picks, live_rows).astype(BF16)
     rows_ahead = rows_used[SPAN:]
 
     weights = []
     for layer in range(LAYERS):
-        qkv_cols = by_columns(w_qkv[layer].reshape(own, 3, n, own), me)
-        up_cols = by_columns(w_up[layer].reshape(own, 1, n, ff_own), me)
+        qkv_cols = by_columns(w_qkv[layer], me, n, 3)
+        up_cols = by_columns(w_up[layer], me, n, 1)
         weights.append((qkv_cols, w_out[layer], up_cols, w_down[layer]))
 
     hidden = tokens.astype(F32)
@@ -294,7 +431,8 @@
     output = hidden.astype(BF16)
 
     upstream = cotangent.astype(F32)
-    grads = [None] * LAYERS
+    out_grads = [None] * 4
+    masks = rising_masks("rep")
     small = [None] * LAYERS
     row_grads = jnp.zeros((SPAN, D), F32)
     for layer in reversed(range(LAYERS)):
@@ -316,12 +454,10 @@
         g_qkv = g_qkv.at[:, : 2 * own].add(mm_tn(rows_ahead, d_rel))
         row_grads = row_grads + mm_nt(d_rel, qkv_cols[:, : 2 * own])
         upstream = d_attn + scatter_tokens(mm_nt(d_qkv, qkv_cols))
-        grads[layer] = (
-            over_replicas(by_rows(g_qkv.astype(BF16), me, n, 3)),
-            over_replicas(g_out),
-            over_replicas(by_rows(g_up.astype(BF16), me, n, 1)),
-            over_replicas(g_down),
-        )
+        out_grads[0] = reduced_columns(g_qkv, masks, layer, out_grads[0], 3)
+        out_grads[1] = reduced_rows(g_out, masks, layer, out_grads[1])
+        out_grads[2] = reduced_columns(g_up, masks, layer, out_grads[2], 1)
+        out_grads[3] = reduced_rows(g_down, masks, layer, out_grads[3])
         small[layer] = (
             jnp.stack([d_gain_one, d_gain_two]),
             jnp.stack([d_bias_one, d_bias_two]),
@@ -339,17 +475,16 @@
     norm_part = norm_part.reshape(2, LAYERS, 2, n, own).transpose(3, 0, 1, 2, 4)
     norm_part = jnp.take(norm_part, owners, axis=0).reshape(n, 2 * LAYERS * 2 * own)
     packed = jnp.concatenate([position_part, norm_part], axis=1)
-    packed = scatter_tokens(packed)
-    packed = over_replicas(packed)[0]
+    packed = scatter_tokens(packed).astype(BF16)[0]
+    near, far = double(halve(packed, masks, 0)[None], masks)
+    packed = jnp.concatenate([near, far], axis=0)
+    packed = jnp.zeros_like(packed).at[block_places(masks)].set(packed).reshape(-1).astype(F32)
     grad_positions = packed[: owned_rows * D].reshape(owned_rows, D)
     norm_part = packed[owned_rows * D :].reshape(2, LAYERS, 2, own).transpose(0, 1, 3, 2)
     return (
         output,
         upstream,
-        jnp.stack([entry[0] for entry in grads]),
-        jnp.stack([entry[1] for entry in grads]),
-        jnp.stack([entry[2] for entry in grads]),
-        jnp.stack([entry[3] for entry in grads]),
+        *out_grads,
         norm_part[0],
         norm_part[1],
         grad_positions,

time: 1090 us -> 746 us (0.68)
  local copies, waits for them, and re-layouts: 283 us -> 46.8 us
  waiting for transfers between devices: 589 us -> 387 us
  starting transfers between devices: 41.8 us -> 106 us
  Pallas kernels: 39.7 us -> 79.2 us
  other arithmetic: 47.9 us -> 64 us
  between operations: 16.4 us -> 4.06 us
    psum x1 -> x0, waiting for transfers between devices: 404 us -> none  [over_replicas(): return lax.psum(value.astype(BF16), 'rep').astype(F32)]
    ppermute x60 -> x115, waiting for transfers between devices: 185 us -> 387 us  [swap(): return lax.ppermute(value, axis, [(i, i ^ mask) for i in range(size)])]
    dynamic_update_slice x17 -> x0, local copies, waits for them, and re-layouts: 159 us -> none  [by_rows(): whole = lax.dynamic_update_slice(whole, block, (0, 0, other, 0))]
    ppermute x60 -> x115, starting transfers between devices: 41.8 us -> 105 us  [swap(): return lax.ppermute(value, axis, [(i, i ^ mask) for i in range(size)])]
    pallas_call x0 -> x8, Pallas kernels: none -> 39.6 us  [place(): pl.pallas_call(partial(place_kernel, parts, n, c, half), grid_spec=pltpu....]
    reshape x11 -> x0, local copies, waits for them, and re-layouts: 22.9 us -> none  [the longest x9 22.1 us: by_rows(): block = block.reshape(rows, parts, 1, c)]
    another operation x12 -> x4, local copies, waits for them, and re-layouts: 22.7 us -> 0.71 us  [the longest x2 8.74 us: per_device(): jnp.stack([entry[2] for entry in grads])]
    dynamic_slice x14 -> x33, local copies, waits for them, and re-layouts: 25.5 us -> 9.23 us  [the longest x26 6.3 us: halve(): sent = lax.dynamic_slice_in_dim(value, (1 - upper) * size, size, axis)]
  transfers between devices with their start and end apart: 62 -> 116, of which waited for: 29 -> 53; matrix products, arithmetic and copies ran while one was open for 30% -> 17% of each run, Pallas kernels for 1% -> 7%
where the time goes in v2:
time: 746 us; the launch traced here: 740 us
  waiting for transfers between devices  387 us (52%)
  starting transfers between devices  106 us (14%)
  Pallas kernels  79.2 us (11%)
  other arithmetic  64 us (9%)
  matrix products  52.4 us (7%)
  local copies, waits for them, and re-layouts  46.8 us (6%)
    ppermute x115, waiting for transfers between devices, swap(): return lax.ppermute(value, axis, [(i, i ^ mask) for i in range(size)])  387 us
    ppermute x115, starting transfers between devices, swap(): return lax.ppermute(value, axis, [(i, i ^ mask) for i in range(size)])  105 us
    pallas_call x8, Pallas kernels, place(): pl.pallas_call(partial(place_kernel, parts, n, c, half), grid_spec=pltpu....  39.6 us
    dot_general x12, matrix products, mm(): return jnp.dot(a, b, preferred_element_type=F32)  21.7 us
    pallas_call x2, Pallas kernels, attention_backward(): pl.pallas_call(partial(attention_backward_kernel, heads), grid=(count,),...  20.9 us
    pallas_call x2, Pallas kernels, attention_forward(): pl.pallas_call(partial(attention_forward_kernel, heads), grid=(count,), i...  18.7 us
    dot_general x10, matrix products, mm_tn(): lax.dot_general(a, b, (((0,), (0,)), ((), ())), preferred_element_type=F32)  16.3 us
  transfers between devices with their start and end apart: 116, of which 53 were waited for; matrix products, arithmetic and copies ran while one was open for 17% of the time, Pallas kernels for 7%

profile of v2, /device:TPU:0, one launch (start us, length us, event | category | flops | bytes accessed | tf_op | source)
XLA Modules:
  0.0 739.6 jit_solution(6366885598509072644)
XLA Ops:
  46.8 9.5 %attention_forward.2 = (bf16[512,256]{1,0:T(8,128)(2,1)S(1)}, f32[4,4,128,128]{3,2,1,0:T(8,128)S(1)}) custom-call(bf16[512,768]{1,0:T(8,128)(2,1)S(1)} %convolution_convert_fusion.6.qkv_ref, bf16[256,512]{1,0:T(8,128)(2,1)S(1)} %get-tuple-element.124.rel_ref, f32[4,128,128]{2,1,0:T(8,128)S(1)} %or_convert_fusion.allowed_ref), custom_call_target="tpu_custom_call" | custom-call | tf_op jit(solution)/shard_map/attention_forward/pallas_call | solution.py:253
  66.7 6.8 collective-permute-done.10
  88.4 8.0 %collective-permute-done.14 = bf16[256,1024]{1,0:T(8,128)(2,1)} collective-permute-done((bf16[256,1024]{1,0:T(8,128)(2,1)}, bf16[256,1024]{1,0:T(8,128)(2,1)}, u32[]{:S(2)}, u32[]{:S(2)}) %collective-permute-start.14) | collective-permute-done | bytes 524320 | tf_op jit(solution)/shard_map/ppermute | solution.py:40
  97.4 6.8 collective-permute-done.15
  117.2 6.4 collective-permute-done.17
  125.3 6.7 collective-permute-done.21
  132.1 7.3 collective-permute-done.22
  148.6 9.3 %attention_forward.3 = (bf16[512,256]{1,0:T(8,128)(2,1)S(1)}, f32[4,4,128,128]{3,2,1,0:T(8,128)S(1)}) custom-call(bf16[512,768]{1,0:T(8,128)(2,1)S(1)} %convolution_convert_fusion.5.qkv_ref, bf16[256,512]{1,0:T(8,128)(2,1)S(1)} %get-tuple-element.126.rel_ref, f32[4,128,128]{2,1,0:T(8,128)S(1)} %or_convert_fusion.allowed_ref), custom_call_target="tpu_custom_call" | custom-call | tf_op jit(solution)/shard_map/attention_forward/pallas_call | solution.py:253
  161.5 7.5 %collective-permute-done.24 = bf16[128,1024]{1,0:T(8,128)(2,1)S(1)} collective-permute-done((bf16[128,1024]{1,0:T(8,128)(2,1)S(1)}, bf16[128,1024]{1,0:T(8,128)(2,1)S(1)}, u32[]{:S(2)}, u32[]{:S(2)}) %collective-permute-start.24) | collective-permute-done | bytes 262176 | tf_op jit(solution)/shard_map/ppermute | solution.py:40
  179.5 10.7 %collective-permute-done.28 = bf16[256,1024]{1,0:T(8,128)(2,1)S(1)} collective-permute-done((bf16[256,1024]{1,0:T(8,128)(2,1)S(1)}, bf16[256,1024]{1,0:T(8,128)(2,1)S(1)}, u32[]{:S(2)}, u32[]{:S(2)}) %collective-permute-start.28) | collective-permute-done | bytes 524320 | tf_op jit(solution)/shard_map/ppermute | solution.py:40
  190.3 7.9 %collective-permute-done.29 = bf16[256,1024]{1,0:T(8,128)(2,1)S(1)} collective-permute-done((bf16[256,1024]{1,0:T(8,128)(2,1)S(1)}, bf16[256,1024]{1,0:T(8,128)(2,1)S(1)}, u32[]{:S(2)}, u32[]{:S(2)}) %collective-permute-start.29) | collective-permute-done | bytes 524320 | tf_op jit(solution)/shard_map/ppermute | solution.py:40
  208.2 7.1 collective-permute-done.31
  250.7 12.7 %collective-permute-done.102 = bf16[512,1024]{1,0:T(8,128)(2,1)S(1)} collective-permute-done((bf16[512,1024]{1,0:T(8,128)(2,1)S(1)}, bf16[512,1024]{1,0:T(8,128)(2,1)S(1)}, u32[]{:S(2)}, u32[]{:S(2)}) %collective-permute-start.102) | collective-permute-done | bytes 1048608 | tf_op jit(solution)/shard_map/ppermute | solution.py:40
  266.3 19.0 %collective-permute-done.87 = bf16[4,128,1024]{2,1,0:T(8,128)(2,1)S(1)} collective-permute-done((bf16[4,128,1024]{2,1,0:T(8,128)(2,1)S(1)}, bf16[4,128,1024]{2,1,0:T(8,128)(2,1)S(1)}, u32[]{:S(2)}, u32[]{:S(2)}) %collective-permute-start.87) | collective-permute-done | bytes 1048608 | tf_op jit(solution)/shard_map/ppermute | solution.py:40
  294.2 11.8 %collective-permute-done.88 = bf16[4,64,1024]{2,1,0:T(8,128)(2,1)} collective-permute-done((bf16[4,64,1024]{2,1,0:T(8,128)(2,1)}, bf16[4,64,1024]{2,1,0:T(8,128)(2,1)}, u32[]{:S(2)}, u32[]{:S(2)}) %collective-permute-start.88) | collective-permute-done | bytes 524320 | tf_op jit(solution)/shard_map/ppermute | solution.py:40
  313.6 10.4 %attention_backward.2 = (bf16[512,768]{1,0:T(8,128)(2,1)S(1)}, f32[256,512]{1,0:T(8,128)S(1)}) custom-call(bf16[512,768]{1,0:T(8,128)(2,1)S(1)} %convolution_convert_fusion.5.qkv_ref, bf16[256,512]{1,0:T(8,128)(2,1)S(1)} %copy-done.2, f32[4,4,128,128]{3,2,1,0:T(8,128)S(1)} %copy-done.1, bf16[512,256]{1,0:T(8,128)(2,1)S(1)} %convolution_convert_fusion.12.grad_ref), custom_call_target="tpu_custom_call" | custom-call | tf_op jit(solution)/shard_map/attention_backward/pallas_call | solution.py:317
  344.8 20.4 %collective-permute-done.75 = bf16[1,32,1024]{2,1,0:T(8,128)(2,1)S(1)} collective-permute-done((bf16[1,32,1024]{2,1,0:T(8,128)(2,1)S(1)}, bf16[1,32,1024]{2,1,0:T(8,128)(2,1)S(1)}, u32[]{:S(2)}, u32[]{:S(2)}) %collective-permute-start.75) | collective-permute-done | bytes 65568 | tf_op jit(solution)/shard_map/ppermute | solution.py:40
  385.0 19.1 %collective-permute-done.58 = bf16[4,64,768]{2,1,0:T(8,128)(2,1)S(1)} collective-permute-done((bf16[4,64,768]{2,1,0:T(8,128)(2,1)S(1)}, bf16[4,64,768]{2,1,0:T(8,128)(2,1)S(1)}, u32[]{:S(2)}, u32[]{:S(2)}) %collective-permute-start.58) | collective-permute-done | bytes 393248 | tf_op jit(solution)/shard_map/ppermute | solution.py:40
  406.2 9.1 %collective-permute-done.59 = bf16[4,32,768]{2,1,0:T(8,128)(2,1)S(1)} collective-permute-done((bf16[4,32,768]{2,1,0:T(8,128)(2,1)S(1)}, bf16[4,32,768]{2,1,0:T(8,128)(2,1)S(1)}, u32[]{:S(2)}, u32[]{:S(2)}) %collective-permute-start.59) | collective-permute-done | bytes 196640 | tf_op jit(solution)/shard_map/ppermute | solution.py:40
  436.0 7.7 %collective-permute-done.64 = bf16[2,4,32,768]{3,2,1,0:T(8,128)(2,1)S(1)} collective-permute-done((bf16[2,4,32,768]{3,2,1,0:T(8,128)(2,1)S(1)}, bf16[2,4,32,768]{3,2,1,0:T(8,128)(2,1)S(1)}, u32[]{:S(2)}, u32[]{:S(2)}) %collective-permute-start.64) | collective-permute-done | bytes 393248 | tf_op jit(solution)/shard_map/ppermute | solution.py:40
  464.2 11.4 %collective-permute-done.78 = bf16[4,128,1024]{2,1,0:T(8,128)(2,1)} collective-permute-done((bf16[4,128,1024]{2,1,0:T(8,128)(2,1)}, bf16[4,128,1024]{2,1,0:T(8,128)(2,1)}, u32[]{:S(2)}, u32[]{:S(2)}) %collective-permute-start.78) | collective-permute-done | bytes 1048608 | tf_op jit(solution)/shard_map/ppermute | solution.py:40
  479.8 18.3 %collective-permute-done.96 = bf16[512,1024]{1,0:T(8,128)(2,1)} collective-permute-done((bf16[512,1024]{1,0:T(8,128)(2,1)}, bf16[512,1024]{1,0:T(8,128)(2,1)}, u32[]{:S(2)}, u32[]{:S(2)}) %collective-permute-start.96) | collective-permute-done | bytes 1048608 | tf_op jit(solution)/shard_map/ppermute | solution.py:40
  502.1 11.9 %collective-permute-done.65.far_ref = bf16[4,4,32,768]{3,2,1,0:T(8,128)(2,1)} collective-permute-done((bf16[4,4,32,768]{3,2,1,0:T(8,128)(2,1)S(1)}, bf16[4,4,32,768]{3,2,1,0:T(8,128)(2,1)}, u32[]{:S(2)}, u32[]{:S(2)}) %collective-permute-start.65) | collective-permute-done | bytes 786464 | tf_op jit(solution)/shard_map/ppermute | solution.py:40
  525.5 10.5 %attention_backward.3 = (bf16[512,768]{1,0:T(8,128)(2,1)S(1)}, f32[256,512]{1,0:T(8,128)S(1)}) custom-call(bf16[512,768]{1,0:T(8,128)(2,1)S(1)} %convolution_convert_fusion.6.qkv_ref, bf16[256,512]{1,0:T(8,128)(2,1)S(1)} %get-tuple-element.123.rel_ref, f32[4,4,128,128]{3,2,1,0:T(8,128)S(1)} %get-tuple-element.45.probs_ref, ...), custom_call_target="tpu_custom_call" | custom-call | tf_op jit(solution)/shard_map/attention_backward/pallas_call | solution.py:317
  570.7 14.6 %collective-permute-done.68 = bf16[32,1024]{1,0:T(8,128)(2,1)S(1)} collective-permute-done((bf16[32,1024]{1,0:T(8,128)(2,1)S(1)}, bf16[32,1024]{1,0:T(8,128)(2,1)S(1)}, u32[]{:S(2)}, u32[]{:S(2)}) %collective-permute-start.68) | collective-permute-done | bytes 65568 | tf_op jit(solution)/shard_map/ppermute | solution.py:40
  588.3 13.6 %collective-permute-done.69 = bf16[1,32,1024]{2,1,0:T(8,128)(2,1)S(1)} collective-permute-done((bf16[1,32,1024]{2,1,0:T(8,128)(2,1)S(1)}, bf16[1,32,1024]{2,1,0:T(8,128)(2,1)S(1)}, u32[]{:S(2)}, u32[]{:S(2)}) %collective-permute-start.69) | collective-permute-done | bytes 65568 | tf_op jit(solution)/shard_map/ppermute | solution.py:40
  608.8 9.7 %collective-permute-done.70 = bf16[2,32,1024]{2,1,0:T(8,128)(2,1)S(1)} collective-permute-done((bf16[2,32,1024]{2,1,0:T(8,128)(2,1)S(1)}, bf16[2,32,1024]{2,1,0:T(8,128)(2,1)S(1)}, u32[]{:S(2)}, u32[]{:S(2)}) %collective-permute-start.70) | collective-permute-done | bytes 131104 | tf_op jit(solution)/shard_map/ppermute | solution.py:40
  635.4 6.7 collective-permute-done.49
  642.7 9.4 %collective-permute-done.50 = bf16[4,32,768]{2,1,0:T(8,128)(2,1)S(1)} collective-permute-done((bf16[4,32,768]{2,1,0:T(8,128)(2,1)S(1)}, bf16[4,32,768]{2,1,0:T(8,128)(2,1)S(1)}, u32[]{:S(2)}, u32[]{:S(2)}) %collective-permute-start.50) | collective-permute-done | bytes 196640 | tf_op jit(solution)/shard_map/ppermute | solution.py:40
  665.5 7.5 %collective-permute-done.54 = bf16[1,4,32,768]{3,2,1,0:T(8,128)(2,1)S(1)} collective-permute-done((bf16[1,4,32,768]{3,2,1,0:T(8,128)(2,1)S(1)}, bf16[1,4,32,768]{3,2,1,0:T(8,128)(2,1)S(1)}, u32[]{:S(2)}, u32[]{:S(2)}) %collective-permute-start.54) | collective-permute-done | bytes 196640 | tf_op jit(solution)/shard_map/ppermute | solution.py:40
  675.7 10.5 %collective-permute-done.55 = bf16[2,4,32,768]{3,2,1,0:T(8,128)(2,1)S(1)} collective-permute-done((bf16[2,4,32,768]{3,2,1,0:T(8,128)(2,1)S(1)}, bf16[2,4,32,768]{3,2,1,0:T(8,128)(2,1)S(1)}, u32[]{:S(2)}, u32[]{:S(2)}) %collective-permute-start.55) | collective-permute-done | bytes 393248 | tf_op jit(solution)/shard_map/ppermute | solution.py:40
  692.6 20.5 %collective-permute-done.115 = bf16[4,16640]{1,0:T(4,128)(2,1)S(1)} collective-permute-done((bf16[4,16640]{1,0:T(4,128)(2,1)S(1)}, bf16[4,16640]{1,0:T(4,128)(2,1)S(1)}, u32[]{:S(2)}, u32[]{:S(2)}) %collective-permute-start.115) | collective-permute-done | bytes 133152 | tf_op jit(solution)/shard_map/ppermute | solution.py:40
  (730 shorter events, 386.8 us)
Async XLA Ops:
  7.5 27.8 %collective-permute-start.5 = (bf16[96,1024]{1,0:T(8,128)(2,1)}, bf16[96,1024]{1,0:T(8,128)(2,1)}, u32[]{:S(2)}, u32[]{:S(2)}) collective-permute-start(bf16[96,1024]{1,0:T(8,128)(2,1)} %slice_select_fusion), channel_id=1, source_target_pairs={{1,3},{2,0},{5,7},{6,4},{9,11},{10,8},{13,15},{14,12},{17,19},{18,... | collective-permute-start | bytes 589832 | tf_op jit(solution)/shard_map/ppermute | solution.py:73
  8.8 27.6 %collective-permute-start = (bf16[128,1024]{1,0:T(8,128)(2,1)}, bf16[128,1024]{1,0:T(8,128)(2,1)}, u32[]{:S(2)}, u32[]{:S(2)}) collective-permute-start(bf16[128,1024]{1,0:T(8,128)(2,1)} %param.27), channel_id=1, source_target_pairs={{0,2},{1,3},{2,0},{3,1},{4,6},{5,7},{6,4},{7,5},{8,10},{9,11},{10,... | collective-permute-start | bytes 786440 | tf_op jit(solution)/shard_map/ppermute | solution.py:40
  241.5 43.8 %collective-permute-start.87 = (bf16[4,128,1024]{2,1,0:T(8,128)(2,1)S(1)}, bf16[4,128,1024]{2,1,0:T(8,128)(2,1)S(1)}, u32[]{:S(2)}, u32[]{:S(2)}) collective-permute-start(bf16[4,128,1024]{2,1,0:T(8,128)(2,1)S(1)} %constant_dynamic-slice_fusion.9), channel_id=1, source_target_pairs={{0,4},{4,0},{8,12},{12,8},{16,20},{20,16},{24,28},{28,24},{1,5},{5... | collective-permute-start | bytes 3145736 | tf_op jit(solution)/shard_map/ppermute | solution.py:40
  249.8 39.2 %collective-permute-start.36 = (bf16[128,1024]{1,0:T(8,128)(2,1)S(1)}, bf16[128,1024]{1,0:T(8,128)(2,1)}, u32[]{:S(2)}, u32[]{:S(2)}) collective-permute-start(bf16[128,1024]{1,0:T(8,128)(2,1)S(1)} %get-tuple-element.75), channel_id=1, source_target_pairs={{0,2},{1,3},{2,0},{3,1},{4,6},{5,7},{6,4},{7,5},{8,10},{9,11},{10,... | collective-permute-start | bytes 786440 | tf_op jit(solution)/shard_map/ppermute | solution.py:40
  291.6 44.2 %collective-permute-start.104 = (bf16[128,1024]{1,0:T(8,128)(2,1)S(1)}, bf16[128,1024]{1,0:T(8,128)(2,1)S(1)}, u32[]{:S(2)}, u32[]{:S(2)}) collective-permute-start(bf16[128,1024]{1,0:T(8,128)(2,1)S(1)} %constant_dynamic-slice_fusion), channel_id=1, source_target_pairs={{0,16},{4,20},{8,24},{12,28},{16,0},{20,4},{24,8},{28,12},{1,17},{... | collective-permute-start | bytes 786440 | tf_op jit(solution)/shard_map/ppermute | solution.py:40
  325.1 40.2 %collective-permute-start.38 = (bf16[256,1024]{1,0:T(8,128)(2,1)S(1)}, bf16[256,1024]{1,0:T(8,128)(2,1)S(1)}, u32[]{:S(2)}, u32[]{:S(2)}) collective-permute-start(bf16[256,1024]{1,0:T(8,128)(2,1)S(1)} %slice.547), channel_id=1, source_target_pairs={{0,1},{1,0},{2,3},{3,2},{4,5},{5,4},{6,7},{7,6},{8,9},{9,8},{10,11... | collective-permute-start | bytes 1572872 | tf_op jit(solution)/shard_map/ppermute | solution.py:40
  327.8 47.5 %collective-permute-start.57 = (bf16[4,128,768]{2,1,0:T(8,128)(2,1)S(1)}, bf16[4,128,768]{2,1,0:T(8,128)(2,1)S(1)}, u32[]{:S(2)}, u32[]{:S(2)}) collective-permute-start(bf16[4,128,768]{2,1,0:T(8,128)(2,1)S(1)} %constant_dynamic-slice_fusion.23), channel_id=1, source_target_pairs={{0,4},{4,0},{8,12},{12,8},{16,20},{20,16},{24,28},{28,24},{1,5},{5... | collective-permute-start | bytes 2359304 | tf_op jit(solution)/shard_map/ppermute | solution.py:40
  344.1 26.4 %collective-permute-start.93 = (bf16[1,4,32,1024]{3,2,1,0:T(8,128)(2,1)S(1)}, bf16[1,4,32,1024]{3,2,1,0:T(8,128)(2,1)S(1)}, u32[]{:S(2)}, u32[]{:S(2)}) collective-permute-start(bf16[1,4,32,1024]{3,2,1,0:T(8,128)(2,1)S(1)} %maximum_bitcast_fusion.1), channel_id=1, source_target_pairs={{0,16},{4,20},{8,24},{12,28},{16,0},{20,4},{24,8},{28,12},{1,17},{... | collective-permute-start | bytes 786440 | tf_op jit(solution)/shard_map/ppermute | solution.py:40
  366.7 37.6 %collective-permute-start.106 = (bf16[2,128,1024]{2,1,0:T(8,128)(2,1)S(1)}, bf16[2,128,1024]{2,1,0:T(8,128)(2,1)S(1)}, u32[]{:S(2)}, u32[]{:S(2)}) collective-permute-start(bf16[2,128,1024]{2,1,0:T(8,128)(2,1)S(1)} %pad_maximum_fusion.25), channel_id=1, source_target_pairs={{0,8},{4,12},{8,0},{12,4},{16,24},{20,28},{24,16},{28,20},{1,9},{5... | collective-permute-start | bytes 1572872 | tf_op jit(solution)/shard_map/ppermute | solution.py:40
  370.6 46.5 %collective-permute-start.94 = (bf16[2,4,32,1024]{3,2,1,0:T(8,128)(2,1)S(1)}, bf16[2,4,32,1024]{3,2,1,0:T(8,128)(2,1)S(1)}, u32[]{:S(2)}, u32[]{:S(2)}) collective-permute-start(bf16[2,4,32,1024]{3,2,1,0:T(8,128)(2,1)S(1)} %pad_maximum_fusion.23), channel_id=1, source_target_pairs={{0,8},{4,12},{8,0},{12,4},{16,24},{20,28},{24,16},{28,20},{1,9},{5... | collective-permute-start | bytes 1572872 | tf_op jit(solution)/shard_map/ppermute | solution.py:40
  375.5 28.6 %collective-permute-start.58 = (bf16[4,64,768]{2,1,0:T(8,128)(2,1)S(1)}, bf16[4,64,768]{2,1,0:T(8,128)(2,1)S(1)}, u32[]{:S(2)}, u32[]{:S(2)}) collective-permute-start(bf16[4,64,768]{2,1,0:T(8,128)(2,1)S(1)} %constant_dynamic-slice_fusion.22), channel_id=1, source_target_pairs={{0,8},{4,12},{8,0},{12,4},{16,24},{20,28},{24,16},{28,20},{1,9},{5... | collective-permute-start | bytes 1179656 | tf_op jit(solution)/shard_map/ppermute | solution.py:40
  375.9 30.2 %collective-permute-start.40 = (bf16[128,1024]{1,0:T(8,128)(2,1)S(1)}, bf16[128,1024]{1,0:T(8,128)(2,1)S(1)}, u32[]{:S(2)}, u32[]{:S(2)}) collective-permute-start(bf16[128,1024]{1,0:T(8,128)(2,1)S(1)} %get-tuple-element.72), channel_id=1, source_target_pairs={{0,2},{1,3},{2,0},{3,1},{4,6},{5,7},{6,4},{7,5},{8,10},{9,11},{10,... | collective-permute-start | bytes 786440 | tf_op jit(solution)/shard_map/ppermute | solution.py:40
  404.5 40.1 %collective-permute-start.107 = (bf16[4,128,1024]{2,1,0:T(8,128)(2,1)S(1)}, bf16[4,128,1024]{2,1,0:T(8,128)(2,1)S(1)}, u32[]{:S(2)}, u32[]{:S(2)}) collective-permute-start(bf16[4,128,1024]{2,1,0:T(8,128)(2,1)S(1)} %pad_maximum_fusion.11.near_ref), channel_id=1, source_target_pairs={{0,4},{4,0},{8,12},{12,8},{16,20},{20,16},{24,28},{28,24},{1,5},{5... | collective-permute-start | bytes 3145736 | tf_op jit(solution)/shard_map/ppermute | solution.py:40
  419.2 33.8 %collective-permute-start.95 = (bf16[4,4,32,1024]{3,2,1,0:T(8,128)(2,1)S(1)}, bf16[4,4,32,1024]{3,2,1,0:T(8,128)(2,1)S(1)}, u32[]{:S(2)}, u32[]{:S(2)}) collective-permute-start(bf16[4,4,32,1024]{3,2,1,0:T(8,128)(2,1)S(1)} %pad_maximum_fusion.9.near_ref), channel_id=1, source_target_pairs={{0,4},{4,0},{8,12},{12,8},{16,20},{20,16},{24,28},{28,24},{1,5},{5... | collective-permute-start | bytes 3145736 | tf_op jit(solution)/shard_map/ppermute | solution.py:40
  428.4 47.3 %collective-permute-start.78 = (bf16[4,128,1024]{2,1,0:T(8,128)(2,1)}, bf16[4,128,1024]{2,1,0:T(8,128)(2,1)}, u32[]{:S(2)}, u32[]{:S(2)}) collective-permute-start(bf16[4,128,1024]{2,1,0:T(8,128)(2,1)} %constant_dynamic-slice_fusion.13), channel_id=1, source_target_pairs={{0,4},{4,0},{8,12},{12,8},{16,20},{20,16},{24,28},{28,24},{1,5},{5... | collective-permute-start | bytes 3145736 | tf_op jit(solution)/shard_map/ppermute | solution.py:40
  443.7 54.4 %collective-permute-start.96 = (bf16[512,1024]{1,0:T(8,128)(2,1)}, bf16[512,1024]{1,0:T(8,128)(2,1)}, u32[]{:S(2)}, u32[]{:S(2)}) collective-permute-start(bf16[512,1024]{1,0:T(8,128)(2,1)} %constant_dynamic-slice_fusion.5), channel_id=1, source_target_pairs={{0,4},{4,0},{8,12},{12,8},{16,20},{20,16},{24,28},{28,24},{1,5},{5... | collective-permute-start | bytes 3145736 | tf_op jit(solution)/shard_map/ppermute | solution.py:40
  444.6 69.4 %collective-permute-start.65 = (bf16[4,4,32,768]{3,2,1,0:T(8,128)(2,1)S(1)}, bf16[4,4,32,768]{3,2,1,0:T(8,128)(2,1)}, u32[]{:S(2)}, u32[]{:S(2)}) collective-permute-start(bf16[4,4,32,768]{3,2,1,0:T(8,128)(2,1)S(1)} %pad_maximum_fusion.13.near_ref), channel_id=1, source_target_pairs={{0,4},{4,0},{8,12},{12,8},{16,20},{20,16},{24,28},{28,24},{1,5},{5... | collective-permute-start | bytes 2359304 | tf_op jit(solution)/shard_map/ppermute | solution.py:40
  463.1 38.9 %collective-permute-start.44 = (bf16[128,1024]{1,0:T(8,128)(2,1)S(1)}, bf16[128,1024]{1,0:T(8,128)(2,1)S(1)}, u32[]{:S(2)}, u32[]{:S(2)}) collective-permute-start(bf16[128,1024]{1,0:T(8,128)(2,1)S(1)} %get-tuple-element.69), channel_id=1, source_target_pairs={{0,2},{1,3},{2,0},{3,1},{4,6},{5,7},{6,4},{7,5},{8,10},{9,11},{10,... | collective-permute-start | bytes 786440 | tf_op jit(solution)/shard_map/ppermute | solution.py:40
  477.6 42.5 %collective-permute-start.79 = (bf16[4,64,1024]{2,1,0:T(8,128)(2,1)S(1)}, bf16[4,64,1024]{2,1,0:T(8,128)(2,1)S(1)}, u32[]{:S(2)}, u32[]{:S(2)}) collective-permute-start(bf16[4,64,1024]{2,1,0:T(8,128)(2,1)S(1)} %constant_dynamic-slice_fusion.12), channel_id=1, source_target_pairs={{0,8},{4,12},{8,0},{12,4},{16,24},{20,28},{24,16},{28,20},{1,9},{5... | collective-permute-start | bytes 1572872 | tf_op jit(solution)/shard_map/ppermute | solution.py:40
  521.0 35.4 %collective-permute-start.80 = (bf16[4,32,1024]{2,1,0:T(8,128)(2,1)}, bf16[4,32,1024]{2,1,0:T(8,128)(2,1)}, u32[]{:S(2)}, u32[]{:S(2)}) collective-permute-start(bf16[4,32,1024]{2,1,0:T(8,128)(2,1)} %constant_dynamic-slice_fusion.11), channel_id=1, source_target_pairs={{0,16},{4,20},{8,24},{12,28},{16,0},{20,4},{24,8},{28,12},{1,17},{... | collective-permute-start | bytes 786440 | tf_op jit(solution)/shard_map/ppermute | solution.py:40
  524.6 36.4 %collective-permute-start.98 = (bf16[128,1024]{1,0:T(8,128)(2,1)}, bf16[128,1024]{1,0:T(8,128)(2,1)}, u32[]{:S(2)}, u32[]{:S(2)}) collective-permute-start(bf16[128,1024]{1,0:T(8,128)(2,1)} %constant_dynamic-slice_fusion.3), channel_id=1, source_target_pairs={{0,16},{4,20},{8,24},{12,28},{16,0},{20,4},{24,8},{28,12},{1,17},{... | collective-permute-start | bytes 786440 | tf_op jit(solution)/shard_map/ppermute | solution.py:40
  551.4 54.9 %collective-permute-start.46 = (bf16[256,1024]{1,0:T(8,128)(2,1)S(1)}, bf16[256,1024]{1,0:T(8,128)(2,1)S(1)}, u32[]{:S(2)}, u32[]{:S(2)}) collective-permute-start(bf16[256,1024]{1,0:T(8,128)(2,1)S(1)} %slice.545), channel_id=1, source_target_pairs={{0,1},{1,0},{2,3},{3,2},{4,5},{5,4},{6,7},{7,6},{8,9},{9,8},{10,11... | collective-permute-start | bytes 1572872 | tf_op jit(solution)/shard_map/ppermute | solution.py:40
  553.4 48.5 %collective-permute-start.108 = (bf16[2,133120]{1,0:T(2,128)(2,1)S(1)}, bf16[2,133120]{1,0:T(2,128)(2,1)S(1)}, u32[]{:S(2)}, u32[]{:S(2)}) collective-permute-start(bf16[2,133120]{1,0:T(2,128)(2,1)S(1)} %fusion.34), channel_id=1, source_target_pairs={{0,1},{1,0},{2,3},{3,2},{4,5},{5,4},{6,7},{7,6},{8,9},{9,8},{10,11... | collective-permute-start | bytes 1597448 | tf_op jit(solution)/shard_map/ppermute | solution.py:40
  566.9 58.2 %collective-permute-start.48 = (bf16[4,128,768]{2,1,0:T(8,128)(2,1)S(1)}, bf16[4,128,768]{2,1,0:T(8,128)(2,1)S(1)}, u32[]{:S(2)}, u32[]{:S(2)}) collective-permute-start(bf16[4,128,768]{2,1,0:T(8,128)(2,1)S(1)} %constant_dynamic-slice_fusion.27), channel_id=1, source_target_pairs={{0,4},{4,0},{8,12},{12,8},{16,20},{20,16},{24,28},{28,24},{1,5},{5... | collective-permute-start | bytes 2359304 | tf_op jit(solution)/shard_map/ppermute | solution.py:40
  601.8 51.6 %collective-permute-start.100 = (bf16[2,128,1024]{2,1,0:T(8,128)(2,1)S(1)}, bf16[2,128,1024]{2,1,0:T(8,128)(2,1)S(1)}, u32[]{:S(2)}, u32[]{:S(2)}) collective-permute-start(bf16[2,128,1024]{2,1,0:T(8,128)(2,1)S(1)} %pad_maximum_fusion.24), channel_id=1, source_target_pairs={{0,8},{4,12},{8,0},{12,4},{16,24},{20,28},{24,16},{28,20},{1,9},{5... | collective-permute-start | bytes 1572872 | tf_op jit(solution)/shard_map/ppermute | solution.py:40
  607.8 78.8 %collective-permute-start.47 = (bf16[128,1024]{1,0:T(8,128)(2,1)S(1)}, bf16[128,1024]{1,0:T(8,128)(2,1)S(1)}, u32[]{:S(2)}, u32[]{:S(2)}) collective-permute-start(bf16[128,1024]{1,0:T(8,128)(2,1)S(1)} %slice.554), channel_id=1, source_target_pairs={{0,2},{1,3},{2,0},{3,1},{4,6},{5,7},{6,4},{7,5},{8,10},{9,11},{10,... | collective-permute-start | bytes 786440 | tf_op jit(solution)/shard_map/ppermute | solution.py:40
  618.5 44.6 %collective-permute-start.85 = (bf16[2,4,32,1024]{3,2,1,0:T(8,128)(2,1)S(1)}, bf16[2,4,32,1024]{3,2,1,0:T(8,128)(2,1)S(1)}, u32[]{:S(2)}, u32[]{:S(2)}) collective-permute-start(bf16[2,4,32,1024]{3,2,1,0:T(8,128)(2,1)S(1)} %pad_maximum_fusion.22), channel_id=1, source_target_pairs={{0,8},{4,12},{8,0},{12,4},{16,24},{20,28},{24,16},{28,20},{1,9},{5... | collective-permute-start | bytes 1572872 | tf_op jit(solution)/shard_map/ppermute | solution.py:40
  656.1 33.2 %collective-permute-start.71 = (bf16[4,32,1024]{2,1,0:T(8,128)(2,1)S(1)}, bf16[4,32,1024]{2,1,0:T(8,128)(2,1)S(1)}, u32[]{:S(2)}, u32[]{:S(2)}) collective-permute-start(bf16[4,32,1024]{2,1,0:T(8,128)(2,1)S(1)} %pad_maximum_fusion.48.near_ref), channel_id=1, source_target_pairs={{0,4},{4,0},{8,12},{12,8},{16,20},{20,16},{24,28},{28,24},{1,5},{5... | collective-permute-start | bytes 786440 | tf_op jit(solution)/shard_map/ppermute | solution.py:40
  657.6 62.8 %collective-permute-start.101 = (bf16[4,128,1024]{2,1,0:T(8,128)(2,1)S(1)}, bf16[4,128,1024]{2,1,0:T(8,128)(2,1)}, u32[]{:S(2)}, u32[]{:S(2)}) collective-permute-start(bf16[4,128,1024]{2,1,0:T(8,128)(2,1)S(1)} %pad_maximum_fusion.10.near_ref), channel_id=1, source_target_pairs={{0,4},{4,0},{8,12},{12,8},{16,20},{20,16},{24,28},{28,24},{1,5},{5... | collective-permute-start | bytes 3145736 | tf_op jit(solution)/shard_map/ppermute | solution.py:40
  672.9 53.8 %collective-permute-start.86 = (bf16[4,4,32,1024]{3,2,1,0:T(8,128)(2,1)S(1)}, bf16[4,4,32,1024]{3,2,1,0:T(8,128)(2,1)}, u32[]{:S(2)}, u32[]{:S(2)}) collective-permute-start(bf16[4,4,32,1024]{3,2,1,0:T(8,128)(2,1)S(1)} %pad_maximum_fusion.8.near_ref), channel_id=1, source_target_pairs={{0,4},{4,0},{8,12},{12,8},{16,20},{20,16},{24,28},{28,24},{1,5},{5... | collective-permute-start | bytes 3145736 | tf_op jit(solution)/shard_map/ppermute | solution.py:40
  686.2 26.9 %collective-permute-start.115 = (bf16[4,16640]{1,0:T(4,128)(2,1)S(1)}, bf16[4,16640]{1,0:T(4,128)(2,1)S(1)}, u32[]{:S(2)}, u32[]{:S(2)}) collective-permute-start(bf16[4,16640]{1,0:T(4,128)(2,1)S(1)} %pad_maximum_fusion.50), channel_id=1, source_target_pairs={{0,4},{4,0},{8,12},{12,8},{16,20},{20,16},{24,28},{28,24},{1,5},{5... | collective-permute-start | bytes 399368 | tf_op jit(solution)/shard_map/ppermute | solution.py:40
  686.6 46.4 %collective-permute-start.56 = (bf16[4,4,32,768]{3,2,1,0:T(8,128)(2,1)S(1)}, bf16[4,4,32,768]{3,2,1,0:T(8,128)(2,1)}, u32[]{:S(2)}, u32[]{:S(2)}) collective-permute-start(bf16[4,4,32,768]{3,2,1,0:T(8,128)(2,1)S(1)} %pad_maximum_fusion.12.near_ref), channel_id=1, source_target_pairs={{0,4},{4,0},{8,12},{12,8},{16,20},{20,16},{24,28},{28,24},{1,5},{5... | collective-permute-start | bytes 2359304 | tf_op jit(solution)/shard_map/ppermute | solution.py:40
  (206 other events, 1955.1 us)

commit v3 on v1

--- a/solution.py
+++ b/solution.py
@@ -14,6 +14,8 @@
 LAYERS = 2
 LEN = 128
 SPAN = 2 * LEN
+FIRST_ROW = 160
+LIVE_ROWS = 192
 SCALE = 1.0 / math.sqrt(3 * DH)
 NEG_FILL = -1e30
 NORM_EPS = 1e-07
@@ -38,61 +40,354 @@
     return lax.ppermute(value, axis, [(i, i ^ mask) for i in range(size)])
 
 
-def rising_masks(axis):
-    size = lax.axis_size(axis)
-    masks, mask = [], 1
-    while mask < size:
-        masks.append(mask)
+def far_order(n):
+    span, mask = [0], n // 2
+    while mask > 1:
+        span = span + [place ^ mask for place in span]
+        mask //= 2
+    return span[1:]
+
+
+def group_order(n):
+    far = far_order(n)
+    return [0, 1] + far + [place ^ 1 for place in far]
+
+
+def gather_sides(own):
+    n = lax.axis_size("shard")
+    near = jnp.concatenate([own, swap(own, "shard", 1)], axis=0)
+    span, mask = own, n // 2
+    while mask > 1:
+        passed = swap(span, "shard", mask)
+        span = passed if mask == 2 and n == 4 else jnp.concatenate([span, passed], axis=0)
+        mask //= 2
+    far = span if n == 4 else span[own.shape[0] :]
+    return near, jnp.concatenate([far, swap(far, "shard", 1)], axis=0)
+
+
+def gather_group(own):
+    return jnp.concatenate(gather_sides(own), axis=0)
+
+
+def scatter_positions(row_grads, ahead, rows, n, me):
+    live = jnp.arange(SPAN) < SPAN - 1
+    if n == 4 and rows == 128:
+        wanted = FIRST_ROW + jnp.arange(LIVE_ROWS)
+    else:
+        owners = jnp.bitwise_xor(me, jnp.array(group_order(n)))
+        wanted = (owners[:, None] * rows + jnp.arange(rows)[None, :]).reshape(-1)
+    picks = ((wanted[:, None] == ahead[None, :]) & live[None, :]).astype(BF16)
+    by_row = mm(picks, row_grads.astype(BF16))
+    if n != 4 or rows != 128:
+        return scatter_sides(by_row[: 2 * rows], by_row[2 * rows :])
+    size = LIVE_ROWS // 2
+    odd = me % 2 == 1
+    mine = jnp.where(odd, by_row[:size], by_row[size:])
+    total = mine + swap(jnp.where(odd, by_row[size:], by_row[:size]).astype(BF16), "shard", 1).astype(F32)
+    return total + swap(total.astype(BF16), "shard", 2).astype(F32)
+
+
+def scatter_sides(near, far):
+    n = lax.axis_size("shard")
+    half = far.shape[0] // 2
+    far = far[:half] + swap(far[half:].astype(BF16), "shard", 1).astype(F32)
+    half = near.shape[0] // 2
+    near = near[:half] + swap(near[half:].astype(BF16), "shard", 1).astype(F32)
+    if n == 4:
+        return near + swap(far.astype(BF16), "shard", 2).astype(F32)
+    total, mask = jnp.concatenate([near, far], axis=0), 2
+    while mask < n:
+        half = total.shape[0] // 2
+        total = total[:half] + swap(total[half:].astype(BF16), "shard", mask).astype(F32)
         mask *= 2
-    return masks
-
-
-def group_order(axis):
-    order = [0]
-    for mask in reversed(rising_masks(axis)):
-        order = order + [place ^ mask for place in order]
-    return order
-
-
-def gather_tokens(rows):
-    for mask in reversed(rising_masks("shard")):
-        rows = jnp.concatenate([rows, swap(rows, "shard", mask)], axis=0)
-    return rows
-
-
-def scatter_tokens(partial_rows):
-    total = partial_rows
-    for mask in rising_masks("shard"):
-        half = total.shape[0] // 2
-        sent = total[half:].astype(BF16)
-        total = total[:half] + swap(sent, "shard", mask).astype(F32)
     return total
 
 
-def by_columns(owned, me):
-    rows, parts, n, c = owned.shape
-    whole = jnp.zeros((n * rows, parts * c), owned.dtype)
+def gather_positions(positions, n, me):
+    last_row = FIRST_ROW + LIVE_ROWS
+    rows = positions.shape[0]
+    if n != 4 or rows != 128:
+        whole = lax.all_gather(positions, "shard", axis=0, tiled=True)
+        return whole[FIRST_ROW:last_row]
+    size = LIVE_ROWS // 2
+    mine = jnp.where(me == 1, positions[rows - size :], positions[:size])
+    passed = lax.ppermute(mine, "shard", [(1, 3), (2, 0)])
+    held = jnp.where((me == 1) | (me == 2), mine, passed)
+    other = swap(held, "shard", 1)
+    low = me % 2 == 1
+    return jnp.concatenate([jnp.where(low, held, other), jnp.where(low, other, held)], axis=0)
+
+
+def copy_blocks_kernel(n, me_ref, *refs):
+    for source, target in zip(refs[:n], refs[n:]):
+        target[...] = source[0]
+
+
+def deal(weight, layer, me, n, parts):
+    rows = weight.shape[1]
+    c = weight.shape[2] // (parts * n)
+    if c % 128:
+        blocks = []
+        for mask in range(n):
+            other = jnp.bitwise_xor(me, mask)
+            pieces = [
+                lax.dynamic_slice(weight, (layer, 0, (part * n + other) * c), (1, rows, c))[0]
+                for part in range(parts)
+            ]
+            blocks.append(jnp.concatenate(pieces, axis=1))
+        return blocks
+    split = 1 if parts > 1 or c % 512 else 4
+
+    def source_spec(mask):
+        def where(part, cut, me):
+            return (layer, 0, (part * n + jnp.bitwise_xor(me[0], mask)) * split + cut)
+
+        return pl.BlockSpec((1, rows, c // split), where)
+
+    target = pl.BlockSpec((rows, c // split), lambda part, cut, me: (0, part * split + cut))
+    return pl.pallas_call(
+        partial(copy_blocks_kernel, n),
+        grid_spec=pltpu.PrefetchScalarGridSpec(
+            num_scalar_prefetch=1,
+            grid=(parts, split),
+            in_specs=[source_spec(mask) for mask in range(n)],
+            out_specs=[target] * n,
+        ),
+        out_shape=[jax.ShapeDtypeStruct((rows, parts * c), BF16)] * n,
+        compiler_params=pltpu.CompilerParams(vmem_limit_bytes=24 * 1024 * 1024),
+        name="deal",
+    )(me.reshape(1), *([weight] * n))
+
+
+def collect_kernel(n, me_ref, *refs):
+    step = pl.program_id(1)
     for mask in range(n):
-        other = jnp.bitwise_xor(me, mask)
-        block = lax.dynamic_index_in_dim(owned, other, 2, keepdims=False).reshape(rows, parts * c)
-        if mask:
-            block = swap(block, "shard", mask)
-        whole = lax.dynamic_update_slice(whole, block, (other * rows, 0))
-    return whole
-
-
-def by_rows(columns, me, n, parts):
-    rows = columns.shape[0] // n
-    c = columns.shape[1] // parts
-    whole = jnp.zeros((rows, parts, n, c), columns.dtype)
+
+        @pl.when(step == jnp.bitwise_xor(me_ref[0], mask))
+        def _():
+            refs[n][...] = refs[mask][...]
+
+
+def collect(blocks, me, n):
+    rows, width = blocks[0].shape
+    if rows % 16 or width % 256:
+        whole = jnp.zeros((n * rows, width), BF16)
+        for mask, block in enumerate(blocks):
+            other = jnp.bitwise_xor(me, mask)
+            whole = lax.dynamic_update_slice(whole, block, (other * rows, 0))
+        return whole
+    c = width // 2
+    return pl.pallas_call(
+        partial(collect_kernel, n),
+        grid_spec=pltpu.PrefetchScalarGridSpec(
+            num_scalar_prefetch=1,
+            grid=(width // c, n),
+            in_specs=[pl.BlockSpec((rows, c), lambda cut, step, me: (0, cut))] * n,
+            out_specs=pl.BlockSpec((rows, c), lambda cut, step, me: (step, cut)),
+        ),
+        out_shape=jax.ShapeDtypeStruct((n * rows, width), BF16),
+        compiler_params=pltpu.CompilerParams(vmem_limit_bytes=24 * 1024 * 1024),
+        name="collect",
+    )(me.reshape(1), *blocks)
+
+
+def passed_around(blocks, n):
+    return [swap(block, "shard", mask) if mask else block for mask, block in enumerate(blocks)]
+
+
+def to_owners(columns, me, n):
+    blocks = []
     for mask in range(n):
-        other = jnp.bitwise_xor(me, mask)
-        block = lax.dynamic_slice_in_dim(columns, other * rows, rows, 0)
-        if mask:
-            block = swap(block, "shard", mask)
-        block = block.reshape(rows, parts, 1, c)
-        whole = lax.dynamic_update_slice(whole, block, (0, 0, other, 0))
-    return whole.reshape(rows, parts * n * c)
+        block = lax.dynamic_index_in_dim(columns, jnp.bitwise_xor(me, mask), 0, keepdims=False)
+        blocks.append(swap(block, "shard", mask) if mask else block)
+    return jnp.stack(blocks)
+
+
+def tie(value, after):
+    return lax.optimization_barrier((value, after))[0]
+
+
+INWARDS = [(0, 2), (1, 3), (6, 4), (7, 5)]
+ACROSS = [(2, 4), (3, 5), (4, 2), (5, 3)]
+OUTWARDS = [(2, 0), (3, 1), (4, 6), (5, 7)]
+
+
+def line_stages(value):
+    rep = lax.axis_index("rep")
+    for pairs in (INWARDS, ACROSS):
+        passed = yield value, lax.ppermute(value, "rep", pairs)
+        value = (value.astype(F32) + passed.astype(F32)).astype(BF16)
+    passed = yield value, lax.ppermute(value, "rep", OUTWARDS)
+    return jnp.where((rep >= 2) & (rep < 6), value, passed)
+
+
+def halves_of(grads, upper):
+    pieces = []
+    for grad in grads:
+        size = grad.shape[-2] // 2
+        pieces.append(lax.dynamic_slice_in_dim(grad, upper * size, size, grad.ndim - 2))
+    return pieces[0] if len(pieces) == 1 else jnp.concatenate(pieces, axis=0)
+
+
+def half_stages(grads):
+    upper = lax.axis_index("rep") % 2
+    me = lax.axis_index("shard")
+    sent = halves_of(grads, 1 - upper)
+    held = halves_of(grads, upper)
+    passed = yield sent, swap(sent, "rep", 1)
+    value = (held.astype(F32) + passed.astype(F32)).astype(BF16)
+    value = yield from line_stages(value)
+    if value.ndim == 3:
+        blocks = []
+        for mask in range(value.shape[0]):
+            other = jnp.bitwise_xor(me, mask)
+            blocks.append(lax.dynamic_index_in_dim(value, other, 0, keepdims=False))
+        moved = [swap(block, "shard", mask) if mask else block for mask, block in enumerate(blocks)]
+        blocks = yield blocks, moved
+        value = jnp.stack(blocks)
+    far = yield value, swap(value, "rep", 1)
+    return value, far
+
+
+class Sums:
+    def __init__(self, index, shapes):
+        self.index, self.shapes = index, shapes
+        self.outs = [None] * len(shapes)
+        self.stages, self.moving, self.results = {}, {}, {}
+        self.last, self.placed = (), None
+
+    def ordered(self, value):
+        out = () if self.placed is None else self.outs[self.placed]
+        value, _, out = lax.optimization_barrier((value, self.last, out))
+        if self.placed is not None:
+            self.outs[self.placed] = out
+            self.placed = None
+        return value
+
+    def start(self, name, *grads):
+        grads = self.ordered([grad.astype(BF16) for grad in grads])
+        self.stages[name] = half_stages(grads)
+        self.last, self.moving[name] = next(self.stages[name])
+
+    def step(self, *names):
+        for name in names:
+            moving = self.ordered(self.moving.pop(name))
+            try:
+                self.last, self.moving[name] = self.stages[name].send(moving)
+            except StopIteration as stop:
+                self.results[name] = stop.value
+
+    def place(self, total, which, layer, parts, n, offset=0):
+        shape, out = self.shapes[which], self.outs[which]
+        total = self.ordered(total)
+        if isinstance(total, tuple):
+            out = place(total, self.index, layer, out, shape, parts, n, offset)
+        else:
+            out = place_whole(total, self.index, layer, out, shape, parts, n)
+        self.outs[which], self.placed = out, which
+
+
+def place_kernel(parts, n, c, steps, index_ref, near_ref, far_ref, *rest):
+    out_ref = rest[-1]
+
+    def put(source):
+        if n == 0:
+            out_ref[0] = source[...].astype(F32)
+            return
+        for mask in range(n):
+            for part in range(parts):
+                at = pl.multiple_of(index_ref[1 + mask] * c + part * n * c, c)
+                out_ref[0, :, pl.ds(at, c)] = source[mask, :, part * c : (part + 1) * c].astype(F32)
+
+    @pl.when(pl.program_id(0) < steps)
+    def _():
+        put(near_ref)
+
+    @pl.when(pl.program_id(0) >= steps)
+    def _():
+        put(far_ref)
+
+
+def place(halves, index, layer, out, shape, parts, n, offset):
+    size = shape[1] // 2
+    rows = size // 4 if size % 64 == 0 else size
+    steps, skip = size // rows, offset // rows
+    c = shape[2] // (parts * n) if n else 0
+    lead = (n,) if n else ()
+    block = lead + (rows, parts * c if n else shape[2])
+    zeros = (0,) * len(lead)
+
+    def target(s, index):
+        first = index[0] * steps + s
+        second = (1 - index[0]) * steps + s - steps
+        return (layer, jnp.where(s < steps, first, second), 0)
+
+    in_specs = [
+        pl.BlockSpec(block, lambda s, index: zeros + (skip + jnp.minimum(s, steps - 1), 0)),
+        pl.BlockSpec(block, lambda s, index: zeros + (skip + jnp.maximum(s - steps, 0), 0)),
+    ]
+    operands = [index, *halves]
+    aliases = {}
+    if out is not None:
+        in_specs.append(pl.BlockSpec(memory_space=pl.ANY))
+        operands.append(out)
+        aliases = {3: 0}
+    return pl.pallas_call(
+        partial(place_kernel, parts, n, c, steps),
+        grid_spec=pltpu.PrefetchScalarGridSpec(
+            num_scalar_prefetch=1,
+            grid=(2 * steps,),
+            in_specs=in_specs,
+            out_specs=pl.BlockSpec((1, rows, shape[2]), target),
+        ),
+        out_shape=jax.ShapeDtypeStruct(shape, F32),
+        input_output_aliases=aliases,
+        compiler_params=pltpu.CompilerParams(vmem_limit_bytes=32 * 1024 * 1024),
+        name="place",
+    )(*operands)
+
+
+def place_whole_kernel(parts, n, c, index_ref, blocks_ref, *rest):
+    out_ref = rest[-1]
+    if n == 0:
+        out_ref[0] = blocks_ref[...].astype(F32)
+        return
+    for mask in range(n):
+        for part in range(parts):
+            at = pl.multiple_of(index_ref[1 + mask] * c + part * n * c, c)
+            out_ref[0, :, pl.ds(at, c)] = blocks_ref[mask, :, part * c : (part + 1) * c].astype(F32)
+
+
+def place_whole(blocks, index, layer, out, shape, parts, n):
+    rows = shape[1] // 8
+    c = shape[2] // (parts * n) if n else 0
+    lead = (n,) if n else ()
+    zeros = (0,) * len(lead)
+    block = lead + (rows, parts * c if n else shape[2])
+    in_specs = [pl.BlockSpec(block, lambda s, index: zeros + (s, 0))]
+    operands, aliases = [index, blocks], {}
+    if out is not None:
+        in_specs.append(pl.BlockSpec(memory_space=pl.ANY))
+        operands.append(out)
+        aliases = {2: 0}
+    return pl.pallas_call(
+        partial(place_whole_kernel, parts, n, c),
+        grid_spec=pltpu.PrefetchScalarGridSpec(
+            num_scalar_prefetch=1,
+            grid=(shape[1] // rows,),
+            in_specs=in_specs,
+            out_specs=pl.BlockSpec((1, rows, shape[2]), lambda s, index: (layer, s, 0)),
+        ),
+        out_shape=jax.ShapeDtypeStruct(shape, F32),
+        input_output_aliases=aliases,
+        compiler_params=pltpu.CompilerParams(vmem_limit_bytes=32 * 1024 * 1024),
+        name="place_whole",
+    )(*operands)
+
+
+def put_layer(total, layer, out, shape):
+    out = jnp.zeros(shape, F32) if out is None else out
+    return out.at[layer].set(total.astype(F32))
 
 
 def attention_forward_kernel(heads, qkv_ref, rel_ref, allowed_ref, context_ref, probs_ref):
@@ -228,10 +523,6 @@
     return 0.5 * (1.0 + lax.erf(x * math.sqrt(0.5))) + x * density
 
 
-def over_replicas(value):
-    return lax.psum(value.astype(BF16), "rep").astype(F32)
-
-
 def per_device(
     tokens,
     cotangent,
@@ -250,110 +541,219 @@
     me = lax.axis_index("shard")
     own = D // n
     heads = H // n
-    ff_own = w_down.shape[1]
-    order = group_order("shard")
-
-    labels = gather_tokens(jnp.stack([segments, keep_mask]).reshape(1, 2, LEN).astype(F32))
-    segment, keep = labels[:, 0], labels[:, 1]
+    order = group_order(n)
+
+    qkv_blocks = deal(w_qkv, 0, me, n, 3)
+    up_blocks = deal(w_up, 0, me, n, 1)
+    hidden = tokens.astype(F32)
+    small_part = jnp.concatenate(
+        [
+            segments.astype(BF16),
+            keep_mask.astype(BF16),
+            jnp.stack([ln_gain, ln_bias]).transpose(0, 1, 3, 2).reshape(-1),
+        ]
+    )
+    small_count = small_part.shape[0]
+    small_part = jnp.pad(small_part, (0, 16 * D - small_count)).reshape(16, D)
+    sides = gather_sides(jnp.concatenate([tokens, small_part], axis=0))
+    sides = [side.reshape(-1, LEN + 16, D) for side in sides]
+    hidden_sides = [side[:, :LEN].reshape(-1, D) for side in sides]
+    small_all = jnp.concatenate([side[:, LEN:] for side in sides], axis=0)
+    small_all = small_all.reshape(n, 16 * D)[:, :small_count].astype(F32)
+    segment, keep = small_all[:, :LEN], small_all[:, LEN : 2 * LEN]
     allowed = (segment[:, :, None] == segment[:, None, :]) & (keep[:, None, :] == 1.0)
     allowed = (allowed | jnp.eye(LEN, dtype=bool)[None]).astype(F32)
-    norms = jnp.stack([ln_gain, ln_bias]).reshape(1, 2, LAYERS, own, 2)
-    norms = lax.all_gather(norms, "shard", axis=0, tiled=True)
-    norms = norms.transpose(1, 2, 4, 0, 3).reshape(2, LAYERS, 2, D).astype(F32)
-    gains, biases = norms[0], norms[1]
-    all_positions = lax.all_gather(positions, "shard", axis=0, tiled=True)
+    allowed_sides = (allowed[:2], allowed[2:])
+    live_rows = gather_positions(positions, n, me)
     ahead = jnp.concatenate([buckets, buckets[-1:]])
     back = jnp.concatenate([buckets[::-1], buckets[:1]])
-    rows_used = jnp.take(all_positions, jnp.concatenate([back, ahead]), axis=0)
+    wanted = jnp.concatenate([back, ahead]) - FIRST_ROW
+    picks = (wanted[:, None] == jnp.arange(LIVE_ROWS)[None, :]).astype(BF16)
+    rows_used = mm(picks, live_rows).astype(BF16)
     rows_ahead = rows_used[SPAN:]
+    places = [order.index(place) for place in range(n)]
+    places = jnp.take(jnp.array(places), jnp.bitwise_xor(me, jnp.arange(n)))
+    norms = jnp.take(small_all[:, 2 * LEN :], places, axis=0).reshape(n, 2, LAYERS, 2, own)
+    norms = norms.transpose(1, 2, 3, 0, 4).reshape(2, LAYERS, 2, D)
+    gains, biases = norms[0], norms[1]
 
     weights = []
     for layer in range(LAYERS):
-        qkv_cols = by_columns(w_qkv[layer].reshape(own, 3, n, own), me)
-        up_cols = by_columns(w_up[layer].reshape(own, 1, n, ff_own), me)
-        weights.append((qkv_cols, w_out[layer], up_cols, w_down[layer]))
-
-    hidden = tokens.astype(F32)
+        if layer:
+            qkv_blocks = deal(w_qkv, layer, me, n, 3)
+            qkv_blocks = [tie(block, up_blocks[-1]) for block in qkv_blocks]
+        qkv_blocks = passed_around(qkv_blocks, n)
+        if layer:
+            up_blocks = deal(w_up, layer, me, n, 1)
+        up_blocks = passed_around([tie(block, qkv_blocks[-1]) for block in up_blocks], n)
+        qkv_cols = collect(qkv_blocks, me, n)
+        weights.append((qkv_cols, w_out[layer], collect(up_blocks, me, n), w_down[layer]))
+
+    staged = lax.axis_size("rep") == 8 and n == 4
     kept = []
     for layer in range(LAYERS):
         qkv_cols, out_rows, up_cols, down_rows = weights[layer]
-        hidden_all = gather_tokens(hidden.astype(BF16))
-        qkv = mm(hidden_all, qkv_cols).astype(BF16)
         rel = mm(rows_used, qkv_cols[:, : 2 * own]).astype(BF16)
-        context, probs = attention_forward(qkv, rel[:SPAN], allowed, heads)
-        attn_sum = hidden + scatter_tokens(mm(context, out_rows))
+        qkv = [mm(side, qkv_cols).astype(BF16) for side in hidden_sides]
+        attended = [
+            attention_forward(side, rel[:SPAN], mask, heads)
+            for side, mask in zip(qkv, allowed_sides)
+        ]
+        context = [side[0] for side in attended]
+        probs = [side[1] for side in attended]
+        attn_sum = hidden + scatter_sides(*[mm(side, out_rows) for side in context])
         mid = normed(attn_sum)[0] * gains[layer, 0] + biases[layer, 0]
-        mid_all = gather_tokens(mid.astype(BF16))
-        pre_act = mm(mid_all, up_cols)
-        activation = gelu(pre_act).astype(BF16)
-        ffn_sum = mid + scatter_tokens(mm(activation, down_rows))
+        mid_sides = gather_sides(mid.astype(BF16))
+        pre_act = [mm(side, up_cols) for side in mid_sides]
+        activation = [gelu(side).astype(BF16) for side in pre_act]
+        ffn_sum = mid + scatter_sides(*[mm(side, down_rows) for side in activation])
+        kept.append((hidden_sides, qkv, rel[SPAN:], context, probs, attn_sum, mid_sides, pre_act, activation, ffn_sum))
         hidden = normed(ffn_sum)[0] * gains[layer, 1] + biases[layer, 1]
-        kept.append(
-            (hidden_all, qkv, rel[SPAN:], context, probs, attn_sum, mid_all, pre_act, activation, ffn_sum)
-        )
+        if layer < LAYERS - 1:
+            hidden_sides = gather_sides(hidden.astype(BF16))
     output = hidden.astype(BF16)
 
+    def over_tokens(left, right):
+        return mm_tn(left[0], right[0]) + mm_tn(left[1], right[1])
+
     upstream = cotangent.astype(F32)
-    grads = [None] * LAYERS
+    others = jnp.bitwise_xor(me, jnp.arange(n, dtype=jnp.int32))
+    shapes = [(LAYERS,) + weight.shape[1:] for weight in (w_qkv, w_out, w_up, w_down)]
+    upper = lax.axis_index("rep") % 2
+    sums = Sums(jnp.concatenate([upper.reshape(1), others]), shapes)
+    grads = {}
     small = [None] * LAYERS
     row_grads = jnp.zeros((SPAN, D), F32)
+    top = LAYERS - 1
+
     for layer in reversed(range(LAYERS)):
         qkv_cols, out_rows, up_cols, down_rows = weights[layer]
-        hidden_all, qkv, rel, context, probs, attn_sum, mid_all, pre_act, activation, ffn_sum = kept[layer]
+        hidden_sides, qkv, rel, context, probs, attn_sum, mid_sides, pre_act, activation, ffn_sum = kept[layer]
         d_ffn, d_gain_two, d_bias_two = norm_backward(upstream, ffn_sum, gains[layer, 1])
-        branch_all = gather_tokens(d_ffn.astype(BF16))
-        g_down = mm_tn(activation, branch_all)
-        d_pre = (mm_nt(branch_all, down_rows) * gelu_slope(pre_act)).astype(BF16)
-        g_up = mm_tn(mid_all, d_pre)
-        d_mid = d_ffn + scatter_tokens(mm_nt(d_pre, up_cols))
+        branch = gather_sides(d_ffn.astype(BF16))
+        if staged and layer < top:
+            sums.last = branch
+            sums.start("Q1", grads[top][0])
+            branch = sums.ordered(branch)
+        d_pre = [
+            (mm_nt(side, down_rows) * gelu_slope(pre)).astype(BF16)
+            for side, pre in zip(branch, pre_act)
+        ]
+        d_mid = d_ffn + scatter_sides(*[mm_nt(side, up_cols) for side in d_pre])
+        g_down = over_tokens(activation, branch).astype(BF16)
+        g_up = over_tokens(mid_sides, d_pre).astype(BF16).reshape(n, own, -1)
+        if staged:
+            d_mid, g_down = lax.optimization_barrier((d_mid, g_down))
+            if layer == top:
+                sums.start("D1", g_down)
+            else:
+                sums.last = d_mid
+                sums.step("D1", "U1")
+                sums.start("D0", g_down, out_top)
+            d_mid = sums.ordered(d_mid)
         d_attn, d_gain_one, d_bias_one = norm_backward(d_mid, attn_sum, gains[layer, 0])
-        att_all = gather_tokens(d_attn.astype(BF16))
-        g_out = mm_tn(context, att_all)
-        d_context = mm_nt(att_all, out_rows).astype(BF16)
-        d_qkv, d_rel = attention_backward(qkv, rel, probs, d_context, heads)
-        d_rel = d_rel.astype(BF16)
-        g_qkv = mm_tn(hidden_all, d_qkv)
-        g_qkv = g_qkv.at[:, : 2 * own].add(mm_tn(rows_ahead, d_rel))
+        att = gather_sides(d_attn.astype(BF16))
+        d_context = [mm_nt(side, out_rows).astype(BF16) for side in att]
+        attended = [
+            attention_backward(side, rel, p, grad, heads)
+            for side, p, grad in zip(qkv, probs, d_context)
+        ]
+        d_qkv = [part[0] for part in attended]
+        d_rel = (attended[0][1] + attended[1][1]).astype(BF16)
+        if staged:
+            sums.last = d_qkv
+            if layer == top:
+                sums.step("D1")
+                sums.start("U1", g_up)
+            else:
+                sums.step("D1", "U1", "Q1", "D0")
+                sums.start("U0", g_up)
+            d_qkv = sums.ordered(d_qkv)
+        upstream = d_attn + scatter_sides(*[mm_nt(side, qkv_cols) for side in d_qkv])
+        g_out = over_tokens(context, att).astype(BF16)
+        g_qkv = over_tokens(hidden_sides, d_qkv) + mm_tn(
+            rows_ahead, jnp.concatenate([d_rel, jnp.zeros((SPAN, own), BF16)], axis=1)
+        )
+        g_qkv = g_qkv.astype(BF16).reshape(n, own, -1)
         row_grads = row_grads + mm_nt(d_rel, qkv_cols[:, : 2 * own])
-        upstream = d_attn + scatter_tokens(mm_nt(d_qkv, qkv_cols))
-        grads[layer] = (
-            over_replicas(by_rows(g_qkv.astype(BF16), me, n, 3)),
-            over_replicas(g_out),
-            over_replicas(by_rows(g_up.astype(BF16), me, n, 1)),
-            over_replicas(g_down),
-        )
         small[layer] = (
             jnp.stack([d_gain_one, d_gain_two]),
             jnp.stack([d_bias_one, d_bias_two]),
         )
-
-    owned_rows = positions.shape[0]
+        if staged and layer < top:
+            sums.last = (upstream, g_out, g_qkv)
+            sums.start("Q0", g_qkv)
+            upstream = sums.ordered(upstream)
+        out_top = g_out
+        grads[layer] = (g_qkv, g_out, g_up, g_down)
+
     owners = jnp.bitwise_xor(me, jnp.array(order))
-    row_ids = (owners[:, None] * owned_rows + jnp.arange(owned_rows)[None, :]).reshape(-1)
-    live = jnp.arange(SPAN) < 2 * LEN - 1
-    picks = ((row_ids[:, None] == ahead[None, :]) & live[None, :]).astype(BF16)
-    position_part = mm(picks, row_grads.astype(BF16)).reshape(n, owned_rows * D)
     norm_part = jnp.stack(
         [jnp.stack([entry[0] for entry in small]), jnp.stack([entry[1] for entry in small])]
     )
     norm_part = norm_part.reshape(2, LAYERS, 2, n, own).transpose(3, 0, 1, 2, 4)
     norm_part = jnp.take(norm_part, owners, axis=0).reshape(n, 2 * LAYERS * 2 * own)
-    packed = jnp.concatenate([position_part, norm_part], axis=1)
-    packed = scatter_tokens(packed)
-    packed = over_replicas(packed)[0]
-    grad_positions = packed[: owned_rows * D].reshape(owned_rows, D)
-    norm_part = packed[owned_rows * D :].reshape(2, LAYERS, 2, own).transpose(0, 1, 3, 2)
-    return (
-        output,
-        upstream,
-        jnp.stack([entry[0] for entry in grads]),
-        jnp.stack([entry[1] for entry in grads]),
-        jnp.stack([entry[2] for entry in grads]),
-        jnp.stack([entry[3] for entry in grads]),
-        norm_part[0],
-        norm_part[1],
-        grad_positions,
-    )
+    norm_part = scatter_sides(norm_part[:2], norm_part[2:])
+    position_part = scatter_positions(row_grads, ahead, positions.shape[0], n, me)
+    norm_count = 2 * LAYERS * 2 * own
+    norm_rows = (norm_count + D - 1) // D
+    norm_part = jnp.pad(norm_part.reshape(-1), (0, norm_rows * D - norm_count)).reshape(norm_rows, D)
+    packed = jnp.concatenate([position_part, norm_part], axis=0).astype(BF16)
+
+    if staged:
+        rows = packed.shape[0]
+        packed = jnp.pad(packed, ((0, -rows % 32), (0, 0)))
+        sums.start("R", g_out, packed)
+        sums.step("D1", "U1", "Q1", "D0", "U0")
+        sums.step("U1", "Q1")
+        sums.step("D1")
+        sums.place(sums.results["D1"], 3, 1, 1, 0)
+        sums.step("D0", "U0", "Q0", "U1", "Q1")
+        sums.step("D0", "U0", "Q0", "R", "Q1")
+        sums.step("U1")
+        sums.place(sums.results["U1"], 2, 1, 1, n)
+        sums.step("U0", "Q0", "R")
+        sums.step("U0", "D0")
+        sums.place(sums.results["D0"], 3, 0, 1, 0)
+        sums.place(sums.results["D0"], 1, 1, 1, 0, own * 2)
+        sums.step("Q0", "R", "Q0")
+        sums.step("Q1")
+        sums.place(sums.results["Q1"], 0, 1, 3, n)
+        sums.step("R", "U0")
+        sums.place(sums.results["U0"], 2, 0, 1, n)
+        sums.step("Q0")
+        sums.place(sums.results["Q0"], 0, 0, 3, n)
+        sums.step("R")
+        sums.place(sums.results["R"], 1, 0, 1, 0)
+        out_grads = sums.outs
+        near, far = [half[own // 2 :] for half in sums.results["R"]]
+        lower, higher = jnp.where(upper == 0, near, far), jnp.where(upper == 0, far, near)
+        packed = jnp.concatenate([lower, higher], axis=0)[:rows]
+    else:
+        packed = lax.psum(packed, "rep")
+        out_grads = []
+        for which, shape in enumerate(shapes):
+            out = None
+            for layer in range(LAYERS):
+                total = grads[layer][which].astype(BF16)
+                if which in (0, 2):
+                    parts = 3 if which == 0 else 1
+                    total = to_owners(total.reshape(n, own, -1), me, n)
+                    total = jnp.take(total, others, axis=0).reshape(n, own, parts, -1)
+                    total = total.transpose(1, 2, 0, 3).reshape(shape[1:])
+                out = put_layer(lax.psum(total, "rep"), layer, out, shape)
+            out_grads.append(out)
+
+    grad_positions = packed[:-norm_rows].astype(F32)
+    if grad_positions.shape[0] < positions.shape[0]:
+        gap = positions.shape[0] - grad_positions.shape[0]
+        grad_positions = jnp.where(
+            me == 1,
+            jnp.pad(grad_positions, ((gap, 0), (0, 0))),
+            jnp.where(me == 2, jnp.pad(grad_positions, ((0, gap), (0, 0))), 0.0),
+        )
+    norm_part = packed[-norm_rows:].astype(F32).reshape(-1)[:norm_count].reshape(2, LAYERS, 2, own).transpose(0, 1, 3, 2)
+    return (output, upstream, *out_grads, norm_part[0], norm_part[1], grad_positions)
 
 
 def solution(mesh):

time: 1090 us -> 614 us (0.56)
  waiting for transfers between devices: 589 us -> 253 us
  local copies, waits for them, and re-layouts: 283 us -> 30.7 us
  starting transfers between devices: 41.8 us -> 133 us
  Pallas kernels: 39.7 us -> 85.2 us
  between operations: 16.4 us -> 4.14 us
    psum x1 -> x0, waiting for transfers between devices: 404 us -> none  [over_replicas(): return lax.psum(value.astype(BF16), 'rep').astype(F32)]
    dynamic_update_slice x33 -> x0, local copies, waits for them, and re-layouts: 169 us -> none  [the longest x17 159 us: by_rows(): whole = lax.dynamic_update_slice(whole, block, (0, 0, other, 0))]
    ppermute x0 -> x22, starting transfers between devices: none -> 72.4 us  [the longest x14 61.7 us: line_stages(): passed = (yield (value, lax.ppermute(value, 'rep', pairs)))]
    ppermute x0 -> x22, waiting for transfers between devices: none -> 57.6 us  [the longest x7 36.4 us: line_stages(): passed = (yield (value, lax.ppermute(value, 'rep', OUTWARDS)))]
    pallas_call x0 -> x16, Pallas kernels: none -> 45.7 us  [the longest x8 35.3 us: place(): pl.pallas_call(partial(place_kernel, parts, n, c, steps), grid_spec=pltpu...]
    reshape x12 -> x2, local copies, waits for them, and re-layouts: 25.7 us -> 0.03 us  [the longest x1 0.02 us: per_device(): small_part = jnp.pad(small_part, (0, 16 * D - small_count)).reshape(16, D)]
    another operation x12 -> x1, local copies, waits for them, and re-layouts: 22.7 us -> 0.01 us  [the longest x2 8.74 us: per_device(): jnp.stack([entry[2] for entry in grads])]
    dynamic_slice x14 -> x9, local copies, waits for them, and re-layouts: 25.5 us -> 5.16 us  [halves_of(): lax.dynamic_slice_in_dim(grad, upper * size, size, grad.ndim - 2)]
  transfers between devices with their start and end apart: 62 -> 114, of which waited for: 29 -> 53; matrix products, arithmetic and copies ran while one was open for 30% -> 17% of each run, Pallas kernels for 1% -> 12%
where the time goes in v3:
time: 614 us; the launch traced here: 604 us
  waiting for transfers between devices  253 us (41%)
  starting transfers between devices  133 us (22%)
  Pallas kernels  85.2 us (14%)
  matrix products  49.3 us (8%)
  other arithmetic  49.2 us (8%)
  local copies, waits for them, and re-layouts  30.7 us (5%)
    ppermute x92, waiting for transfers between devices, swap(): return lax.ppermute(value, axis, [(i, i ^ mask) for i in range(size)])  195 us
    ppermute x14, starting transfers between devices, line_stages(): passed = (yield (value, lax.ppermute(value, 'rep', pairs)))  61.7 us
    ppermute x92, starting transfers between devices, swap(): return lax.ppermute(value, axis, [(i, i ^ mask) for i in range(size)])  60.1 us
    ppermute x7, waiting for transfers between devices, line_stages(): passed = (yield (value, lax.ppermute(value, 'rep', OUTWARDS)))  36.4 us
    pallas_call x8, Pallas kernels, place(): pl.pallas_call(partial(place_kernel, parts, n, c, steps), grid_spec=pltpu...  35.3 us
    ppermute x14, waiting for transfers between devices, line_stages(): passed = (yield (value, lax.ppermute(value, 'rep', pairs)))  21.2 us
    pallas_call x4, Pallas kernels, attention_backward(): pl.pallas_call(partial(attention_backward_kernel, heads), grid=(count,),...  20.9 us
    dot_general x18, matrix products, mm_tn(): lax.dot_general(a, b, (((0,), (0,)), ((), ())), preferred_element_type=F32)  18.9 us
  transfers between devices with their start and end apart: 114, of which 53 were waited for; matrix products, arithmetic and copies ran while one was open for 17% of the time, Pallas kernels for 12%

profile of v3, /device:TPU:0, one launch (start us, length us, event | category | flops | bytes accessed | tf_op | source)
XLA Modules:
  0.0 603.6 jit_solution(12800956405561039040)
XLA Ops:
  27.1 9.5 %collective-permute-done.3.refs_3_ = bf16[256,768]{1,0:T(8,128)(2,1)S(1)} collective-permute-done((bf16[256,768]{1,0:T(8,128)(2,1)S(1)}, bf16[256,768]{1,0:T(8,128)(2,1)S(1)}, u32[]{:S(2)}, u32[]{:S(2)}) %collective-permute-start.3) | collective-permute-done | bytes 393248 | tf_op jit(solution)/shard_map/ppermute | solution.py:40
  62.6 7.2 %collective-permute-done.10 = bf16[128,1024]{1,0:T(8,128)(2,1)} collective-permute-done((bf16[128,1024]{1,0:T(8,128)(2,1)}, bf16[128,1024]{1,0:T(8,128)(2,1)}, u32[]{:S(2)}, u32[]{:S(2)}) %collective-permute-start.10) | collective-permute-done | bytes 262176 | tf_op jit(solution)/shard_map/ppermute | solution.py:40
  89.4 6.8 %collective-permute-done.23.refs_3_ = bf16[256,768]{1,0:T(8,128)(2,1)S(1)} collective-permute-done((bf16[256,768]{1,0:T(8,128)(2,1)S(1)}, bf16[256,768]{1,0:T(8,128)(2,1)S(1)}, u32[]{:S(2)}, u32[]{:S(2)}) %collective-permute-start.23) | collective-permute-done | bytes 393248 | tf_op jit(solution)/shard_map/ppermute | solution.py:40
  104.7 4.9 collective-permute-done.25
  127.6 4.8 collective-permute-done.28
  134.6 9.0 %collective-permute-done.31.refs_2_ = bf16[256,1024]{1,0:T(8,128)(2,1)S(1)} collective-permute-done((bf16[256,1024]{1,0:T(8,128)(2,1)S(1)}, bf16[256,1024]{1,0:T(8,128)(2,1)S(1)}, u32[]{:S(2)}, u32[]{:S(2)}) %collective-permute-start.31) | collective-permute-done | bytes 524320 | tf_op jit(solution)/shard_map/ppermute | solution.py:40
  143.6 10.2 %collective-permute-done.32.refs_3_ = bf16[256,1024]{1,0:T(8,128)(2,1)S(1)} collective-permute-done((bf16[256,1024]{1,0:T(8,128)(2,1)S(1)}, bf16[256,1024]{1,0:T(8,128)(2,1)S(1)}, u32[]{:S(2)}, u32[]{:S(2)}) %collective-permute-start.32) | collective-permute-done | bytes 524320 | tf_op jit(solution)/shard_map/ppermute | solution.py:40
  155.0 4.9 collective-permute-done.34
  167.8 6.3 %collective-permute-done.37 = bf16[128,1024]{1,0:T(8,128)(2,1)S(1)} collective-permute-done((bf16[128,1024]{1,0:T(8,128)(2,1)S(1)}, bf16[128,1024]{1,0:T(8,128)(2,1)S(1)}, u32[]{:S(2)}, u32[]{:S(2)}) %collective-permute-start.37) | collective-permute-done | bytes 262176 | tf_op jit(solution)/shard_map/ppermute | solution.py:40
  195.7 6.3 %collective-permute-done.43 = bf16[128,1024]{1,0:T(8,128)(2,1)S(1)} collective-permute-done((bf16[128,1024]{1,0:T(8,128)(2,1)S(1)}, bf16[128,1024]{1,0:T(8,128)(2,1)S(1)}, u32[]{:S(2)}, u32[]{:S(2)}) %collective-permute-start.43) | collective-permute-done | bytes 262176 | tf_op jit(solution)/shard_map/ppermute | solution.py:40
  208.0 5.5 attention_backward.4
  215.5 5.1 attention_backward.5
  221.4 10.3 %collective-permute-done.47 = bf16[512,1024]{1,0:T(8,128)(2,1)S(1)} collective-permute-done((bf16[512,1024]{1,0:T(8,128)(2,1)S(1)}, bf16[512,1024]{1,0:T(8,128)(2,1)S(1)}, u32[]{:S(2)}, u32[]{:S(2)}) %collective-permute-start.47) | collective-permute-done | bytes 1048608 | tf_op jit(solution)/shard_map/ppermute | solution.py:40
  245.8 6.3 %collective-permute-done.52 = bf16[128,1024]{1,0:T(8,128)(2,1)S(1)} collective-permute-done((bf16[128,1024]{1,0:T(8,128)(2,1)S(1)}, bf16[128,1024]{1,0:T(8,128)(2,1)S(1)}, u32[]{:S(2)}, u32[]{:S(2)}) %collective-permute-start.52) | collective-permute-done | bytes 262176 | tf_op jit(solution)/shard_map/ppermute | solution.py:40
  266.2 5.0 collective-permute-done.56
  295.9 5.1 attention_backward.6
  302.7 5.1 attention_backward.7
  317.2 6.0 collective-permute-done.70
  331.0 7.5 %collective-permute-start.78 = (bf16[4,128,768]{2,1,0:T(8,128)(2,1)S(1)}, bf16[4,128,768]{2,1,0:T(8,128)(2,1)S(1)}, u32[]{:S(2)}, u32[]{:S(2)}) collective-permute-start(bf16[4,128,768]{2,1,0:T(8,128)(2,1)S(1)} %add_convert_fusion.23), channel_id=1, source_target_pairs={{0,8},{4,12},{24,16},{28,20},{1,9},{5,13},{25,17},{29,21},{2,10},{... | collective-permute-start | bytes 2359304 | tf_op jit(solution)/shard_map/ppermute | solution.py:218
  348.9 5.5 collective-permute-done.68
  361.5 20.8 %collective-permute-done.77 = bf16[640,1024]{1,0:T(8,128)(2,1)S(1)} collective-permute-done((bf16[640,1024]{1,0:T(8,128)(2,1)S(1)}, bf16[640,1024]{1,0:T(8,128)(2,1)S(1)}, u32[]{:S(2)}, u32[]{:S(2)}) %collective-permute-start.77) | collective-permute-done | bytes 1310752 | tf_op jit(solution)/shard_map/ppermute | solution.py:218
  391.3 7.1 %collective-permute-start.81 = (bf16[4,128,1024]{2,1,0:T(8,128)(2,1)S(1)}, bf16[4,128,1024]{2,1,0:T(8,128)(2,1)S(1)}, u32[]{:S(2)}, u32[]{:S(2)}) collective-permute-start(bf16[4,128,1024]{2,1,0:T(8,128)(2,1)S(1)} %add_convert_fusion.11), channel_id=1, source_target_pairs={{0,8},{4,12},{24,16},{28,20},{1,9},{5,13},{25,17},{29,21},{2,10},{... | collective-permute-start | bytes 3145736 | tf_op jit(solution)/shard_map/ppermute | solution.py:218
  401.4 11.9 %collective-permute-done.85.far_ref = bf16[512,1024]{1,0:T(8,128)(2,1)S(1)} collective-permute-done((bf16[512,1024]{1,0:T(8,128)(2,1)S(1)}, bf16[512,1024]{1,0:T(8,128)(2,1)S(1)}, u32[]{:S(2)}, u32[]{:S(2)}) %collective-permute-start.85) | collective-permute-done | bytes 1048608 | tf_op jit(solution)/shard_map/ppermute | solution.py:40
  434.9 24.3 %collective-permute-start.86 = (bf16[4,128,768]{2,1,0:T(8,128)(2,1)S(1)}, bf16[4,128,768]{2,1,0:T(8,128)(2,1)S(1)}, u32[]{:S(2)}, u32[]{:S(2)}) collective-permute-start(bf16[4,128,768]{2,1,0:T(8,128)(2,1)S(1)} %add_convert_fusion.20), channel_id=1, source_target_pairs={{0,8},{4,12},{24,16},{28,20},{1,9},{5,13},{25,17},{29,21},{2,10},{... | collective-permute-start | bytes 2359304 | tf_op jit(solution)/shard_map/ppermute | solution.py:218
  460.8 25.2 %collective-permute-done.89 = bf16[4,128,768]{2,1,0:T(8,128)(2,1)S(1)} collective-permute-done((bf16[4,128,768]{2,1,0:T(8,128)(2,1)S(1)}, bf16[4,128,768]{2,1,0:T(8,128)(2,1)S(1)}, u32[]{:S(2)}, u32[]{:S(2)}) %collective-permute-start.89) | collective-permute-done | bytes 786464 | tf_op jit(solution)/shard_map/ppermute | solution.py:220
  490.4 5.6 collective-permute-done.74
  499.8 4.8 collective-permute-start.93
  513.9 6.6 %collective-permute-done.104 = bf16[128,1024]{1,0:T(8,128)(2,1)S(1)} collective-permute-done((bf16[128,1024]{1,0:T(8,128)(2,1)S(1)}, bf16[128,1024]{1,0:T(8,128)(2,1)S(1)}, u32[]{:S(2)}, u32[]{:S(2)}) %collective-permute-start.104) | collective-permute-done | bytes 262176 | tf_op jit(solution)/shard_map/ppermute | solution.py:40
  555.4 9.9 %collective-permute-done.106 = bf16[192,1024]{1,0:T(8,128)(2,1)S(1)} collective-permute-done((bf16[192,1024]{1,0:T(8,128)(2,1)S(1)}, bf16[192,1024]{1,0:T(8,128)(2,1)S(1)}, u32[]{:S(2)}, u32[]{:S(2)}) %collective-permute-start.106) | collective-permute-done | bytes 393248 | tf_op jit(solution)/shard_map/ppermute | solution.py:220
  574.4 12.7 %collective-permute-done.112.far_ref = bf16[4,128,768]{2,1,0:T(8,128)(2,1)} collective-permute-done((bf16[4,128,768]{2,1,0:T(8,128)(2,1)S(1)}, bf16[4,128,768]{2,1,0:T(8,128)(2,1)}, u32[]{:S(2)}, u32[]{:S(2)}) %collective-permute-start.112) | collective-permute-done | bytes 786464 | tf_op jit(solution)/shard_map/ppermute | solution.py:40
  587.1 6.2 %place.14 = f32[2,256,3072]{2,1,0:T(8,128)} custom-call(s32[5]{0:T(128)S(1)} %pad_add_fusion.1.index_ref, bf16[4,128,768]{2,1,0:T(8,128)(2,1)S(1)} %pad_maximum_fusion.4.near_ref, bf16[4,128,768]{2,1,0:T(8,128)(2,1)} %collective-permute-done.112.far_ref, f32[2,256,3072]{2,1,0:T(8,128)} %place.12.rest_0_), custom_call_target="tpu_custom_call", output_to_operand_aliasing={{}: (3, {})} | custom-call | tf_op jit(solution)/shard_map/place/pallas_call | solution.py:335
  598.0 5.2 place.15
  (725 shorter events, 327.8 us)
Async XLA Ops:
  38.3 34.9 %collective-permute-start.14 = (bf16[256,1024]{1,0:T(8,128)(2,1)}, bf16[256,1024]{1,0:T(8,128)(2,1)}, u32[]{:S(2)}, u32[]{:S(2)}) collective-permute-start(bf16[256,1024]{1,0:T(8,128)(2,1)} %get-tuple-element.161), channel_id=1, source_target_pairs={{0,3},{1,2},{2,1},{3,0},{4,7},{5,6},{6,5},{7,4},{8,11},{9,10},{10,... | collective-permute-start | bytes 1572872 | tf_op jit(solution)/shard_map/ppermute | solution.py:40
  39.0 34.9 %collective-permute-start.13 = (bf16[256,1024]{1,0:T(8,128)(2,1)}, bf16[256,1024]{1,0:T(8,128)(2,1)}, u32[]{:S(2)}, u32[]{:S(2)}) collective-permute-start(bf16[256,1024]{1,0:T(8,128)(2,1)} %get-tuple-element.159), channel_id=1, source_target_pairs={{0,2},{1,3},{2,0},{3,1},{4,6},{5,7},{6,4},{7,5},{8,10},{9,11},{10,... | collective-permute-start | bytes 1572872 | tf_op jit(solution)/shard_map/ppermute | solution.py:40
  40.5 34.6 %collective-permute-start.12 = (bf16[256,1024]{1,0:T(8,128)(2,1)}, bf16[256,1024]{1,0:T(8,128)(2,1)}, u32[]{:S(2)}, u32[]{:S(2)}) collective-permute-start(bf16[256,1024]{1,0:T(8,128)(2,1)} %get-tuple-element.157), channel_id=1, source_target_pairs={{0,1},{1,0},{2,3},{3,2},{4,5},{5,4},{6,7},{7,6},{8,9},{9,8},{10,11... | collective-permute-start | bytes 1572872 | tf_op jit(solution)/shard_map/ppermute | solution.py:40
  126.4 27.5 %collective-permute-start.32 = (bf16[256,1024]{1,0:T(8,128)(2,1)S(1)}, bf16[256,1024]{1,0:T(8,128)(2,1)S(1)}, u32[]{:S(2)}, u32[]{:S(2)}) collective-permute-start(bf16[256,1024]{1,0:T(8,128)(2,1)S(1)} %get-tuple-element.179), channel_id=1, source_target_pairs={{0,3},{1,2},{2,1},{3,0},{4,7},{5,6},{6,5},{7,4},{8,11},{9,10},{10,... | collective-permute-start | bytes 1572872 | tf_op jit(solution)/shard_map/ppermute | solution.py:40
  133.1 26.8 %collective-permute-start.34 = (bf16[128,1024]{1,0:T(8,128)(2,1)S(1)}, bf16[128,1024]{1,0:T(8,128)(2,1)S(1)}, u32[]{:S(2)}, u32[]{:S(2)}) collective-permute-start(bf16[128,1024]{1,0:T(8,128)(2,1)S(1)} %fusion.121), channel_id=1, source_target_pairs={{0,2},{1,3},{2,0},{3,1},{4,6},{5,7},{6,4},{7,5},{8,10},{9,11},{10,... | collective-permute-start | bytes 786440 | tf_op jit(solution)/shard_map/ppermute | solution.py:40
  236.3 35.0 %collective-permute-start.58 = (bf16[512,1024]{1,0:T(8,128)(2,1)S(1)}, bf16[512,1024]{1,0:T(8,128)(2,1)S(1)}, u32[]{:S(2)}, u32[]{:S(2)}) collective-permute-start(bf16[512,1024]{1,0:T(8,128)(2,1)S(1)} %add_convert_fusion.17), channel_id=1, source_target_pairs={{0,8},{4,12},{24,16},{28,20},{1,9},{5,13},{25,17},{29,21},{2,10},{... | collective-permute-start | bytes 3145736 | tf_op jit(solution)/shard_map/ppermute | solution.py:218
  240.1 32.7 %collective-permute-start.57 = (bf16[4,128,1024]{2,1,0:T(8,128)(2,1)S(1)}, bf16[4,128,1024]{2,1,0:T(8,128)(2,1)S(1)}, u32[]{:S(2)}, u32[]{:S(2)}) collective-permute-start(bf16[4,128,1024]{2,1,0:T(8,128)(2,1)S(1)} %constant_dynamic-slice_fusion.11), channel_id=1, source_target_pairs={{0,4},{4,0},{8,12},{12,8},{16,20},{20,16},{24,28},{28,24},{1,5},{5... | collective-permute-start | bytes 3145736 | tf_op jit(solution)/shard_map/ppermute | solution.py:40
  254.6 75.0 %collective-permute-start.63 = (bf16[4,128,768]{2,1,0:T(8,128)(2,1)}, bf16[4,128,768]{2,1,0:T(8,128)(2,1)}, u32[]{:S(2)}, u32[]{:S(2)}) collective-permute-start(bf16[4,128,768]{2,1,0:T(8,128)(2,1)} %constant_dynamic-slice_fusion.10), channel_id=1, source_target_pairs={{0,4},{4,0},{8,12},{12,8},{16,20},{20,16},{24,28},{28,24},{1,5},{5... | collective-permute-start | bytes 2359304 | tf_op jit(solution)/shard_map/ppermute | solution.py:40
  287.3 39.6 %collective-permute-start.64 = (bf16[4,128,1024]{2,1,0:T(8,128)(2,1)}, bf16[4,128,1024]{2,1,0:T(8,128)(2,1)}, u32[]{:S(2)}, u32[]{:S(2)}) collective-permute-start(bf16[4,128,1024]{2,1,0:T(8,128)(2,1)} %add_convert_fusion.15), channel_id=1, source_target_pairs={{0,8},{4,12},{24,16},{28,20},{1,9},{5,13},{25,17},{29,21},{2,10},{... | collective-permute-start | bytes 3145736 | tf_op jit(solution)/shard_map/ppermute | solution.py:218
  291.9 31.4 %collective-permute-start.65 = (bf16[512,1024]{1,0:T(8,128)(2,1)}, bf16[512,1024]{1,0:T(8,128)(2,1)}, u32[]{:S(2)}, u32[]{:S(2)}) collective-permute-start(bf16[512,1024]{1,0:T(8,128)(2,1)} %add_convert_fusion.16), channel_id=1, source_target_pairs={{8,16},{12,20},{16,8},{20,12},{9,17},{13,21},{17,9},{21,13},{10,18... | collective-permute-start | bytes 3145736 | tf_op jit(solution)/shard_map/ppermute | solution.py:218
  293.9 44.7 %collective-permute-start.62 = (bf16[640,1024]{1,0:T(8,128)(2,1)}, bf16[640,1024]{1,0:T(8,128)(2,1)}, u32[]{:S(2)}, u32[]{:S(2)}) collective-permute-start(bf16[640,1024]{1,0:T(8,128)(2,1)} %pad_maximum_fusion), channel_id=1, source_target_pairs={{0,4},{4,0},{8,12},{12,8},{16,20},{20,16},{24,28},{28,24},{1,5},{5... | collective-permute-start | bytes 3932168 | tf_op jit(solution)/shard_map/ppermute | solution.py:40
  325.4 33.2 %collective-permute-start.80 = (bf16[512,1024]{1,0:T(8,128)(2,1)S(1)}, bf16[512,1024]{1,0:T(8,128)(2,1)S(1)}, u32[]{:S(2)}, u32[]{:S(2)}) collective-permute-start(bf16[512,1024]{1,0:T(8,128)(2,1)S(1)} %add_convert_fusion.14), channel_id=1, source_target_pairs={{8,0},{12,4},{16,24},{20,28},{9,1},{13,5},{17,25},{21,29},{10,2},{... | collective-permute-start | bytes 3145736 | tf_op jit(solution)/shard_map/ppermute | solution.py:220
  328.9 29.8 %collective-permute-start.79 = (bf16[4,128,1024]{2,1,0:T(8,128)(2,1)S(1)}, bf16[4,128,1024]{2,1,0:T(8,128)(2,1)S(1)}, u32[]{:S(2)}, u32[]{:S(2)}) collective-permute-start(bf16[4,128,1024]{2,1,0:T(8,128)(2,1)S(1)} %add_convert_fusion.13), channel_id=1, source_target_pairs={{8,16},{12,20},{16,8},{20,12},{9,17},{13,21},{17,9},{21,13},{10,18... | collective-permute-start | bytes 3145736 | tf_op jit(solution)/shard_map/ppermute | solution.py:218
  331.0 29.4 %collective-permute-start.78 = (bf16[4,128,768]{2,1,0:T(8,128)(2,1)S(1)}, bf16[4,128,768]{2,1,0:T(8,128)(2,1)S(1)}, u32[]{:S(2)}, u32[]{:S(2)}) collective-permute-start(bf16[4,128,768]{2,1,0:T(8,128)(2,1)S(1)} %add_convert_fusion.23), channel_id=1, source_target_pairs={{0,8},{4,12},{24,16},{28,20},{1,9},{5,13},{25,17},{29,21},{2,10},{... | collective-permute-start | bytes 2359304 | tf_op jit(solution)/shard_map/ppermute | solution.py:218
  347.2 35.1 %collective-permute-start.77 = (bf16[640,1024]{1,0:T(8,128)(2,1)S(1)}, bf16[640,1024]{1,0:T(8,128)(2,1)S(1)}, u32[]{:S(2)}, u32[]{:S(2)}) collective-permute-start(bf16[640,1024]{1,0:T(8,128)(2,1)S(1)} %add_convert_fusion.8), channel_id=1, source_target_pairs={{0,8},{4,12},{24,16},{28,20},{1,9},{5,13},{25,17},{29,21},{2,10},{... | collective-permute-start | bytes 3932168 | tf_op jit(solution)/shard_map/ppermute | solution.py:218
  354.4 34.4 %collective-permute-start.76 = (bf16[4,128,1024]{2,1,0:T(8,128)(2,1)}, bf16[4,128,1024]{2,1,0:T(8,128)(2,1)}, u32[]{:S(2)}, u32[]{:S(2)}) collective-permute-start(bf16[4,128,1024]{2,1,0:T(8,128)(2,1)} %constant_dynamic-slice_fusion.5), channel_id=1, source_target_pairs={{0,4},{4,0},{8,12},{12,8},{16,20},{20,16},{24,28},{28,24},{1,5},{5... | collective-permute-start | bytes 3145736 | tf_op jit(solution)/shard_map/ppermute | solution.py:40
  359.1 32.2 %collective-permute-start.84 = (bf16[4,128,1024]{2,1,0:T(8,128)(2,1)S(1)}, bf16[4,128,1024]{2,1,0:T(8,128)(2,1)}, u32[]{:S(2)}, u32[]{:S(2)}) collective-permute-start(bf16[4,128,1024]{2,1,0:T(8,128)(2,1)S(1)} %add_convert_fusion.12), channel_id=1, source_target_pairs={{8,0},{12,4},{16,24},{20,28},{9,1},{13,5},{17,25},{21,29},{10,2},{... | collective-permute-start | bytes 3145736 | tf_op jit(solution)/shard_map/ppermute | solution.py:220
  383.9 33.5 %collective-permute-start.82 = (bf16[640,1024]{1,0:T(8,128)(2,1)}, bf16[640,1024]{1,0:T(8,128)(2,1)}, u32[]{:S(2)}, u32[]{:S(2)}) collective-permute-start(bf16[640,1024]{1,0:T(8,128)(2,1)} %add_convert_fusion.7), channel_id=1, source_target_pairs={{8,16},{12,20},{16,8},{20,12},{9,17},{13,21},{17,9},{21,13},{10,18... | collective-permute-start | bytes 3932168 | tf_op jit(solution)/shard_map/ppermute | solution.py:218
  388.8 38.2 %collective-permute-start.75 = (bf16[4,128,768]{2,1,0:T(8,128)(2,1)}, bf16[4,128,768]{2,1,0:T(8,128)(2,1)S(1)}, u32[]{:S(2)}, u32[]{:S(2)}) collective-permute-start(bf16[4,128,768]{2,1,0:T(8,128)(2,1)} %constant_dynamic-slice_fusion.4), channel_id=1, source_target_pairs={{0,4},{4,0},{8,12},{12,8},{16,20},{20,16},{24,28},{28,24},{1,5},{5... | collective-permute-start | bytes 2359304 | tf_op jit(solution)/shard_map/ppermute | solution.py:40
  391.3 31.2 %collective-permute-start.81 = (bf16[4,128,1024]{2,1,0:T(8,128)(2,1)S(1)}, bf16[4,128,1024]{2,1,0:T(8,128)(2,1)S(1)}, u32[]{:S(2)}, u32[]{:S(2)}) collective-permute-start(bf16[4,128,1024]{2,1,0:T(8,128)(2,1)S(1)} %add_convert_fusion.11), channel_id=1, source_target_pairs={{0,8},{4,12},{24,16},{28,20},{1,9},{5,13},{25,17},{29,21},{2,10},{... | collective-permute-start | bytes 3145736 | tf_op jit(solution)/shard_map/ppermute | solution.py:218
  419.7 66.5 %collective-permute-start.88 = (bf16[640,1024]{1,0:T(8,128)(2,1)S(1)}, bf16[640,1024]{1,0:T(8,128)(2,1)S(1)}, u32[]{:S(2)}, u32[]{:S(2)}) collective-permute-start(bf16[640,1024]{1,0:T(8,128)(2,1)S(1)} %add_convert_fusion.6), channel_id=1, source_target_pairs={{8,0},{12,4},{16,24},{20,28},{9,1},{13,5},{17,25},{21,29},{10,2},{... | collective-permute-start | bytes 3932168 | tf_op jit(solution)/shard_map/ppermute | solution.py:220
  421.1 64.9 %collective-permute-start.89 = (bf16[4,128,768]{2,1,0:T(8,128)(2,1)S(1)}, bf16[4,128,768]{2,1,0:T(8,128)(2,1)S(1)}, u32[]{:S(2)}, u32[]{:S(2)}) collective-permute-start(bf16[4,128,768]{2,1,0:T(8,128)(2,1)S(1)} %add_convert_fusion.21), channel_id=1, source_target_pairs={{8,0},{12,4},{16,24},{20,28},{9,1},{13,5},{17,25},{21,29},{10,2},{... | collective-permute-start | bytes 2359304 | tf_op jit(solution)/shard_map/ppermute | solution.py:220
  427.0 32.2 %collective-permute-start.90 = (bf16[128,1024]{1,0:T(8,128)(2,1)S(1)}, bf16[128,1024]{1,0:T(8,128)(2,1)S(1)}, u32[]{:S(2)}, u32[]{:S(2)}) collective-permute-start(bf16[128,1024]{1,0:T(8,128)(2,1)S(1)} %get-tuple-element.328), channel_id=1, source_target_pairs={{0,1},{1,0},{2,3},{3,2},{4,5},{5,4},{6,7},{7,6},{8,9},{9,8},{10,11... | collective-permute-start | bytes 786440 | tf_op jit(solution)/shard_map/ppermute | solution.py:40
  431.1 55.3 %collective-permute-start.87 = (bf16[4,128,1024]{2,1,0:T(8,128)(2,1)S(1)}, bf16[4,128,1024]{2,1,0:T(8,128)(2,1)S(1)}, u32[]{:S(2)}, u32[]{:S(2)}) collective-permute-start(bf16[4,128,1024]{2,1,0:T(8,128)(2,1)S(1)} %add_convert_fusion.10), channel_id=1, source_target_pairs={{8,16},{12,20},{16,8},{20,12},{9,17},{13,21},{17,9},{21,13},{10,18... | collective-permute-start | bytes 3145736 | tf_op jit(solution)/shard_map/ppermute | solution.py:218
  434.9 54.8 %collective-permute-start.86 = (bf16[4,128,768]{2,1,0:T(8,128)(2,1)S(1)}, bf16[4,128,768]{2,1,0:T(8,128)(2,1)S(1)}, u32[]{:S(2)}, u32[]{:S(2)}) collective-permute-start(bf16[4,128,768]{2,1,0:T(8,128)(2,1)S(1)} %add_convert_fusion.20), channel_id=1, source_target_pairs={{0,8},{4,12},{24,16},{28,20},{1,9},{5,13},{25,17},{29,21},{2,10},{... | collective-permute-start | bytes 2359304 | tf_op jit(solution)/shard_map/ppermute | solution.py:218
  459.3 45.4 %collective-permute-start.99 = (bf16[4,128,1024]{2,1,0:T(8,128)(2,1)S(1)}, bf16[4,128,1024]{2,1,0:T(8,128)(2,1)S(1)}, u32[]{:S(2)}, u32[]{:S(2)}) collective-permute-start(bf16[4,128,1024]{2,1,0:T(8,128)(2,1)S(1)} %pad_maximum_fusion.1.near_ref), channel_id=1, source_target_pairs={{0,4},{4,0},{8,12},{12,8},{16,20},{20,16},{24,28},{28,24},{1,5},{5... | collective-permute-start | bytes 3145736 | tf_op jit(solution)/shard_map/ppermute | solution.py:40
  499.2 31.6 %collective-permute-start.105 = (bf16[640,1024]{1,0:T(8,128)(2,1)S(1)}, bf16[640,1024]{1,0:T(8,128)(2,1)S(1)}, u32[]{:S(2)}, u32[]{:S(2)}) collective-permute-start(bf16[640,1024]{1,0:T(8,128)(2,1)S(1)} %broadcast_select_fusion.near_ref), channel_id=1, source_target_pairs={{0,4},{4,0},{8,12},{12,8},{16,20},{20,16},{24,28},{28,24},{1,5},{5... | collective-permute-start | bytes 3932168 | tf_op jit(solution)/shard_map/ppermute | solution.py:40
  510.5 28.0 %collective-permute-start.101 = (bf16[4,128,768]{2,1,0:T(8,128)(2,1)S(1)}, bf16[4,128,768]{2,1,0:T(8,128)(2,1)S(1)}, u32[]{:S(2)}, u32[]{:S(2)}) collective-permute-start(bf16[4,128,768]{2,1,0:T(8,128)(2,1)S(1)} %add_convert_fusion.18), channel_id=1, source_target_pairs={{8,0},{12,4},{16,24},{20,28},{9,1},{13,5},{17,25},{21,29},{10,2},{... | collective-permute-start | bytes 2359304 | tf_op jit(solution)/shard_map/ppermute | solution.py:220
  520.5 30.9 %collective-permute-start.110 = (bf16[4,128,768]{2,1,0:T(8,128)(2,1)S(1)}, bf16[4,128,768]{2,1,0:T(8,128)(2,1)S(1)}, u32[]{:S(2)}, u32[]{:S(2)}) collective-permute-start(bf16[4,128,768]{2,1,0:T(8,128)(2,1)S(1)} %pad_maximum_fusion.3.near_ref), channel_id=1, source_target_pairs={{0,4},{4,0},{8,12},{12,8},{16,20},{20,16},{24,28},{28,24},{1,5},{5... | collective-permute-start | bytes 2359304 | tf_op jit(solution)/shard_map/ppermute | solution.py:40
  526.3 43.9 %collective-permute-start.113 = (bf16[4,128,1024]{2,1,0:T(8,128)(2,1)S(1)}, bf16[4,128,1024]{2,1,0:T(8,128)(2,1)S(1)}, u32[]{:S(2)}, u32[]{:S(2)}) collective-permute-start(bf16[4,128,1024]{2,1,0:T(8,128)(2,1)S(1)} %pad_maximum_fusion.2.near_ref), channel_id=1, source_target_pairs={{0,4},{4,0},{8,12},{12,8},{16,20},{20,16},{24,28},{28,24},{1,5},{5... | collective-permute-start | bytes 3145736 | tf_op jit(solution)/shard_map/ppermute | solution.py:40
  550.2 36.9 %collective-permute-start.112 = (bf16[4,128,768]{2,1,0:T(8,128)(2,1)S(1)}, bf16[4,128,768]{2,1,0:T(8,128)(2,1)}, u32[]{:S(2)}, u32[]{:S(2)}) collective-permute-start(bf16[4,128,768]{2,1,0:T(8,128)(2,1)S(1)} %pad_maximum_fusion.4.near_ref), channel_id=1, source_target_pairs={{0,4},{4,0},{8,12},{12,8},{16,20},{20,16},{24,28},{28,24},{1,5},{5... | collective-permute-start | bytes 2359304 | tf_op jit(solution)/shard_map/ppermute | solution.py:40
  565.3 30.2 %collective-permute-start.111 = (bf16[192,1024]{1,0:T(8,128)(2,1)S(1)}, bf16[192,1024]{1,0:T(8,128)(2,1)}, u32[]{:S(2)}, u32[]{:S(2)}) collective-permute-start(bf16[192,1024]{1,0:T(8,128)(2,1)S(1)} %broadcast_select_fusion.6.near_ref), channel_id=1, source_target_pairs={{0,4},{4,0},{8,12},{12,8},{16,20},{20,16},{24,28},{28,24},{1,5},{5... | collective-permute-start | bytes 1179656 | tf_op jit(solution)/shard_map/ppermute | solution.py:40
  (205 other events, 1596.4 us)
